TPU v7x, 512 devices: a whole 4x8x8 slice. The times are simulated.
512 devices in a mesh: wide: 64 (over y, x, core), narrow: 8 (over z).
Axes of the slice: x: 4, y: 8, z: 8, core: 2. Of those that a mesh axis runs over, the one named last changes fastest.
Arguments:
- source: float32 [256, 128, 128], P('wide', 'narrow'), may hold values from -120 to 120
- row_scale: float32 [256, 128, 128], P('wide', 'narrow'), may hold values from 0.5 to 2
- shift_field: float32 [256, 128, 128], P('wide', 'narrow'), may hold values from 0.03 to 1
Outputs:
- correction: float32 [256, 128, 128], P('wide', 'narrow')
All inputs are finite; a program needn't handle non-finite values.
Results may differ from a plain program's by a relative error of at most 0.0001.
Values sent between devices are 32-bit elements; how exact they have to be, the bound alone decides.
No kernel may reach another device: no remote copies, remote signals or barrier semaphores. Data moves between devices by JAX's collectives and lax.ppermute only.
A program may use at most 64 MiB of HBM per device.

v0:
```python
import jax
import jax.numpy as jnp
from jax import lax
from jax.sharding import PartitionSpec as P

PRE = 2
POST = 2
COARSE = 4


DAMPING = 0.8


def with_halo(value, sides, width):
    for axis, dim in sides:
        size, length = (lax.axis_size(axis), value.shape[dim])
        up = [(i, (i + 1) % size) for i in range(size - 1)]
        down = [(j, i) for i, j in up]
        last = lax.slice_in_dim(value, length - width, length, axis=dim)
        leading = lax.slice_in_dim(value, 0, width, axis=dim)
        before = lax.ppermute(last, axis, up)
        after = lax.ppermute(leading, axis, down)
        value = jnp.concatenate([before, value, after], axis=dim)
    return value


def box_sum(padded):
    total = padded[:-2] + padded[1:-1] + padded[2:]
    total = total[:, :-2] + total[:, 1:-1] + total[:, 2:]
    return total[:, :, :-2] + total[:, :, 1:-1] + total[:, :, 2:]


def operate(field, padded, row_scale, shift_field, level_scale):
    return level_scale * row_scale * (27.0 * field - box_sum(padded)) + shift_field * field


def coarsen(field):
    sx, sy, sz = field.shape
    return field.reshape(sx // 2, 2, sy // 2, 2, sz // 2, 2).mean(axis=(1, 3, 5))


def refine(field):
    sx, sy, sz = field.shape
    spread = jnp.broadcast_to(field[:, None, :, None, :, None], (sx, 2, sy, 2, sz, 2))
    return spread.reshape(2 * sx, 2 * sy, 2 * sz)


def smooth(field, rhs, diagonal, apply_fn, count):
    for repeat in range(count):
        field = field + DAMPING * (rhs - apply_fn(field)) / diagonal
    return field


def min_residual(rhs, diagonal, apply_fn, sums_fn, count):
    field = jnp.zeros_like(rhs)
    remain = rhs
    for repeat in range(count):
        search = remain / diagonal
        image = apply_fn(search)
        upper, lower = sums_fn(image * remain, image * image)
        alpha = upper / lower
        field = field + alpha * search
        remain = remain - alpha * image
    return field


def local_sums(first, second):
    return (jnp.sum(first), jnp.sum(second))


def shards(source, row_scale, shift_field):
    cells_y = source.shape[1]

    def fine_apply(field):
        padded = with_halo(field, (("wide", 0), ("narrow", 1)), 1)
        padded = jnp.pad(padded, ((0, 0), (0, 0), (1, 1)))
        return operate(field, padded, row_scale, shift_field, 1.0)

    fine_diag = 26.0 * row_scale + shift_field
    fine_iter = smooth(jnp.zeros_like(source), source, fine_diag, fine_apply, PRE)
    fine_resid = source - fine_apply(fine_iter)
    rhs_one, scale_one, shift_one = (
        lax.all_gather(coarsen(fine_resid), "narrow", axis=1, tiled=True),
        lax.all_gather(coarsen(row_scale), "narrow", axis=1, tiled=True),
        lax.all_gather(coarsen(shift_field), "narrow", axis=1, tiled=True),
    )

    def middle_apply(field):
        padded = with_halo(field, (("wide", 0),), 1)
        padded = jnp.pad(padded, ((0, 0), (1, 1), (1, 1)))
        return operate(field, padded, scale_one, shift_one, 0.25)

    middle_diag = 26.0 * 0.25 * scale_one + shift_one
    middle_iter = smooth(jnp.zeros_like(rhs_one), rhs_one, middle_diag, middle_apply, PRE)
    middle_resid = rhs_one - middle_apply(middle_iter)
    rhs_two = coarsen(middle_resid)
    scale_two = coarsen(scale_one)
    shift_two = coarsen(shift_one)
    whole_rhs, whole_scale, whole_shift = (
        lax.all_gather(rhs_two, "wide", axis=0, tiled=True),
        lax.all_gather(scale_two, "wide", axis=0, tiled=True),
        lax.all_gather(shift_two, "wide", axis=0, tiled=True),
    )

    def whole_apply(field):
        return operate(field, jnp.pad(field, 1), whole_scale, whole_shift, 0.0625)

    whole_diag = 26.0 * 0.0625 * whole_scale + whole_shift
    whole_iter = min_residual(whole_rhs, whole_diag, whole_apply, local_sums, COARSE)
    thickness = rhs_two.shape[0]
    coarse_iter = lax.dynamic_slice_in_dim(
        whole_iter, lax.axis_index("wide") * thickness, thickness, 0
    )
    middle_iter = smooth(
        middle_iter + refine(coarse_iter), rhs_one, middle_diag, middle_apply, POST
    )
    half_rows = cells_y // 2
    own_part = lax.dynamic_slice_in_dim(
        middle_iter, lax.axis_index("narrow") * half_rows, half_rows, 1
    )
    return smooth(fine_iter + refine(own_part), source, fine_diag, fine_apply, POST)


def solution(mesh):
    in_specs = (P("wide", "narrow", None), P("wide", "narrow", None), P("wide", "narrow", None))
    out_specs = P("wide", "narrow", None)
    return jax.shard_map(shards, mesh=mesh, in_specs=in_specs, out_specs=out_specs, check_vma=False)
```

profile of v0, /device:TPU:31, one launch (start us, length us, event | category | flops | bytes accessed | tf_op | source)
XLA Modules:
  0.0 420.8 jit_solution(11961410456769818006)
XLA Ops:
  0.0 4.9 %collective-permute-start = (f32[1,16,128]{2,1,0:T(8,128)S(1)}, f32[1,16,128]{2,1,0:T(8,128)S(1)}, u32[]{:S(2)}, u32[]{:S(2)}) collective-permute-start(f32[1,16,128]{2,1,0:T(8,128)S(1)} %broadcast.106), channel_id=1, source_target_pairs={{0,8},{8,16},{16,24},{24,32},{32,40},{40,48},{48,56},{56,64},{64,7... | collective-permute-start | bytes 24584 | tf_op jit(solution)/shard_map/ppermute | solution.py:21
  6.8 7.0 %collective-permute-start.12 = (f32[1,64,64]{2,1,0:T(8,128)S(1)}, f32[1,64,64]{2,1,0:T(8,128)S(1)}, u32[]{:S(2)}, u32[]{:S(2)}) collective-permute-start(f32[1,64,64]{2,1,0:T(8,128)S(1)} %broadcast.112), channel_id=1, source_target_pairs={{0,8},{8,16},{16,24},{24,32},{32,40},{40,48},{48,56},{56,64},{64,7... | collective-permute-start | bytes 49160 | tf_op jit(solution)/shard_map/ppermute | solution.py:21
  15.7 2.8 reshape.59
  21.7 4.0 collective-permute-start.2
  27.0 25.0 %all_gather.20 = f32[2,64,64]{2,1,0:T(8,128)S(1)} all-gather(f32[2,8,64]{2,1,0:T(8,128)S(1)} %broadcast_multiply_fusion.6), channel_id=1, replica_groups=mesh['wide'=64,'narrow'=8] {'narrow'}, dimensions={1}, use_global_device_ids=true | all-gather | bytes 36864 | tf_op jit(solution)/shard_map/all_gather | solution.py:85
  52.3 13.4 %collective-permute-start.4 = (f32[1,16,128]{2,1,0:T(8,128)S(1)}, f32[1,16,128]{2,1,0:T(8,128)S(1)}, u32[]{:S(2)}, u32[]{:S(2)}) collective-permute-start(f32[1,16,128]{2,1,0:T(8,128)S(1)} %get-tuple-element.55), channel_id=1, source_target_pairs={{0,8},{8,16},{16,24},{24,32},{32,40},{40,48},{48,56},{56,64},{64,7... | collective-permute-start | bytes 24584 | tf_op jit(solution)/shard_map/ppermute | solution.py:21
  67.7 18.5 %all_gather.19 = f32[2,64,64]{2,1,0:T(8,128)S(1)} all-gather(f32[2,8,64]{2,1,0:T(8,128)S(1)} %broadcast_multiply_fusion.7), channel_id=1, replica_groups=mesh['wide'=64,'narrow'=8] {'narrow'}, dimensions={1}, use_global_device_ids=true | all-gather | bytes 36864 | tf_op jit(solution)/shard_map/all_gather | solution.py:84
  86.2 2.9 collective-permute-start.6
  90.6 3.0 collective-permute-done.7
  93.8 14.6 %collective-permute-start.8 = (f32[1,16,128]{2,1,0:T(8,128)S(1)}, f32[1,16,128]{2,1,0:T(8,128)S(1)}, u32[]{:S(2)}, u32[]{:S(2)}) collective-permute-start(f32[1,16,128]{2,1,0:T(8,128)S(1)} %get-tuple-element.53), channel_id=1, source_target_pairs={{0,8},{8,16},{16,24},{24,32},{32,40},{40,48},{48,56},{56,64},{64,7... | collective-permute-start | bytes 24584 | tf_op jit(solution)/shard_map/ppermute | solution.py:21
  110.4 6.3 %collective-permute-done.9 = f32[1,16,128]{2,1,0:T(8,128)S(1)} collective-permute-done((f32[1,16,128]{2,1,0:T(8,128)S(1)}, f32[1,16,128]{2,1,0:T(8,128)S(1)}, u32[]{:S(2)}, u32[]{:S(2)}) %collective-permute-start.9) | collective-permute-done | bytes 8224 | tf_op jit(solution)/shard_map/ppermute | solution.py:22
  116.7 2.5 collective-permute-start.10
  120.5 3.0 collective-permute-done.11
  126.2 19.7 %all_gather.18 = f32[2,64,64]{2,1,0:T(8,128)S(1)} all-gather(f32[2,8,64]{2,1,0:T(8,128)S(1)} %broadcast_multiply_fusion.8), channel_id=1, replica_groups=mesh['wide'=64,'narrow'=8] {'narrow'}, dimensions={1}, use_global_device_ids=true | all-gather | bytes 36864 | tf_op jit(solution)/shard_map/all_gather | solution.py:83
  146.0 9.5 %collective-permute-start.14 = (f32[1,64,64]{2,1,0:T(8,128)S(1)}, f32[1,64,64]{2,1,0:T(8,128)S(1)}, u32[]{:S(2)}, u32[]{:S(2)}) collective-permute-start(f32[1,64,64]{2,1,0:T(8,128)S(1)} %get-tuple-element.37), channel_id=1, source_target_pairs={{0,8},{8,16},{16,24},{24,32},{32,40},{40,48},{48,56},{56,64},{64,7... | collective-permute-start | bytes 49160 | tf_op jit(solution)/shard_map/ppermute | solution.py:21
  157.4 6.6 %collective-permute-done.15 = f32[1,64,64]{2,1,0:T(8,128)S(1)} collective-permute-done((f32[1,64,64]{2,1,0:T(8,128)S(1)}, f32[1,64,64]{2,1,0:T(8,128)S(1)}, u32[]{:S(2)}, u32[]{:S(2)}) %collective-permute-start.15) | collective-permute-done | bytes 16416 | tf_op jit(solution)/shard_map/ppermute | solution.py:22
  169.2 6.1 %collective-permute-done.17 = f32[1,64,64]{2,1,0:T(8,128)S(1)} collective-permute-done((f32[1,64,64]{2,1,0:T(8,128)S(1)}, f32[1,64,64]{2,1,0:T(8,128)S(1)}, u32[]{:S(2)}, u32[]{:S(2)}) %collective-permute-start.17) | collective-permute-done | bytes 16416 | tf_op jit(solution)/shard_map/ppermute | solution.py:22
  177.4 47.5 %all-gather = f32[2048,32]{1,0:T(8,128)S(1)} all-gather(f32[32,32]{1,0:T(8,128)S(1)} %broadcast_multiply_fusion.5), channel_id=2, replica_groups=mesh['wide'=64,'narrow'=8] {'wide'}, dimensions={0}, use_global_device_ids=true | all-gather | bytes 266240 | tf_op jit(solution)/shard_map/all_gather | solution.py:101
  227.4 47.8 %all-gather.1 = f32[2048,32]{1,0:T(8,128)S(1)} all-gather(f32[32,32]{1,0:T(8,128)S(1)} %broadcast_multiply_fusion.4), channel_id=3, replica_groups=mesh['wide'=64,'narrow'=8] {'wide'}, dimensions={0}, use_global_device_ids=true | all-gather | bytes 266240 | tf_op jit(solution)/shard_map/all_gather | solution.py:100
  277.2 50.1 %all-gather.2 = f32[2048,32]{1,0:T(8,128)S(1)} all-gather(f32[32,32]{1,0:T(8,128)S(1)} %broadcast_multiply_fusion.3), channel_id=4, replica_groups=mesh['wide'=64,'narrow'=8] {'wide'}, dimensions={0}, use_global_device_ids=true | all-gather | bytes 266240 | tf_op jit(solution)/shard_map/all_gather | solution.py:102
  356.9 4.3 %collective-permute-start.18 = (f32[1,64,64]{2,1,0:T(8,128)S(1)}, f32[1,64,64]{2,1,0:T(8,128)S(1)}, u32[]{:S(2)}, u32[]{:S(2)}) collective-permute-start(f32[1,64,64]{2,1,0:T(8,128)S(1)} %get-tuple-element.33), channel_id=1, source_target_pairs={{0,8},{8,16},{16,24},{24,32},{32,40},{40,48},{48,56},{56,64},{64,7... | collective-permute-start | bytes 49160 | tf_op jit(solution)/shard_map/ppermute | solution.py:21
  363.2 6.6 %collective-permute-done.19 = f32[1,64,64]{2,1,0:T(8,128)S(1)} collective-permute-done((f32[1,64,64]{2,1,0:T(8,128)S(1)}, f32[1,64,64]{2,1,0:T(8,128)S(1)}, u32[]{:S(2)}, u32[]{:S(2)}) %collective-permute-start.19) | collective-permute-done | bytes 16416 | tf_op jit(solution)/shard_map/ppermute | solution.py:22
  372.0 2.4 collective-permute-start.21
  374.4 6.1 %collective-permute-done.21 = f32[1,64,64]{2,1,0:T(8,128)S(1)} collective-permute-done((f32[1,64,64]{2,1,0:T(8,128)S(1)}, f32[1,64,64]{2,1,0:T(8,128)S(1)}, u32[]{:S(2)}, u32[]{:S(2)}) %collective-permute-start.21) | collective-permute-done | bytes 16416 | tf_op jit(solution)/shard_map/ppermute | solution.py:22
  385.0 2.4 collective-permute-start.23
  387.4 5.9 %collective-permute-done.23 = f32[1,16,128]{2,1,0:T(8,128)S(1)} collective-permute-done((f32[1,16,128]{2,1,0:T(8,128)S(1)}, f32[1,16,128]{2,1,0:T(8,128)S(1)}, u32[]{:S(2)}, u32[]{:S(2)}) %collective-permute-start.23) | collective-permute-done | bytes 8224 | tf_op jit(solution)/shard_map/ppermute | solution.py:22
  393.3 2.8 collective-permute-start.24
  397.5 3.0 collective-permute-done.25
  400.8 3.4 collective-permute-start.26
  406.1 6.4 %collective-permute-done.27 = f32[1,16,128]{2,1,0:T(8,128)S(1)} collective-permute-done((f32[1,16,128]{2,1,0:T(8,128)S(1)}, f32[1,16,128]{2,1,0:T(8,128)S(1)}, u32[]{:S(2)}, u32[]{:S(2)}) %collective-permute-start.27) | collective-permute-done | bytes 8224 | tf_op jit(solution)/shard_map/ppermute | solution.py:22
  412.5 2.8 collective-permute-start.28
  416.6 3.3 collective-permute-done.29
  (154 shorter events, 69.8 us)
Async XLA Ops:
  0.0 21.7 %collective-permute-start = (f32[1,16,128]{2,1,0:T(8,128)S(1)}, f32[1,16,128]{2,1,0:T(8,128)S(1)}, u32[]{:S(2)}, u32[]{:S(2)}) collective-permute-start(f32[1,16,128]{2,1,0:T(8,128)S(1)} %broadcast.106), channel_id=1, source_target_pairs={{0,8},{8,16},{16,24},{24,32},{32,40},{40,48},{48,56},{56,64},{64,7... | collective-permute-start | bytes 24584 | tf_op jit(solution)/shard_map/ppermute | solution.py:21
  4.9 16.8 %collective-permute-start.1 = (f32[1,16,128]{2,1,0:T(8,128)S(1)}, f32[1,16,128]{2,1,0:T(8,128)S(1)}, u32[]{:S(2)}, u32[]{:S(2)}) collective-permute-start(f32[1,16,128]{2,1,0:T(8,128)S(1)} %broadcast.106), channel_id=1, source_target_pairs={{8,0},{16,8},{24,16},{32,24},{40,32},{48,40},{56,48},{64,56},{72,6... | collective-permute-start | bytes 24584 | tf_op jit(solution)/shard_map/ppermute | solution.py:22
  6.8 83.6 %collective-permute-start.12 = (f32[1,64,64]{2,1,0:T(8,128)S(1)}, f32[1,64,64]{2,1,0:T(8,128)S(1)}, u32[]{:S(2)}, u32[]{:S(2)}) collective-permute-start(f32[1,64,64]{2,1,0:T(8,128)S(1)} %broadcast.112), channel_id=1, source_target_pairs={{0,8},{8,16},{16,24},{24,32},{32,40},{40,48},{48,56},{56,64},{64,7... | collective-permute-start | bytes 49160 | tf_op jit(solution)/shard_map/ppermute | solution.py:21
  13.8 76.6 %collective-permute-start.13 = (f32[1,64,64]{2,1,0:T(8,128)S(1)}, f32[1,64,64]{2,1,0:T(8,128)S(1)}, u32[]{:S(2)}, u32[]{:S(2)}) collective-permute-start(f32[1,64,64]{2,1,0:T(8,128)S(1)} %broadcast.112), channel_id=1, source_target_pairs={{8,0},{16,8},{24,16},{32,24},{40,32},{48,40},{56,48},{64,56},{72,6... | collective-permute-start | bytes 49160 | tf_op jit(solution)/shard_map/ppermute | solution.py:22
  21.4 30.8 %copy-start.8 = (f32[4,16,128]{2,1,0:T(8,128)S(1)}, f32[4,16,128]{2,1,0:T(8,128)}, u32[]{:S(2)}) copy-start(f32[4,16,128]{2,1,0:T(8,128)} %param.5) | copy-start | bytes 98308
  21.7 30.3 %collective-permute-start.2 = (f32[6,1,128]{2,1,0:T(1,128)S(1)}, f32[6,1,128]{2,1,0:T(1,128)S(1)}, u32[]{:S(2)}, u32[]{:S(2)}) collective-permute-start(f32[6,1,128]{2,1,0:T(1,128)S(1)} %get-tuple-element.47), channel_id=1, source_target_pairs={{0,1},{1,2},{2,3},{3,4},{4,5},{5,6},{6,7},{8,9},{9,10},{10,11},{11... | collective-permute-start | bytes 9224 | tf_op jit(solution)/shard_map/ppermute | solution.py:21
  25.7 26.3 %collective-permute-start.3 = (f32[6,1,128]{2,1,0:T(1,128)S(1)}, f32[6,1,128]{2,1,0:T(1,128)S(1)}, u32[]{:S(2)}, u32[]{:S(2)}) collective-permute-start(f32[6,1,128]{2,1,0:T(1,128)S(1)} %get-tuple-element.48), channel_id=1, source_target_pairs={{1,0},{2,1},{3,2},{4,3},{5,4},{6,5},{7,6},{9,8},{10,9},{11,10},{12... | collective-permute-start | bytes 9224 | tf_op jit(solution)/shard_map/ppermute | solution.py:22
  52.3 33.8 %collective-permute-start.4 = (f32[1,16,128]{2,1,0:T(8,128)S(1)}, f32[1,16,128]{2,1,0:T(8,128)S(1)}, u32[]{:S(2)}, u32[]{:S(2)}) collective-permute-start(f32[1,16,128]{2,1,0:T(8,128)S(1)} %get-tuple-element.55), channel_id=1, source_target_pairs={{0,8},{8,16},{16,24},{24,32},{32,40},{40,48},{48,56},{56,64},{64,7... | collective-permute-start | bytes 24584 | tf_op jit(solution)/shard_map/ppermute | solution.py:21
  65.8 20.4 %collective-permute-start.5 = (f32[1,16,128]{2,1,0:T(8,128)S(1)}, f32[1,16,128]{2,1,0:T(8,128)S(1)}, u32[]{:S(2)}, u32[]{:S(2)}) collective-permute-start(f32[1,16,128]{2,1,0:T(8,128)S(1)} %get-tuple-element.56), channel_id=1, source_target_pairs={{8,0},{16,8},{24,16},{32,24},{40,32},{48,40},{56,48},{64,56},{72,6... | collective-permute-start | bytes 24584 | tf_op jit(solution)/shard_map/ppermute | solution.py:22
  86.2 4.4 %collective-permute-start.6 = (f32[6,1,128]{2,1,0:T(1,128)S(1)}, f32[6,1,128]{2,1,0:T(1,128)S(1)}, u32[]{:S(2)}, u32[]{:S(2)}) collective-permute-start(f32[6,1,128]{2,1,0:T(1,128)S(1)} %get-tuple-element.45), channel_id=1, source_target_pairs={{0,1},{1,2},{2,3},{3,4},{4,5},{5,6},{6,7},{8,9},{9,10},{10,11},{11... | collective-permute-start | bytes 9224 | tf_op jit(solution)/shard_map/ppermute | solution.py:21
  89.1 4.4 %collective-permute-start.7 = (f32[6,1,128]{2,1,0:T(1,128)S(1)}, f32[6,1,128]{2,1,0:T(1,128)S(1)}, u32[]{:S(2)}, u32[]{:S(2)}) collective-permute-start(f32[6,1,128]{2,1,0:T(1,128)S(1)} %get-tuple-element.46), channel_id=1, source_target_pairs={{1,0},{2,1},{3,2},{4,3},{5,4},{6,5},{7,6},{9,8},{10,9},{11,10},{12... | collective-permute-start | bytes 9224 | tf_op jit(solution)/shard_map/ppermute | solution.py:22
  93.8 16.5 %collective-permute-start.8 = (f32[1,16,128]{2,1,0:T(8,128)S(1)}, f32[1,16,128]{2,1,0:T(8,128)S(1)}, u32[]{:S(2)}, u32[]{:S(2)}) collective-permute-start(f32[1,16,128]{2,1,0:T(8,128)S(1)} %get-tuple-element.53), channel_id=1, source_target_pairs={{0,8},{8,16},{16,24},{24,32},{32,40},{40,48},{48,56},{56,64},{64,7... | collective-permute-start | bytes 24584 | tf_op jit(solution)/shard_map/ppermute | solution.py:21
  108.4 8.3 %collective-permute-start.9 = (f32[1,16,128]{2,1,0:T(8,128)S(1)}, f32[1,16,128]{2,1,0:T(8,128)S(1)}, u32[]{:S(2)}, u32[]{:S(2)}) collective-permute-start(f32[1,16,128]{2,1,0:T(8,128)S(1)} %get-tuple-element.54), channel_id=1, source_target_pairs={{8,0},{16,8},{24,16},{32,24},{40,32},{48,40},{56,48},{64,56},{72,6... | collective-permute-start | bytes 24584 | tf_op jit(solution)/shard_map/ppermute | solution.py:22
  116.7 3.8 collective-permute-start.10
  119.2 4.3 %collective-permute-start.11 = (f32[6,1,128]{2,1,0:T(1,128)S(1)}, f32[6,1,128]{2,1,0:T(1,128)S(1)}, u32[]{:S(2)}, u32[]{:S(2)}) collective-permute-start(f32[6,1,128]{2,1,0:T(1,128)S(1)} %get-tuple-element.44), channel_id=1, source_target_pairs={{1,0},{2,1},{3,2},{4,3},{5,4},{6,5},{7,6},{9,8},{10,9},{11,10},{12... | collective-permute-start | bytes 9224 | tf_op jit(solution)/shard_map/ppermute | solution.py:22
  146.0 11.4 %collective-permute-start.14 = (f32[1,64,64]{2,1,0:T(8,128)S(1)}, f32[1,64,64]{2,1,0:T(8,128)S(1)}, u32[]{:S(2)}, u32[]{:S(2)}) collective-permute-start(f32[1,64,64]{2,1,0:T(8,128)S(1)} %get-tuple-element.37), channel_id=1, source_target_pairs={{0,8},{8,16},{16,24},{24,32},{32,40},{40,48},{48,56},{56,64},{64,7... | collective-permute-start | bytes 49160 | tf_op jit(solution)/shard_map/ppermute | solution.py:21
  155.4 8.6 %collective-permute-start.15 = (f32[1,64,64]{2,1,0:T(8,128)S(1)}, f32[1,64,64]{2,1,0:T(8,128)S(1)}, u32[]{:S(2)}, u32[]{:S(2)}) collective-permute-start(f32[1,64,64]{2,1,0:T(8,128)S(1)} %get-tuple-element.38), channel_id=1, source_target_pairs={{8,0},{16,8},{24,16},{32,24},{40,32},{48,40},{56,48},{64,56},{72,6... | collective-permute-start | bytes 49160 | tf_op jit(solution)/shard_map/ppermute | solution.py:22
  164.8 4.3 %collective-permute-start.16 = (f32[1,64,64]{2,1,0:T(8,128)S(1)}, f32[1,64,64]{2,1,0:T(8,128)S(1)}, u32[]{:S(2)}, u32[]{:S(2)}) collective-permute-start(f32[1,64,64]{2,1,0:T(8,128)S(1)} %get-tuple-element.35), channel_id=1, source_target_pairs={{0,8},{8,16},{16,24},{24,32},{32,40},{40,48},{48,56},{56,64},{64,7... | collective-permute-start | bytes 49160 | tf_op jit(solution)/shard_map/ppermute | solution.py:21
  166.7 8.6 %collective-permute-start.17 = (f32[1,64,64]{2,1,0:T(8,128)S(1)}, f32[1,64,64]{2,1,0:T(8,128)S(1)}, u32[]{:S(2)}, u32[]{:S(2)}) collective-permute-start(f32[1,64,64]{2,1,0:T(8,128)S(1)} %get-tuple-element.36), channel_id=1, source_target_pairs={{8,0},{16,8},{24,16},{32,24},{40,32},{48,40},{56,48},{64,56},{72,6... | collective-permute-start | bytes 49160 | tf_op jit(solution)/shard_map/ppermute | solution.py:22
  277.2 50.1 %copy-start.6 = (f32[2048,32]{1,0:T(8,128)S(1)}, f32[2048,32]{1,0:T(8,128)}, u32[]{:S(2)}) copy-start(f32[2048,32]{1,0:T(8,128)} %get-tuple-element.26) | copy-start | bytes 786436
  356.9 6.3 %collective-permute-start.18 = (f32[1,64,64]{2,1,0:T(8,128)S(1)}, f32[1,64,64]{2,1,0:T(8,128)S(1)}, u32[]{:S(2)}, u32[]{:S(2)}) collective-permute-start(f32[1,64,64]{2,1,0:T(8,128)S(1)} %get-tuple-element.33), channel_id=1, source_target_pairs={{0,8},{8,16},{16,24},{24,32},{32,40},{40,48},{48,56},{56,64},{64,7... | collective-permute-start | bytes 49160 | tf_op jit(solution)/shard_map/ppermute | solution.py:21
  361.2 8.6 %collective-permute-start.19 = (f32[1,64,64]{2,1,0:T(8,128)S(1)}, f32[1,64,64]{2,1,0:T(8,128)S(1)}, u32[]{:S(2)}, u32[]{:S(2)}) collective-permute-start(f32[1,64,64]{2,1,0:T(8,128)S(1)} %get-tuple-element.34), channel_id=1, source_target_pairs={{8,0},{16,8},{24,16},{32,24},{40,32},{48,40},{56,48},{64,56},{72,6... | collective-permute-start | bytes 49160 | tf_op jit(solution)/shard_map/ppermute | solution.py:22
  370.1 4.3 %collective-permute-start.20 = (f32[1,64,64]{2,1,0:T(8,128)S(1)}, f32[1,64,64]{2,1,0:T(8,128)S(1)}, u32[]{:S(2)}, u32[]{:S(2)}) collective-permute-start(f32[1,64,64]{2,1,0:T(8,128)S(1)} %get-tuple-element.31), channel_id=1, source_target_pairs={{0,8},{8,16},{16,24},{24,32},{32,40},{40,48},{48,56},{56,64},{64,7... | collective-permute-start | bytes 49160 | tf_op jit(solution)/shard_map/ppermute | solution.py:21
  372.0 8.6 %collective-permute-start.21 = (f32[1,64,64]{2,1,0:T(8,128)S(1)}, f32[1,64,64]{2,1,0:T(8,128)S(1)}, u32[]{:S(2)}, u32[]{:S(2)}) collective-permute-start(f32[1,64,64]{2,1,0:T(8,128)S(1)} %get-tuple-element.32), channel_id=1, source_target_pairs={{8,0},{16,8},{24,16},{32,24},{40,32},{48,40},{56,48},{64,56},{72,6... | collective-permute-start | bytes 49160 | tf_op jit(solution)/shard_map/ppermute | solution.py:22
  383.1 4.3 %collective-permute-start.22 = (f32[1,16,128]{2,1,0:T(8,128)S(1)}, f32[1,16,128]{2,1,0:T(8,128)S(1)}, u32[]{:S(2)}, u32[]{:S(2)}) collective-permute-start(f32[1,16,128]{2,1,0:T(8,128)S(1)} %get-tuple-element.51), channel_id=1, source_target_pairs={{0,8},{8,16},{16,24},{24,32},{32,40},{40,48},{48,56},{56,64},{64,7... | collective-permute-start | bytes 24584 | tf_op jit(solution)/shard_map/ppermute | solution.py:21
  385.0 8.3 %collective-permute-start.23 = (f32[1,16,128]{2,1,0:T(8,128)S(1)}, f32[1,16,128]{2,1,0:T(8,128)S(1)}, u32[]{:S(2)}, u32[]{:S(2)}) collective-permute-start(f32[1,16,128]{2,1,0:T(8,128)S(1)} %get-tuple-element.52), channel_id=1, source_target_pairs={{8,0},{16,8},{24,16},{32,24},{40,32},{48,40},{56,48},{64,56},{72,6... | collective-permute-start | bytes 24584 | tf_op jit(solution)/shard_map/ppermute | solution.py:22
  393.3 4.1 collective-permute-start.24
  396.1 4.3 %collective-permute-start.25 = (f32[6,1,128]{2,1,0:T(1,128)S(1)}, f32[6,1,128]{2,1,0:T(1,128)S(1)}, u32[]{:S(2)}, u32[]{:S(2)}) collective-permute-start(f32[6,1,128]{2,1,0:T(1,128)S(1)} %get-tuple-element.42), channel_id=1, source_target_pairs={{1,0},{2,1},{3,2},{4,3},{5,4},{6,5},{7,6},{9,8},{10,9},{11,10},{12... | collective-permute-start | bytes 9224 | tf_op jit(solution)/shard_map/ppermute | solution.py:22
  400.8 5.3 %collective-permute-start.26 = (f32[1,16,128]{2,1,0:T(8,128)S(1)}, f32[1,16,128]{2,1,0:T(8,128)S(1)}, u32[]{:S(2)}, u32[]{:S(2)}) collective-permute-start(f32[1,16,128]{2,1,0:T(8,128)S(1)} %get-tuple-element.49), channel_id=1, source_target_pairs={{0,8},{8,16},{16,24},{24,32},{32,40},{40,48},{48,56},{56,64},{64,7... | collective-permute-start | bytes 24584 | tf_op jit(solution)/shard_map/ppermute | solution.py:21
  404.2 8.3 %collective-permute-start.27 = (f32[1,16,128]{2,1,0:T(8,128)S(1)}, f32[1,16,128]{2,1,0:T(8,128)S(1)}, u32[]{:S(2)}, u32[]{:S(2)}) collective-permute-start(f32[1,16,128]{2,1,0:T(8,128)S(1)} %get-tuple-element.50), channel_id=1, source_target_pairs={{8,0},{16,8},{24,16},{32,24},{40,32},{48,40},{56,48},{64,56},{72,6... | collective-permute-start | bytes 24584 | tf_op jit(solution)/shard_map/ppermute | solution.py:22
  412.5 4.2 collective-permute-start.28
  415.3 4.6 %collective-permute-start.29 = (f32[6,1,128]{2,1,0:T(1,128)S(1)}, f32[6,1,128]{2,1,0:T(1,128)S(1)}, u32[]{:S(2)}, u32[]{:S(2)}) collective-permute-start(f32[6,1,128]{2,1,0:T(1,128)S(1)} %get-tuple-element.40), channel_id=1, source_target_pairs={{1,0},{2,1},{3,2},{4,3},{5,4},{6,5},{7,6},{9,8},{10,9},{11,10},{12... | collective-permute-start | bytes 9224 | tf_op jit(solution)/shard_map/ppermute | solution.py:22
  (8 other events, 39.3 us)
where the time goes:
time: 422 us; the launch traced here: 421 us
  blocking collectives  209 us (50%)
  starting transfers between devices  105 us (25%)
  waiting for transfers between devices  56.4 us (13%)
  other arithmetic  29.4 us (7%)
  local copies, waits for them, and re-layouts  15.2 us (4%)
  between operations  6.39 us (2%)
    ppermute x15, starting transfers between devices, with_halo(): before = lax.ppermute(last, axis, up)  77.8 us
    ppermute x15, waiting for transfers between devices, with_halo(): after = lax.ppermute(leading, axis, down)  56.4 us
    all_gather x1, blocking collectives, shards(): lax.all_gather(shift_two, 'wide', axis=0, tiled=True)  50.1 us
    all_gather x1, blocking collectives, shards(): lax.all_gather(rhs_two, 'wide', axis=0, tiled=True)  47.8 us
    all_gather x1, blocking collectives, shards(): lax.all_gather(scale_two, 'wide', axis=0, tiled=True)  47.5 us
    ppermute x15, starting transfers between devices, with_halo(): after = lax.ppermute(leading, axis, down)  27.1 us
    all_gather x1, blocking collectives, shards(): lax.all_gather(coarsen(shift_field), 'narrow', axis=1, tiled=True)  25 us
    all_gather x1, blocking collectives, shards(): lax.all_gather(coarsen(fine_resid), 'narrow', axis=1, tiled=True)  19.7 us
  transfers between devices with their start and end apart: 30, of which 11 were waited for; matrix products, arithmetic and copies ran while one was open for 1% of the time, Pallas kernels for 0%

commit v1 on v0

v1 whole, which is shorter than its diff:
```python
import functools

import jax
import jax.numpy as jnp
from jax import lax
from jax.experimental import pallas as pl
from jax.experimental.pallas import tpu as pltpu
from jax.sharding import Mesh, PartitionSpec as P

COARSE = 4
DAMPING = 0.8
F32 = jnp.float32


def dot(a, b):
    high = a.astype(jnp.bfloat16)
    rest = a - high.astype(F32)
    middle = rest.astype(jnp.bfloat16)
    low = (rest - middle.astype(F32)).astype(jnp.bfloat16)
    parts = lax.dot_general(
        jnp.concatenate([high, middle, low], axis=0),
        b.astype(jnp.bfloat16),
        (((1,), (0,)), ((), ())),
        preferred_element_type=F32,
    )
    n = a.shape[0]
    return parts[:n] + parts[n : 2 * n] + parts[2 * n :]


def iota(shape, dim):
    return lax.broadcasted_iota(jnp.int32, shape, dim)


def ones_where(cond, value=1.0):
    return jnp.where(cond, jnp.float32(value), jnp.float32(0.0))


def lane_box(v, period):
    axis = v.ndim - 1
    lane = iota(v.shape[-2:], 1) % period
    below = jnp.where(lane > 0, pltpu.roll(v, 1, axis), 0.0)
    above = jnp.where(lane < period - 1, pltpu.roll(v, 127, axis), 0.0)
    return v + below + above


def relax_weight(scale, shift, level_scale):
    inside = scale > 0.25
    diag = jnp.where(inside, 26.0 * level_scale * scale + shift, 1.0)
    return jnp.where(inside, DAMPING / diag, 0.0)


def fine_apply(v, scale, shift):
    rows = v.shape[1]
    box = v[:-2] + v[1:-1] + v[2:]
    box = box + pltpu.roll(box, 1, 1) + pltpu.roll(box, rows - 1, 1)
    box = lane_box(box, 128)
    mid = v[1:-1]
    return scale * (27.0 * mid - box) + shift * mid


def pair_planes(quads, rows_ref):
    parts = []
    for k, t in enumerate(quads):
        halves = []
        for i in (0, 2):
            at = 40 * (2 * k + i // 2)
            rows_ref[at : at + 40] = t[i] + t[i + 1]
            halves.append(
                rows_ref[pl.ds(at + 4, 16, stride=2)] + rows_ref[pl.ds(at + 5, 16, stride=2)]
            )
        parts.append(jnp.concatenate(halves, axis=1))
    lane, out = iota((256, 128), 0), iota((256, 128), 1)
    pack = ones_where(lane // 2 == out, 0.125)
    return dot(jnp.concatenate(parts, axis=0), pack).reshape(len(quads), 16, 128)


def fine_kernel(
    own_ref, mate_ref, face_ref, iter_ref, field_ref, piece_ref, one_ref, coef_rows, rows_ref
):
    left = lax.axis_index("c") == 0
    blocks = []
    for k in range(3):
        face, mate = face_ref[k], mate_ref[k]
        before, after = jnp.where(left, face, mate), jnp.where(left, mate, face)
        blocks.append(jnp.concatenate([before, own_ref[k], after], axis=0))
    f, a, s = blocks
    coefs = pair_planes([t[4 * p : 4 * p + 4] for t in (a, s) for p in range(3)], coef_rows)
    w = relax_weight(a[1:11], s[1:11], 1.0)
    u = w * f[1:11]
    u = u[1:-1] + w[1:-1] * (f[2:10] - fine_apply(u, a[2:10], s[2:10]))
    iter_ref[...] = u[:, 8:32]
    for k, t in enumerate((f[2:10], a[2:10], s[2:10], w[1:9])):
        field_ref[k] = t[:, 8:32]
    resid = f[4:8] - fine_apply(u[1:7], a[4:8], s[4:8])
    f = pair_planes([resid], rows_ref)
    a, s = coefs[:3], coefs[3:]
    for k, t in enumerate((f[0], a[1], s[1])):
        one_ref[k] = t

    row = iota((16, 128), 0)
    f = jnp.where((row >= 4) & (row < 12), f, 0.0)
    none = jnp.zeros_like(f)
    f = jnp.concatenate([none, f, none], axis=0)
    w = relax_weight(a, s, 0.25)
    v = w * f
    v = v + w * (f - middle_apply(v, a, s))
    resid = f - middle_apply(v, a, s)
    spread = ones_where(iota((128, 128), 1) % 32 == (iota((128, 128), 0) % 64) // 2, 0.125)
    two = row // 2
    group = iota((16, 128), 1) // 32
    own = ones_where(two == group + 2)
    over = ones_where(((two == 1) & (group == 3)) | ((two == 6) & (group == 0)))
    mixed = dot(resid.reshape(48, 128), spread).reshape(3, 16, 128)
    rows = []
    for k in range(3):
        rows += [mixed[k] * own, mixed[k] * over]
    mixed = dot(jnp.concatenate([a[1], s[1]], axis=0), spread).reshape(2, 16, 128)
    rows += [mixed[0] * own, mixed[1] * own]
    piece = jnp.concatenate([jnp.sum(t, axis=0, keepdims=True) for t in rows], axis=0)
    piece_ref[...] = jnp.broadcast_to(piece[None], piece_ref.shape)


def middle_apply(v, scale, shift):
    rows = v.shape[1]
    lane = iota((rows, 128), 1)
    row = iota((rows, 128), 0)
    swap = pltpu.roll(v, 64, 2)
    edge = jnp.zeros_like(swap[:1])
    prev = jnp.concatenate([edge, swap[:-1]], axis=0)
    later = jnp.concatenate([swap[1:], edge], axis=0)
    box = v + swap + jnp.where(lane < 64, prev, later)
    box = (
        box
        + jnp.where(row > 0, pltpu.roll(box, 1, 1), 0.0)
        + jnp.where(row < rows - 1, pltpu.roll(box, rows - 1, 1), 0.0)
    )
    box = lane_box(box, 64)
    return 0.25 * scale * (27.0 * v - box) + shift * v


def quarter_row(shape, dim):
    i = iota(shape, dim)
    return 4 * (i % 8) + i // 8


def quarter_mask():
    return ones_where(iota((4, 8, 128), 2) // 32 == iota((4, 8, 128), 0))


def gather_kernel(got_ref, piece_ref, rows_ref):
    left = lax.axis_index("c") == 0
    half = got_ref.shape[0] // 2
    ranks = half // 8
    rows_ref[: 2 * half] = got_ref[...]

    def column(core, k):
        return rows_ref[pl.ds(core * half + k, ranks, stride=8)]

    lane, row = iota((ranks, 128), 1), iota((ranks, 128), 0)

    def plane(core, p):
        over = column(core, 2 * p + 1)
        down = jnp.where((lane >= 96) & (row < ranks - 1), pltpu.roll(over, ranks - 1, 0), 0.0)
        up = jnp.where((lane < 32) & (row > 0), pltpu.roll(over, 1, 0), 0.0)
        return column(core, 2 * p) + down + up

    fields = [
        jnp.where(left, plane(0, 0), plane(0, 2) + plane(1, 1)),
        jnp.where(left, plane(0, 1) + plane(1, 0), plane(1, 2)),
    ]
    fields += [jnp.where(left, column(0, k), column(1, k)) for k in (6, 7)]
    piece = jnp.concatenate(fields, axis=0)
    piece_ref[...] = jnp.broadcast_to(piece[None], piece_ref.shape)


def smooth_kernel(own_ref, mate_ref, outer_ref, swap_ref, field_ref, iter_ref):
    left = lax.axis_index("c") == 0
    for k in range(3):
        mate, outer, swapped = mate_ref[k], outer_ref[:, k], swap_ref[:, k]
        field_ref[k, 0] = jnp.where(left, outer[0], swapped[1])
        field_ref[k, 1] = jnp.where(left, outer[1], mate)
        field_ref[k, 2] = own_ref[k]
        field_ref[k, 3] = jnp.where(left, mate, outer[0])
        field_ref[k, 4] = jnp.where(left, swapped[0], outer[1])
    f, a, s = (field_ref[k] for k in range(3))
    w = relax_weight(a, s, 0.25)
    field_ref[3] = w
    v = w * f
    iter_ref[...] = v + w * (f - middle_apply(v, a, s))


def coarse_box(v):
    edge = jnp.zeros_like(v[:1])
    box = v + jnp.concatenate([edge, v[:-1]], axis=0) + jnp.concatenate([v[1:], edge], axis=0)
    lane, row = iota((8, 128), 1), iota((8, 128), 0)
    up = pltpu.roll(box, 32, 2)
    up = jnp.where(lane >= 32, up, jnp.where(row > 0, pltpu.roll(up, 1, 1), 0.0))
    down = pltpu.roll(box, 96, 2)
    down = jnp.where(lane < 96, down, jnp.where(row < 7, pltpu.roll(down, 7, 1), 0.0))
    return lane_box(box + up + down, 32)


def total(v):
    plane = jnp.sum(v, axis=0)
    return jnp.sum(jnp.sum(plane, axis=0, keepdims=True), axis=1, keepdims=True)


def last_kernel(
    got_ref, mate_ref, field_ref, middle_ref, fine_ref, iter_ref, out_ref,
    coarse_ref, middle_rows, fine_rows,
):
    nx = lax.axis_size("x")
    chip = lax.axis_index("y") * nx + lax.axis_index("x")
    core = lax.axis_index("c")
    rank = lax.axis_index("z")
    planes = 2 * got_ref.shape[0]

    got, mate = got_ref[...], mate_ref[...]
    halves = jnp.where(core == 0, got, mate), jnp.where(core == 0, mate, got)

    def part(half, k):
        return halves[half][:, 8 * k : 8 * k + 8]

    def pairs(first, second):
        return jnp.concatenate([first[:, None], second[:, None]], axis=1).reshape(planes, 8, 128)

    edge = jnp.zeros_like(part(0, 0)[:1])
    q = pairs(
        part(0, 1) + jnp.concatenate([edge, part(1, 1)[:-1]], axis=0),
        part(1, 0) + jnp.concatenate([part(0, 0)[1:], edge], axis=0),
    )
    a, s = pairs(part(0, 2), part(1, 2)), pairs(part(0, 3), part(1, 3))
    a = 0.0625 * a
    inverse = 1.0 / (26.0 * a + s)
    e = jnp.zeros_like(q)
    for _ in range(COARSE):
        z = q * inverse
        image = a * (27.0 * z - coarse_box(z)) + s * z
        alpha = (total(image * q) / total(image * image))[None]
        e = e + alpha * z
        q = q - alpha * image
    coarse_ref[...] = jnp.zeros_like(coarse_ref)
    coarse_ref[2 : planes + 2] = e
    near = coarse_ref[pl.ds(chip * 2 + core, 5)]

    mask = quarter_mask()
    stack = jnp.concatenate([(near[p][None] * mask).reshape(32, 128) for p in range(5)], axis=0)
    spread = ones_where(iota((128, 128), 0) % 32 == (iota((128, 128), 1) % 64) // 2)
    mixed = dot(stack, spread)
    size = (middle_rows.shape[0] - 16) // 5
    edge = jnp.zeros((4, 128), F32)
    window = []
    for p in range(5):
        at = size * p
        middle_rows[at : at + 4] = edge
        middle_rows[at + size - 4 : at + size] = edge
        for k in range(4):
            t = mixed[32 * p + 8 * k : 32 * p + 8 * k + 8]
            for i in (4, 5):
                middle_rows[pl.ds(at + 2 * k + i, 8, stride=8)] = t
        window.append(middle_rows[pl.ds(pl.multiple_of(at + rank * 8, 8), 16)][None])
    v = middle_ref[...] + jnp.concatenate(window, axis=0)
    f, a, s, w = (field_ref[k] for k in range(4))
    for _ in range(2):
        v = v + w * (f - middle_apply(v, a, s))

    lane, out = iota((128, 256), 0), iota((128, 256), 1)
    mixed = dot(v[1:4].reshape(48, 128), ones_where(lane == out // 2))
    halves = [mixed[:16, 128:], mixed[16:32, :128], mixed[16:32, 128:], mixed[32:, :128]]
    refined = []
    for p, t in enumerate(halves):
        for i in range(2):
            fine_rows[pl.ds(24 * p + i, 12, stride=2)] = t[2:14]
        refined += [fine_rows[24 * p : 24 * p + 24][None]] * 2
    refined = jnp.concatenate(refined, axis=0)

    f, a, s, w = (fine_ref[k] for k in range(4))
    u = iter_ref[...] + jnp.where(a > 0.25, refined, 0.0)
    for i in (1, 2):
        j = 8 - i
        u = u[1:-1] + w[i:j] * (f[i:j] - fine_apply(u, a[i:j], s[i:j]))
    out_ref[...] = u[:, 4:20]


def call(kernel, outs, *args, scratch=()):
    return pl.pallas_call(
        kernel,
        out_shape=[jax.ShapeDtypeStruct(shape, F32) for shape in outs],
        in_specs=[pl.BlockSpec(memory_space=pltpu.VMEM)] * len(args),
        out_specs=[pl.BlockSpec(memory_space=pltpu.VMEM)] * len(outs),
        scratch_shapes=[pltpu.VMEM(shape, F32) for shape in scratch],
        compiler_params=pltpu.CompilerParams(vmem_limit_bytes=24 * 2**20),
    )(*args)


def shards(source, row_scale, shift_field):
    ny, nx, nz = lax.axis_size("y"), lax.axis_size("x"), lax.axis_size("z")
    chips = ny * nx
    first = lax.axis_index("c") == 0

    own = jnp.stack([source, row_scale, shift_field])
    up = [(i, i + 1) for i in range(nz - 1)]
    down = [(i + 1, i) for i in range(nz - 1)]
    before = lax.ppermute(own[:, :, 6:], "z", up)
    after = lax.ppermute(own[:, :, :10], "z", down)
    fill = jnp.zeros((3, 4, 2, 128), F32)
    own = jnp.concatenate([fill, before, own, after, fill], axis=2)
    facing = []
    for i in range(chips - 1):
        facing += [(2 * i + 1, 2 * i + 2), (2 * i + 2, 2 * i + 1)]
    swap = [(0, 1), (1, 0)]
    face = lax.ppermute(own, ("y", "x", "c"), facing)
    mate = lax.ppermute(own, "c", swap)
    fine_iter, fine_fields, sent, one = call(
        fine_kernel,
        [(8, 24, 128), (4, 8, 24, 128), (2 * nz, 8, 128), (3, 16, 128)],
        own, mate, face,
        scratch=[(12 * 40 + 16, 128), (2 * 40 + 16, 128)],
    )

    got = lax.all_to_all(sent, ("c", "z"), 0, 0).reshape(16 * nz, 128)
    (sent,) = call(
        gather_kernel, [(chips, 32, 128)], got, scratch=[(16 * nz + 16, 128)]
    )
    half = lax.all_to_all(sent, ("y", "x"), 0, 0)

    mate = lax.ppermute(one, "c", swap)
    pairs = jnp.stack([jnp.where(first, one, mate), jnp.where(first, mate, one)])
    ring = []
    for i in range(chips - 1):
        ring += [(2 * i, 2 * i + 2), (2 * i + 3, 2 * i + 1)]
    outer = lax.ppermute(pairs, ("y", "x", "c"), ring)
    swapped = lax.ppermute(outer, "c", swap)
    fields, middle_iter = call(
        smooth_kernel, [(4, 5, 16, 128), (5, 16, 128)], one, mate, outer, swapped
    )
    half, fields, middle_iter = lax.optimization_barrier((half, fields, middle_iter))
    half_mate = lax.ppermute(half, "c", swap)
    (result,) = call(
        last_kernel, [source.shape],
        half, half_mate, fields, middle_iter, fine_fields, fine_iter,
        scratch=[(2 * chips + 4, 8, 128), (5 * (8 * nz + 8) + 16, 128), (4 * 24 + 16, 128)],
    )
    return result


def solution(mesh):
    ny, nx = (8, 4) if mesh.devices.shape[0] == 64 else (mesh.devices.shape[0] // 2, 1)
    nz = mesh.devices.shape[1]
    split = Mesh(mesh.devices.reshape(ny, nx, 2, nz), ("y", "x", "c", "z"))
    spec = P(("y", "x", "c"), "z", None)
    return jax.shard_map(
        shards, mesh=split, in_specs=(spec, spec, spec), out_specs=spec, check_vma=False
    )
```

time: 422 us -> 75.7 us (0.18)
  the two profiles are of different devices: /device:TPU:31 before, /device:TPU:1 now
where the time goes in v1:
time: 75.7 us; the launch traced here: 75.2 us
  starting transfers between devices  39 us (52%)
  blocking collectives  16.8 us (22%)
  waiting for transfers between devices  12.6 us (17%)
  Pallas kernels  5.39 us (7%)
  other arithmetic  0.81 us (1%)
    all_to_all x1, blocking collectives, shards(): got = lax.all_to_all(sent, ('c', 'z'), 0, 0).reshape(16 * nz, 128)  16.8 us
    all_to_all x1, starting transfers between devices, shards(): half = lax.all_to_all(sent, ('y', 'x'), 0, 0)  11.1 us
    ppermute x1, starting transfers between devices, shards(): before = lax.ppermute(own[:, :, 6:], 'z', up)  5.46 us
    pallas_call x4, Pallas kernels, call(): pl.pallas_call(kernel, out_shape=[jax.ShapeDtypeStruct(shape, F32) for sh...  5.39 us
    ppermute x1, starting transfers between devices, shards(): half_mate = lax.ppermute(half, 'c', swap)  5.22 us
    ppermute x1, starting transfers between devices, shards(): mate = lax.ppermute(own, 'c', swap)  4.6 us
    ppermute x1, starting transfers between devices, shards(): face = lax.ppermute(own, ('y', 'x', 'c'), facing)  4.53 us
    ppermute x1, waiting for transfers between devices, shards(): outer = lax.ppermute(pairs, ('y', 'x', 'c'), ring)  4.29 us
  transfers between devices with their start and end apart: 9, of which 8 were waited for; matrix products, arithmetic and copies ran while one was open for 0% of the time, Pallas kernels for 0%

profile of v1, /device:TPU:1, one launch (start us, length us, event | category | flops | bytes accessed | tf_op | source)
XLA Modules:
  0.0 75.2 jit_solution(8690965695222731001)
XLA Ops:
  0.0 0.8 %pad_maximum_fusion = f32[3,4,16,128]{3,2,1,0:T(8,128)S(1)} fusion(f32[1,4,16,128]{3,2,1,0:T(8,128)} %bitcast.9, f32[1,4,16,128]{3,2,1,0:T(8,128)} %bitcast.10, f32[1,4,16,128]{3,2,1,0:T(8,128)} %bitcast.11), kind=kLoop, calls=%fused_computation | loop fusion | flops 49152 | bytes 196608 | tf_op jit(solution)/shard_map/stack | solution.py:301
  0.8 1.3 %collective-permute-start.1 = (f32[3,4,10,128]{3,2,1,0:T(8,128)S(1)}, f32[3,4,10,128]{3,2,1,0:T(8,128)S(1)}, u32[]{:S(2)}, u32[]{:S(2)}) collective-permute-start(f32[3,4,10,128]{3,2,1,0:T(8,128)S(1)} %get-tuple-element.23), channel_id=1, source_target_pairs={{1,0},{2,1},{3,2},{4,3},{5,4},{6,5},{7,6},{9,8},{10,9},{11,10},{12... | collective-permute-start | bytes 184328 | tf_op jit(solution)/shard_map/ppermute | solution.py:305
  2.1 5.5 %collective-permute-start = (f32[3,4,10,128]{3,2,1,0:T(8,128)S(1)}, f32[3,4,10,128]{3,2,1,0:T(8,128)S(1)}, u32[]{:S(2)}, u32[]{:S(2)}) collective-permute-start(f32[3,4,10,128]{3,2,1,0:T(8,128)S(1)} %get-tuple-element.24), channel_id=1, source_target_pairs={{0,1},{1,2},{2,3},{3,4},{4,5},{5,6},{6,7},{8,9},{9,10},{10,11},{11... | collective-permute-start | bytes 184328 | tf_op jit(solution)/shard_map/ppermute | solution.py:304
  7.6 0.1 collective-permute-done.1
  7.6 1.6 %collective-permute-done = f32[3,4,10,128]{3,2,1,0:T(8,128)S(1)} collective-permute-done((f32[3,4,10,128]{3,2,1,0:T(8,128)S(1)}, f32[3,4,10,128]{3,2,1,0:T(8,128)S(1)}, u32[]{:S(2)}, u32[]{:S(2)}) %collective-permute-start) | collective-permute-done | bytes 61472 | tf_op jit(solution)/shard_map/ppermute | solution.py:304
  9.2 0.5 concatenate.3.own_ref
  9.7 4.5 %collective-permute-start.3 = (f32[3,4,40,128]{3,2,1,0:T(8,128)S(1)}, f32[3,4,40,128]{3,2,1,0:T(8,128)S(1)}, u32[]{:S(2)}, u32[]{:S(2)}) collective-permute-start(f32[3,4,40,128]{3,2,1,0:T(8,128)S(1)} %concatenate.3.own_ref), channel_id=1, source_target_pairs={{8,16},{16,8},{24,32},{32,24},{40,48},{48,40},{56,64},{64,56},{72,... | collective-permute-start | bytes 737288 | tf_op jit(solution)/shard_map/ppermute | solution.py:312
  14.2 4.6 %collective-permute-start.2 = (f32[3,4,40,128]{3,2,1,0:T(8,128)S(1)}, f32[3,4,40,128]{3,2,1,0:T(8,128)S(1)}, u32[]{:S(2)}, u32[]{:S(2)}) collective-permute-start(f32[3,4,40,128]{3,2,1,0:T(8,128)S(1)} %concatenate.3.own_ref), channel_id=1, source_target_pairs={{0,8},{8,0},{1,9},{9,1},{2,10},{10,2},{3,11},{11,3},{4,12},{12,4},... | collective-permute-start | bytes 737288 | tf_op jit(solution)/shard_map/ppermute | solution.py:313
  18.8 0.0 collective-permute-done.3.face_ref
  18.9 1.1 %collective-permute-done.2.mate_ref = f32[3,4,40,128]{3,2,1,0:T(8,128)S(1)} collective-permute-done((f32[3,4,40,128]{3,2,1,0:T(8,128)S(1)}, f32[3,4,40,128]{3,2,1,0:T(8,128)S(1)}, u32[]{:S(2)}, u32[]{:S(2)}) %collective-permute-start.2) | collective-permute-done | bytes 245792 | tf_op jit(solution)/shard_map/ppermute | solution.py:313
  20.0 1.0 %shard_map.37 = (f32[8,24,128]{2,1,0:T(8,128)S(1)}, f32[4,8,24,128]{3,2,1,0:T(8,128)S(1)}, f32[16,8,128]{2,1,0:T(8,128)S(1)}, f32[3,16,128]{2,1,0:T(8,128)S(1)}) custom-call(f32[3,4,40,128]{3,2,1,0:T(8,128)S(1)} %concatenate.3.own_ref, f32[3,4,40,128]{3,2,1,0:T(8,128)S(1)} %collective-permute-done.2.mate_ref, ...), custom_call_target="tpu_custom_call" | custom-call | tf_op jit(solution)/shard_map/pallas_call | solution.py:286
  20.9 16.8 %all_to_all.10 = f32[16,8,128]{2,1,0:T(8,128)S(1)} all-to-all(f32[16,8,128]{2,1,0:T(8,128)S(1)} %get-tuple-element.14), channel_id=1, replica_groups=mesh['y'=8,'x'=4,'c'=2,'z'=8] {'c','z'}, dimensions={0} | all-to-all | bytes 131072 | tf_op jit(solution)/shard_map/all_to_all | solution.py:321
  37.7 0.9 %shard_map.38 = f32[32,32,128]{2,1,0:T(8,128)} custom-call(f32[128,128]{1,0:T(8,128)S(1)} %bitcast.8), custom_call_target="tpu_custom_call" | custom-call | tf_op jit(solution)/shard_map/pallas_call | solution.py:286
  38.6 11.1 %all-to-all-start.1 = ((f32[32,32,128]{2,1,0:T(8,128)}), f32[32,32,128]{2,1,0:T(8,128)S(1)}, u32[]{:S(2)}, u32[]{:S(2)}) async-start(f32[32,32,128]{2,1,0:T(8,128)} %shard_map.38), calls=%async_computation.1 | async-start | bytes 1048576 | tf_op jit(solution)/shard_map/all_to_all | solution.py:325
  49.6 3.1 %collective-permute-start.4 = (f32[3,16,128]{2,1,0:T(8,128)S(1)}, f32[3,16,128]{2,1,0:T(8,128)S(1)}, u32[]{:S(2)}, u32[]{:S(2)}) collective-permute-start(f32[3,16,128]{2,1,0:T(8,128)S(1)} %get-tuple-element.15.own_ref), channel_id=1, source_target_pairs={{0,8},{8,0},{1,9},{9,1},{2,10},{10,2},{3,11},{11,3},{4,12},{12,4},... | collective-permute-start | bytes 73736 | tf_op jit(solution)/shard_map/ppermute | solution.py:327
  52.7 0.8 %collective-permute-done.4.mate_ref = f32[3,16,128]{2,1,0:T(8,128)S(1)} collective-permute-done((f32[3,16,128]{2,1,0:T(8,128)S(1)}, f32[3,16,128]{2,1,0:T(8,128)S(1)}, u32[]{:S(2)}, u32[]{:S(2)}) %collective-permute-start.4) | collective-permute-done | bytes 24608 | tf_op jit(solution)/shard_map/ppermute | solution.py:327
  53.6 1.3 %collective-permute-start.5 = (f32[2,3,16,128]{3,2,1,0:T(8,128)S(1)}, f32[2,3,16,128]{3,2,1,0:T(8,128)S(1)}, u32[]{:S(2)}, u32[]{:S(2)}) collective-permute-start(f32[2,3,16,128]{3,2,1,0:T(8,128)S(1)} %pad_maximum_fusion.1), channel_id=1, source_target_pairs={{0,16},{24,8},{16,32},{40,24},{32,48},{56,40},{48,64},{72,56},{64,... | collective-permute-start | bytes 147464 | tf_op jit(solution)/shard_map/ppermute | solution.py:332
  54.9 4.3 %collective-permute-done.5.outer_ref = f32[2,3,16,128]{3,2,1,0:T(8,128)S(1)} collective-permute-done((f32[2,3,16,128]{3,2,1,0:T(8,128)S(1)}, f32[2,3,16,128]{3,2,1,0:T(8,128)S(1)}, u32[]{:S(2)}, u32[]{:S(2)}) %collective-permute-start.5) | collective-permute-done | bytes 49184 | tf_op jit(solution)/shard_map/ppermute | solution.py:332
  59.2 2.5 %collective-permute-start.6 = (f32[2,3,16,128]{3,2,1,0:T(8,128)S(1)}, f32[2,3,16,128]{3,2,1,0:T(8,128)S(1)}, u32[]{:S(2)}, u32[]{:S(2)}) collective-permute-start(f32[2,3,16,128]{3,2,1,0:T(8,128)S(1)} %collective-permute-done.5.outer_ref), channel_id=1, source_target_pairs={{0,8},{8,0},{1,9},{9,1},{2,10},{10,2},{3,11},{11,3},{4,12},{12,4},... | collective-permute-start | bytes 147464 | tf_op jit(solution)/shard_map/ppermute | solution.py:333
  61.6 0.9 %collective-permute-done.6.swap_ref = f32[2,3,16,128]{3,2,1,0:T(8,128)S(1)} collective-permute-done((f32[2,3,16,128]{3,2,1,0:T(8,128)S(1)}, f32[2,3,16,128]{3,2,1,0:T(8,128)S(1)}, u32[]{:S(2)}, u32[]{:S(2)}) %collective-permute-start.6) | collective-permute-done | bytes 49184 | tf_op jit(solution)/shard_map/ppermute | solution.py:333
  62.5 0.2 shard_map.39
  62.7 2.4 %all-to-all-done.1.got_ref = f32[32,32,128]{2,1,0:T(8,128)S(1)} async-done(((f32[32,32,128]{2,1,0:T(8,128)}), f32[32,32,128]{2,1,0:T(8,128)S(1)}, u32[]{:S(2)}, u32[]{:S(2)}) %all-to-all-start.1) | async-done | bytes 524320 | tf_op jit(solution)/shard_map/all_to_all | solution.py:325
  65.1 5.2 %collective-permute-start.7 = (f32[32,32,128]{2,1,0:T(8,128)S(1)}, f32[32,32,128]{2,1,0:T(8,128)S(1)}, u32[]{:S(2)}, u32[]{:S(2)}) collective-permute-start(f32[32,32,128]{2,1,0:T(8,128)S(1)} %all-to-all-done.1.got_ref), channel_id=1, source_target_pairs={{0,8},{8,0},{1,9},{9,1},{2,10},{10,2},{3,11},{11,3},{4,12},{12,4},... | collective-permute-start | bytes 1572872 | tf_op jit(solution)/shard_map/ppermute | solution.py:338
  70.3 1.5 %collective-permute-done.7.mate_ref = f32[32,32,128]{2,1,0:T(8,128)S(1)} collective-permute-done((f32[32,32,128]{2,1,0:T(8,128)S(1)}, f32[32,32,128]{2,1,0:T(8,128)S(1)}, u32[]{:S(2)}, u32[]{:S(2)}) %collective-permute-start.7) | collective-permute-done | bytes 524320 | tf_op jit(solution)/shard_map/ppermute | solution.py:338
  71.8 3.4 %shard_map.40 = f32[4,16,128]{2,1,0:T(8,128)} custom-call(f32[32,32,128]{2,1,0:T(8,128)S(1)} %all-to-all-done.1.got_ref, f32[32,32,128]{2,1,0:T(8,128)S(1)} %collective-permute-done.7.mate_ref, f32[4,5,16,128]{3,2,1,0:T(8,128)S(1)} %get-tuple-element.19.field_ref, f32[5,16,128]{2,1,0:T(8,128)S(1)} %get-tuple-element.20.middle_ref, ...), custom_call_target="tpu_custom_call" | custom-call | tf_op jit(solution)/shard_map/pallas_call | solution.py:286
  (4 shorter events, 0.0 us)
Async XLA Ops:
  0.8 6.8 %collective-permute-start.1 = (f32[3,4,10,128]{3,2,1,0:T(8,128)S(1)}, f32[3,4,10,128]{3,2,1,0:T(8,128)S(1)}, u32[]{:S(2)}, u32[]{:S(2)}) collective-permute-start(f32[3,4,10,128]{3,2,1,0:T(8,128)S(1)} %get-tuple-element.23), channel_id=1, source_target_pairs={{1,0},{2,1},{3,2},{4,3},{5,4},{6,5},{7,6},{9,8},{10,9},{11,10},{12... | collective-permute-start | bytes 184328 | tf_op jit(solution)/shard_map/ppermute | solution.py:305
  2.1 7.1 %collective-permute-start = (f32[3,4,10,128]{3,2,1,0:T(8,128)S(1)}, f32[3,4,10,128]{3,2,1,0:T(8,128)S(1)}, u32[]{:S(2)}, u32[]{:S(2)}) collective-permute-start(f32[3,4,10,128]{3,2,1,0:T(8,128)S(1)} %get-tuple-element.24), channel_id=1, source_target_pairs={{0,1},{1,2},{2,3},{3,4},{4,5},{5,6},{6,7},{8,9},{9,10},{10,11},{11... | collective-permute-start | bytes 184328 | tf_op jit(solution)/shard_map/ppermute | solution.py:304
  9.7 9.1 %collective-permute-start.3 = (f32[3,4,40,128]{3,2,1,0:T(8,128)S(1)}, f32[3,4,40,128]{3,2,1,0:T(8,128)S(1)}, u32[]{:S(2)}, u32[]{:S(2)}) collective-permute-start(f32[3,4,40,128]{3,2,1,0:T(8,128)S(1)} %concatenate.3.own_ref), channel_id=1, source_target_pairs={{8,16},{16,8},{24,32},{32,24},{40,48},{48,40},{56,64},{64,56},{72,... | collective-permute-start | bytes 737288 | tf_op jit(solution)/shard_map/ppermute | solution.py:312
  14.2 5.7 %collective-permute-start.2 = (f32[3,4,40,128]{3,2,1,0:T(8,128)S(1)}, f32[3,4,40,128]{3,2,1,0:T(8,128)S(1)}, u32[]{:S(2)}, u32[]{:S(2)}) collective-permute-start(f32[3,4,40,128]{3,2,1,0:T(8,128)S(1)} %concatenate.3.own_ref), channel_id=1, source_target_pairs={{0,8},{8,0},{1,9},{9,1},{2,10},{10,2},{3,11},{11,3},{4,12},{12,4},... | collective-permute-start | bytes 737288 | tf_op jit(solution)/shard_map/ppermute | solution.py:313
  38.6 26.5 %all-to-all-start.1 = ((f32[32,32,128]{2,1,0:T(8,128)}), f32[32,32,128]{2,1,0:T(8,128)S(1)}, u32[]{:S(2)}, u32[]{:S(2)}) async-start(f32[32,32,128]{2,1,0:T(8,128)} %shard_map.38), calls=%async_computation.1 | async-start | bytes 1048576 | tf_op jit(solution)/shard_map/all_to_all | solution.py:325
  49.6 3.9 %collective-permute-start.4 = (f32[3,16,128]{2,1,0:T(8,128)S(1)}, f32[3,16,128]{2,1,0:T(8,128)S(1)}, u32[]{:S(2)}, u32[]{:S(2)}) collective-permute-start(f32[3,16,128]{2,1,0:T(8,128)S(1)} %get-tuple-element.15.own_ref), channel_id=1, source_target_pairs={{0,8},{8,0},{1,9},{9,1},{2,10},{10,2},{3,11},{11,3},{4,12},{12,4},... | collective-permute-start | bytes 73736 | tf_op jit(solution)/shard_map/ppermute | solution.py:327
  53.6 5.6 %collective-permute-start.5 = (f32[2,3,16,128]{3,2,1,0:T(8,128)S(1)}, f32[2,3,16,128]{3,2,1,0:T(8,128)S(1)}, u32[]{:S(2)}, u32[]{:S(2)}) collective-permute-start(f32[2,3,16,128]{3,2,1,0:T(8,128)S(1)} %pad_maximum_fusion.1), channel_id=1, source_target_pairs={{0,16},{24,8},{16,32},{40,24},{32,48},{56,40},{48,64},{72,56},{64,... | collective-permute-start | bytes 147464 | tf_op jit(solution)/shard_map/ppermute | solution.py:332
  59.2 3.3 %collective-permute-start.6 = (f32[2,3,16,128]{3,2,1,0:T(8,128)S(1)}, f32[2,3,16,128]{3,2,1,0:T(8,128)S(1)}, u32[]{:S(2)}, u32[]{:S(2)}) collective-permute-start(f32[2,3,16,128]{3,2,1,0:T(8,128)S(1)} %collective-permute-done.5.outer_ref), channel_id=1, source_target_pairs={{0,8},{8,0},{1,9},{9,1},{2,10},{10,2},{3,11},{11,3},{4,12},{12,4},... | collective-permute-start | bytes 147464 | tf_op jit(solution)/shard_map/ppermute | solution.py:333
  65.1 6.7 %collective-permute-start.7 = (f32[32,32,128]{2,1,0:T(8,128)S(1)}, f32[32,32,128]{2,1,0:T(8,128)S(1)}, u32[]{:S(2)}, u32[]{:S(2)}) collective-permute-start(f32[32,32,128]{2,1,0:T(8,128)S(1)} %all-to-all-done.1.got_ref), channel_id=1, source_target_pairs={{0,8},{8,0},{1,9},{9,1},{2,10},{10,2},{3,11},{11,3},{4,12},{12,4},... | collective-permute-start | bytes 1572872 | tf_op jit(solution)/shard_map/ppermute | solution.py:338

commit v2 on v1

--- a/solution.py
+++ b/solution.py
@@ -97,8 +97,6 @@
     for k, t in enumerate((f[0], a[1], s[1])):
         one_ref[k] = t
 
-    row = iota((16, 128), 0)
-    f = jnp.where((row >= 4) & (row < 12), f, 0.0)
     none = jnp.zeros_like(f)
     f = jnp.concatenate([none, f, none], axis=0)
     w = relax_weight(a, s, 0.25)
@@ -106,16 +104,11 @@
     v = v + w * (f - middle_apply(v, a, s))
     resid = f - middle_apply(v, a, s)
     spread = ones_where(iota((128, 128), 1) % 32 == (iota((128, 128), 0) % 64) // 2, 0.125)
-    two = row // 2
-    group = iota((16, 128), 1) // 32
-    own = ones_where(two == group + 2)
-    over = ones_where(((two == 1) & (group == 3)) | ((two == 6) & (group == 0)))
+    own = ones_where(iota((16, 128), 0) // 2 == iota((16, 128), 1) // 32 + 2)
     mixed = dot(resid.reshape(48, 128), spread).reshape(3, 16, 128)
-    rows = []
-    for k in range(3):
-        rows += [mixed[k] * own, mixed[k] * over]
+    rows = [mixed[k] * own for k in range(3)]
     mixed = dot(jnp.concatenate([a[1], s[1]], axis=0), spread).reshape(2, 16, 128)
-    rows += [mixed[0] * own, mixed[1] * own]
+    rows += [mixed[k] * own for k in range(2)] + [jnp.zeros((1, 128), F32)] * 3
     piece = jnp.concatenate([jnp.sum(t, axis=0, keepdims=True) for t in rows], axis=0)
     piece_ref[...] = jnp.broadcast_to(piece[None], piece_ref.shape)
 
@@ -148,40 +141,35 @@
 
 
 def gather_kernel(got_ref, piece_ref, rows_ref):
-    left = lax.axis_index("c") == 0
+    core = lax.axis_index("c")
     half = got_ref.shape[0] // 2
-    ranks = half // 8
     rows_ref[: 2 * half] = got_ref[...]
 
-    def column(core, k):
-        return rows_ref[pl.ds(core * half + k, ranks, stride=8)]
-
-    lane, row = iota((ranks, 128), 1), iota((ranks, 128), 0)
-
-    def plane(core, p):
-        over = column(core, 2 * p + 1)
-        down = jnp.where((lane >= 96) & (row < ranks - 1), pltpu.roll(over, ranks - 1, 0), 0.0)
-        up = jnp.where((lane < 32) & (row > 0), pltpu.roll(over, 1, 0), 0.0)
-        return column(core, 2 * p) + down + up
-
-    fields = [
-        jnp.where(left, plane(0, 0), plane(0, 2) + plane(1, 1)),
-        jnp.where(left, plane(0, 1) + plane(1, 0), plane(1, 2)),
-    ]
-    fields += [jnp.where(left, column(0, k), column(1, k)) for k in (6, 7)]
-    piece = jnp.concatenate(fields, axis=0)
+    def column(at, k):
+        return rows_ref[pl.ds(at * half + k, half // 8, stride=8)]
+
+    outward = 2 * core
+    piece = jnp.concatenate(
+        [
+            column(core, outward),
+            column(core, 1) + column(1 - core, outward),
+            column(core, 3),
+            column(core, 4),
+        ],
+        axis=0,
+    )
     piece_ref[...] = jnp.broadcast_to(piece[None], piece_ref.shape)
 
 
-def smooth_kernel(own_ref, mate_ref, outer_ref, swap_ref, field_ref, iter_ref):
+def smooth_kernel(own_ref, mate_ref, outer_ref, inner_ref, field_ref, iter_ref):
     left = lax.axis_index("c") == 0
     for k in range(3):
-        mate, outer, swapped = mate_ref[k], outer_ref[:, k], swap_ref[:, k]
-        field_ref[k, 0] = jnp.where(left, outer[0], swapped[1])
+        mate, outer, inner = mate_ref[k], outer_ref[:, k], inner_ref[k]
+        field_ref[k, 0] = jnp.where(left, outer[0], inner)
         field_ref[k, 1] = jnp.where(left, outer[1], mate)
         field_ref[k, 2] = own_ref[k]
         field_ref[k, 3] = jnp.where(left, mate, outer[0])
-        field_ref[k, 4] = jnp.where(left, swapped[0], outer[1])
+        field_ref[k, 4] = jnp.where(left, inner, outer[1])
     f, a, s = (field_ref[k] for k in range(3))
     w = relax_weight(a, s, 0.25)
     field_ref[3] = w
@@ -190,8 +178,7 @@
 
 
 def coarse_box(v):
-    edge = jnp.zeros_like(v[:1])
-    box = v + jnp.concatenate([edge, v[:-1]], axis=0) + jnp.concatenate([v[1:], edge], axis=0)
+    box = v[:-2] + v[1:-1] + v[2:]
     lane, row = iota((8, 128), 1), iota((8, 128), 0)
     up = pltpu.roll(box, 32, 2)
     up = jnp.where(lane >= 32, up, jnp.where(row > 0, pltpu.roll(up, 1, 1), 0.0))
@@ -200,14 +187,49 @@
     return lane_box(box + up + down, 32)
 
 
-def total(v):
-    plane = jnp.sum(v, axis=0)
+def total(plane):
     return jnp.sum(jnp.sum(plane, axis=0, keepdims=True), axis=1, keepdims=True)
+
+
+def solve_coarse(q_ref, a_ref, d_ref, inverse_ref, z_ref, image_ref, e_ref):
+    planes = q_ref.shape[0]
+    chunk = 8 if planes % 8 == 0 else 2
+    starts = range(0, planes, chunk)
+    none = jnp.zeros((1, 8, 128), F32)
+    z_ref[:1] = none
+    z_ref[planes + 1 :] = none
+    for i in (0, 1, planes + 2, planes + 3):
+        e_ref[i : i + 1] = none
+    for i in starts:
+        own = slice(i, i + chunk)
+        inverse = 1.0 / (d_ref[own] - a_ref[own])
+        inverse_ref[own] = inverse
+        z_ref[i + 1 : i + chunk + 1] = q_ref[own] * inverse
+    for step in range(COARSE):
+        upper = lower = jnp.zeros((8, 128), F32)
+        for i in starts:
+            own = slice(i, i + chunk)
+            z = z_ref[i : i + chunk + 2]
+            image = d_ref[own] * z[1:-1] - a_ref[own] * coarse_box(z)
+            image_ref[own] = image
+            upper = upper + jnp.sum(image * q_ref[own], axis=0)
+            lower = lower + jnp.sum(image * image, axis=0)
+        alpha = (total(upper) / total(lower))[None]
+        for i in starts:
+            own = slice(i, i + chunk)
+            inner = slice(i + 1, i + chunk + 1)
+            outer = slice(i + 2, i + chunk + 2)
+            gain = alpha * z_ref[inner]
+            e_ref[outer] = gain if step == 0 else e_ref[outer] + gain
+            if step < COARSE - 1:
+                q = q_ref[own] - alpha * image_ref[own]
+                q_ref[own] = q
+                z_ref[inner] = q * inverse_ref[own]
 
 
 def last_kernel(
     got_ref, mate_ref, field_ref, middle_ref, fine_ref, iter_ref, out_ref,
-    coarse_ref, middle_rows, fine_rows,
+    q_ref, a_ref, d_ref, inverse_ref, z_ref, image_ref, coarse_ref, middle_rows, fine_rows,
 ):
     nx = lax.axis_size("x")
     chip = lax.axis_index("y") * nx + lax.axis_index("x")
@@ -225,22 +247,14 @@
         return jnp.concatenate([first[:, None], second[:, None]], axis=1).reshape(planes, 8, 128)
 
     edge = jnp.zeros_like(part(0, 0)[:1])
-    q = pairs(
-        part(0, 1) + jnp.concatenate([edge, part(1, 1)[:-1]], axis=0),
-        part(1, 0) + jnp.concatenate([part(0, 0)[1:], edge], axis=0),
-    )
-    a, s = pairs(part(0, 2), part(1, 2)), pairs(part(0, 3), part(1, 3))
-    a = 0.0625 * a
-    inverse = 1.0 / (26.0 * a + s)
-    e = jnp.zeros_like(q)
-    for _ in range(COARSE):
-        z = q * inverse
-        image = a * (27.0 * z - coarse_box(z)) + s * z
-        alpha = (total(image * q) / total(image * image))[None]
-        e = e + alpha * z
-        q = q - alpha * image
-    coarse_ref[...] = jnp.zeros_like(coarse_ref)
-    coarse_ref[2 : planes + 2] = e
+    q_ref[...] = pairs(
+        part(0, 1) + jnp.concatenate([edge, part(1, 0)[:-1]], axis=0),
+        part(1, 1) + jnp.concatenate([part(0, 0)[1:], edge], axis=0),
+    )
+    a = 0.0625 * pairs(part(0, 2), part(1, 2))
+    a_ref[...] = a
+    d_ref[...] = 27.0 * a + pairs(part(0, 3), part(1, 3))
+    solve_coarse(q_ref, a_ref, d_ref, inverse_ref, z_ref, image_ref, coarse_ref)
     near = coarse_ref[pl.ds(chip * 2 + core, 5)]
 
     mask = quarter_mask()
@@ -322,6 +336,7 @@
     (sent,) = call(
         gather_kernel, [(chips, 32, 128)], got, scratch=[(16 * nz + 16, 128)]
     )
+    one, sent = lax.optimization_barrier((one, sent))
     half = lax.all_to_all(sent, ("y", "x"), 0, 0)
 
     mate = lax.ppermute(one, "c", swap)
@@ -330,16 +345,18 @@
     for i in range(chips - 1):
         ring += [(2 * i, 2 * i + 2), (2 * i + 3, 2 * i + 1)]
     outer = lax.ppermute(pairs, ("y", "x", "c"), ring)
-    swapped = lax.ppermute(outer, "c", swap)
+    inner = lax.ppermute(one, ("y", "x", "c"), [(j, i) for i, j in ring])
     fields, middle_iter = call(
-        smooth_kernel, [(4, 5, 16, 128), (5, 16, 128)], one, mate, outer, swapped
+        smooth_kernel, [(4, 5, 16, 128), (5, 16, 128)], one, mate, outer, inner
     )
     half, fields, middle_iter = lax.optimization_barrier((half, fields, middle_iter))
     half_mate = lax.ppermute(half, "c", swap)
     (result,) = call(
         last_kernel, [source.shape],
         half, half_mate, fields, middle_iter, fine_fields, fine_iter,
-        scratch=[(2 * chips + 4, 8, 128), (5 * (8 * nz + 8) + 16, 128), (4 * 24 + 16, 128)],
+        scratch=[(2 * chips, 8, 128)] * 4
+        + [(2 * chips + 2, 8, 128), (2 * chips, 8, 128), (2 * chips + 4, 8, 128)]
+        + [(5 * (8 * nz + 8) + 16, 128), (4 * 24 + 16, 128)],
     )
     return result
 

time: 75.7 us -> 75.7 us (level)
  starting transfers between devices: 39 us -> 40.6 us
  waiting for transfers between devices: 12.6 us -> 11 us
    ppermute x1, waiting for transfers between devices: 4.29 us -> 0.01 us  [shards(): outer = lax.ppermute(pairs, ('y', 'x', 'c'), ring)]
    all_to_all x1, waiting for transfers between devices: 2.37 us -> 5.02 us  [shards(): half = lax.all_to_all(sent, ('y', 'x'), 0, 0)]
    ppermute x1, starting transfers between devices: 2.48 us -> 4.04 us  [shards(): inner = lax.ppermute(one, ('y', 'x', 'c'), [(j, i) for i, j in ring])]
  transfers between devices with their start and end apart: 9 -> 9, of which waited for: 8 -> 7; matrix products, arithmetic and copies ran while one was open for 0% -> 0% of each run, Pallas kernels for 0% -> 0%
where the time goes in v2:
time: 75.7 us; the launch traced here: 75.2 us
  starting transfers between devices  40.6 us (54%)
  blocking collectives  16.8 us (22%)
  waiting for transfers between devices  11 us (15%)
  Pallas kernels  5.41 us (7%)
  other arithmetic  0.81 us (1%)
    all_to_all x1, blocking collectives, shards(): got = lax.all_to_all(sent, ('c', 'z'), 0, 0).reshape(16 * nz, 128)  16.8 us
    all_to_all x1, starting transfers between devices, shards(): half = lax.all_to_all(sent, ('y', 'x'), 0, 0)  11.1 us
    ppermute x1, starting transfers between devices, shards(): before = lax.ppermute(own[:, :, 6:], 'z', up)  5.46 us
    pallas_call x4, Pallas kernels, call(): pl.pallas_call(kernel, out_shape=[jax.ShapeDtypeStruct(shape, F32) for sh...  5.41 us
    ppermute x1, starting transfers between devices, shards(): half_mate = lax.ppermute(half, 'c', swap)  5.22 us
    all_to_all x1, waiting for transfers between devices, shards(): half = lax.all_to_all(sent, ('y', 'x'), 0, 0)  5.02 us
    ppermute x1, starting transfers between devices, shards(): mate = lax.ppermute(own, 'c', swap)  4.6 us
    ppermute x1, starting transfers between devices, shards(): face = lax.ppermute(own, ('y', 'x', 'c'), facing)  4.53 us
  transfers between devices with their start and end apart: 9, of which 7 were waited for; matrix products, arithmetic and copies ran while one was open for 0% of the time, Pallas kernels for 0%

profile of v2, /device:TPU:1, one launch (start us, length us, event | category | flops | bytes accessed | tf_op | source)
XLA Modules:
  0.0 75.2 jit_solution(3480009505257870989)
XLA Ops:
  0.0 0.8 %pad_maximum_fusion = f32[3,4,16,128]{3,2,1,0:T(8,128)S(1)} fusion(f32[1,4,16,128]{3,2,1,0:T(8,128)} %bitcast.9, f32[1,4,16,128]{3,2,1,0:T(8,128)} %bitcast.10, f32[1,4,16,128]{3,2,1,0:T(8,128)} %bitcast.11), kind=kLoop, calls=%fused_computation | loop fusion | flops 49152 | bytes 196608 | tf_op jit(solution)/shard_map/stack | solution.py:315
  0.8 1.3 %collective-permute-start.1 = (f32[3,4,10,128]{3,2,1,0:T(8,128)S(1)}, f32[3,4,10,128]{3,2,1,0:T(8,128)S(1)}, u32[]{:S(2)}, u32[]{:S(2)}) collective-permute-start(f32[3,4,10,128]{3,2,1,0:T(8,128)S(1)} %get-tuple-element.27), channel_id=1, source_target_pairs={{1,0},{2,1},{3,2},{4,3},{5,4},{6,5},{7,6},{9,8},{10,9},{11,10},{12... | collective-permute-start | bytes 184328 | tf_op jit(solution)/shard_map/ppermute | solution.py:319
  2.1 5.5 %collective-permute-start = (f32[3,4,10,128]{3,2,1,0:T(8,128)S(1)}, f32[3,4,10,128]{3,2,1,0:T(8,128)S(1)}, u32[]{:S(2)}, u32[]{:S(2)}) collective-permute-start(f32[3,4,10,128]{3,2,1,0:T(8,128)S(1)} %get-tuple-element.28), channel_id=1, source_target_pairs={{0,1},{1,2},{2,3},{3,4},{4,5},{5,6},{6,7},{8,9},{9,10},{10,11},{11... | collective-permute-start | bytes 184328 | tf_op jit(solution)/shard_map/ppermute | solution.py:318
  7.6 0.1 collective-permute-done.1
  7.6 1.6 %collective-permute-done = f32[3,4,10,128]{3,2,1,0:T(8,128)S(1)} collective-permute-done((f32[3,4,10,128]{3,2,1,0:T(8,128)S(1)}, f32[3,4,10,128]{3,2,1,0:T(8,128)S(1)}, u32[]{:S(2)}, u32[]{:S(2)}) %collective-permute-start) | collective-permute-done | bytes 61472 | tf_op jit(solution)/shard_map/ppermute | solution.py:318
  9.2 0.5 concatenate.3.own_ref
  9.7 4.5 %collective-permute-start.3 = (f32[3,4,40,128]{3,2,1,0:T(8,128)S(1)}, f32[3,4,40,128]{3,2,1,0:T(8,128)S(1)}, u32[]{:S(2)}, u32[]{:S(2)}) collective-permute-start(f32[3,4,40,128]{3,2,1,0:T(8,128)S(1)} %concatenate.3.own_ref), channel_id=1, source_target_pairs={{8,16},{16,8},{24,32},{32,24},{40,48},{48,40},{56,64},{64,56},{72,... | collective-permute-start | bytes 737288 | tf_op jit(solution)/shard_map/ppermute | solution.py:326
  14.2 4.6 %collective-permute-start.2 = (f32[3,4,40,128]{3,2,1,0:T(8,128)S(1)}, f32[3,4,40,128]{3,2,1,0:T(8,128)S(1)}, u32[]{:S(2)}, u32[]{:S(2)}) collective-permute-start(f32[3,4,40,128]{3,2,1,0:T(8,128)S(1)} %concatenate.3.own_ref), channel_id=1, source_target_pairs={{0,8},{8,0},{1,9},{9,1},{2,10},{10,2},{3,11},{11,3},{4,12},{12,4},... | collective-permute-start | bytes 737288 | tf_op jit(solution)/shard_map/ppermute | solution.py:327
  18.8 0.0 collective-permute-done.3.face_ref
  18.9 1.1 %collective-permute-done.2.mate_ref = f32[3,4,40,128]{3,2,1,0:T(8,128)S(1)} collective-permute-done((f32[3,4,40,128]{3,2,1,0:T(8,128)S(1)}, f32[3,4,40,128]{3,2,1,0:T(8,128)S(1)}, u32[]{:S(2)}, u32[]{:S(2)}) %collective-permute-start.2) | collective-permute-done | bytes 245792 | tf_op jit(solution)/shard_map/ppermute | solution.py:327
  20.0 1.0 %shard_map.37 = (f32[8,24,128]{2,1,0:T(8,128)S(1)}, f32[4,8,24,128]{3,2,1,0:T(8,128)S(1)}, f32[16,8,128]{2,1,0:T(8,128)S(1)}, f32[3,16,128]{2,1,0:T(8,128)S(1)}) custom-call(f32[3,4,40,128]{3,2,1,0:T(8,128)S(1)} %concatenate.3.own_ref, f32[3,4,40,128]{3,2,1,0:T(8,128)S(1)} %collective-permute-done.2.mate_ref, ...), custom_call_target="tpu_custom_call" | custom-call | tf_op jit(solution)/shard_map/pallas_call | solution.py:300
  20.9 16.8 %all_to_all.10 = f32[16,8,128]{2,1,0:T(8,128)S(1)} all-to-all(f32[16,8,128]{2,1,0:T(8,128)S(1)} %get-tuple-element.17), channel_id=1, replica_groups=mesh['y'=8,'x'=4,'c'=2,'z'=8] {'c','z'}, dimensions={0} | all-to-all | bytes 131072 | tf_op jit(solution)/shard_map/all_to_all | solution.py:335
  37.7 0.9 %shard_map.38 = f32[32,32,128]{2,1,0:T(8,128)} custom-call(f32[128,128]{1,0:T(8,128)S(1)} %bitcast.8), custom_call_target="tpu_custom_call" | custom-call | tf_op jit(solution)/shard_map/pallas_call | solution.py:300
  38.6 11.1 %all-to-all-start.1 = ((f32[32,32,128]{2,1,0:T(8,128)}), f32[32,32,128]{2,1,0:T(8,128)S(1)}, u32[]{:S(2)}, u32[]{:S(2)}) async-start(f32[32,32,128]{2,1,0:T(8,128)} %shard_map.38), calls=%async_computation.1 | async-start | bytes 1048576 | tf_op jit(solution)/shard_map/all_to_all | solution.py:340
  49.6 3.1 %collective-permute-start.4 = (f32[3,16,128]{2,1,0:T(8,128)S(1)}, f32[3,16,128]{2,1,0:T(8,128)S(1)}, u32[]{:S(2)}, u32[]{:S(2)}) collective-permute-start(f32[3,16,128]{2,1,0:T(8,128)S(1)} %get-tuple-element.19.own_ref), channel_id=1, source_target_pairs={{0,8},{8,0},{1,9},{9,1},{2,10},{10,2},{3,11},{11,3},{4,12},{12,4},... | collective-permute-start | bytes 73736 | tf_op jit(solution)/shard_map/ppermute | solution.py:342
  52.7 0.8 %collective-permute-done.4.mate_ref = f32[3,16,128]{2,1,0:T(8,128)S(1)} collective-permute-done((f32[3,16,128]{2,1,0:T(8,128)S(1)}, f32[3,16,128]{2,1,0:T(8,128)S(1)}, u32[]{:S(2)}, u32[]{:S(2)}) %collective-permute-start.4) | collective-permute-done | bytes 24608 | tf_op jit(solution)/shard_map/ppermute | solution.py:342
  53.6 1.3 %collective-permute-start.5 = (f32[2,3,16,128]{3,2,1,0:T(8,128)S(1)}, f32[2,3,16,128]{3,2,1,0:T(8,128)S(1)}, u32[]{:S(2)}, u32[]{:S(2)}) collective-permute-start(f32[2,3,16,128]{3,2,1,0:T(8,128)S(1)} %pad_maximum_fusion.1), channel_id=1, source_target_pairs={{0,16},{24,8},{16,32},{40,24},{32,48},{56,40},{48,64},{72,56},{64,... | collective-permute-start | bytes 147464 | tf_op jit(solution)/shard_map/ppermute | solution.py:347
  54.9 4.0 %collective-permute-start.6 = (f32[3,16,128]{2,1,0:T(8,128)S(1)}, f32[3,16,128]{2,1,0:T(8,128)S(1)}, u32[]{:S(2)}, u32[]{:S(2)}) collective-permute-start(f32[3,16,128]{2,1,0:T(8,128)S(1)} %get-tuple-element.19.own_ref), channel_id=1, source_target_pairs={{16,0},{8,24},{32,16},{24,40},{48,32},{40,56},{64,48},{56,72},{80,... | collective-permute-start | bytes 73736 | tf_op jit(solution)/shard_map/ppermute | solution.py:348
  58.9 0.9 %collective-permute-done.6.inner_ref = f32[3,16,128]{2,1,0:T(8,128)S(1)} collective-permute-done((f32[3,16,128]{2,1,0:T(8,128)S(1)}, f32[3,16,128]{2,1,0:T(8,128)S(1)}, u32[]{:S(2)}, u32[]{:S(2)}) %collective-permute-start.6) | collective-permute-done | bytes 24608 | tf_op jit(solution)/shard_map/ppermute | solution.py:348
  59.9 0.0 collective-permute-done.5.outer_ref
  59.9 0.2 shard_map.39
  60.1 5.0 %all-to-all-done.1.got_ref = f32[32,32,128]{2,1,0:T(8,128)S(1)} async-done(((f32[32,32,128]{2,1,0:T(8,128)}), f32[32,32,128]{2,1,0:T(8,128)S(1)}, u32[]{:S(2)}, u32[]{:S(2)}) %all-to-all-start.1) | async-done | bytes 524320 | tf_op jit(solution)/shard_map/all_to_all | solution.py:340
  65.1 5.2 %collective-permute-start.7 = (f32[32,32,128]{2,1,0:T(8,128)S(1)}, f32[32,32,128]{2,1,0:T(8,128)S(1)}, u32[]{:S(2)}, u32[]{:S(2)}) collective-permute-start(f32[32,32,128]{2,1,0:T(8,128)S(1)} %all-to-all-done.1.got_ref), channel_id=1, source_target_pairs={{0,8},{8,0},{1,9},{9,1},{2,10},{10,2},{3,11},{11,3},{4,12},{12,4},... | collective-permute-start | bytes 1572872 | tf_op jit(solution)/shard_map/ppermute | solution.py:353
  70.3 1.5 %collective-permute-done.7.mate_ref = f32[32,32,128]{2,1,0:T(8,128)S(1)} collective-permute-done((f32[32,32,128]{2,1,0:T(8,128)S(1)}, f32[32,32,128]{2,1,0:T(8,128)S(1)}, u32[]{:S(2)}, u32[]{:S(2)}) %collective-permute-start.7) | collective-permute-done | bytes 524320 | tf_op jit(solution)/shard_map/ppermute | solution.py:353
  71.8 3.4 %shard_map.40 = f32[4,16,128]{2,1,0:T(8,128)} custom-call(f32[32,32,128]{2,1,0:T(8,128)S(1)} %all-to-all-done.1.got_ref, f32[32,32,128]{2,1,0:T(8,128)S(1)} %collective-permute-done.7.mate_ref, f32[4,5,16,128]{3,2,1,0:T(8,128)S(1)} %get-tuple-element.23.field_ref, f32[5,16,128]{2,1,0:T(8,128)S(1)} %get-tuple-element.24.middle_ref, ...), custom_call_target="tpu_custom_call" | custom-call | tf_op jit(solution)/shard_map/pallas_call | solution.py:300
  (4 shorter events, 0.0 us)
Async XLA Ops:
  0.8 6.8 %collective-permute-start.1 = (f32[3,4,10,128]{3,2,1,0:T(8,128)S(1)}, f32[3,4,10,128]{3,2,1,0:T(8,128)S(1)}, u32[]{:S(2)}, u32[]{:S(2)}) collective-permute-start(f32[3,4,10,128]{3,2,1,0:T(8,128)S(1)} %get-tuple-element.27), channel_id=1, source_target_pairs={{1,0},{2,1},{3,2},{4,3},{5,4},{6,5},{7,6},{9,8},{10,9},{11,10},{12... | collective-permute-start | bytes 184328 | tf_op jit(solution)/shard_map/ppermute | solution.py:319
  2.1 7.1 %collective-permute-start = (f32[3,4,10,128]{3,2,1,0:T(8,128)S(1)}, f32[3,4,10,128]{3,2,1,0:T(8,128)S(1)}, u32[]{:S(2)}, u32[]{:S(2)}) collective-permute-start(f32[3,4,10,128]{3,2,1,0:T(8,128)S(1)} %get-tuple-element.28), channel_id=1, source_target_pairs={{0,1},{1,2},{2,3},{3,4},{4,5},{5,6},{6,7},{8,9},{9,10},{10,11},{11... | collective-permute-start | bytes 184328 | tf_op jit(solution)/shard_map/ppermute | solution.py:318
  9.7 9.1 %collective-permute-start.3 = (f32[3,4,40,128]{3,2,1,0:T(8,128)S(1)}, f32[3,4,40,128]{3,2,1,0:T(8,128)S(1)}, u32[]{:S(2)}, u32[]{:S(2)}) collective-permute-start(f32[3,4,40,128]{3,2,1,0:T(8,128)S(1)} %concatenate.3.own_ref), channel_id=1, source_target_pairs={{8,16},{16,8},{24,32},{32,24},{40,48},{48,40},{56,64},{64,56},{72,... | collective-permute-start | bytes 737288 | tf_op jit(solution)/shard_map/ppermute | solution.py:326
  14.2 5.7 %collective-permute-start.2 = (f32[3,4,40,128]{3,2,1,0:T(8,128)S(1)}, f32[3,4,40,128]{3,2,1,0:T(8,128)S(1)}, u32[]{:S(2)}, u32[]{:S(2)}) collective-permute-start(f32[3,4,40,128]{3,2,1,0:T(8,128)S(1)} %concatenate.3.own_ref), channel_id=1, source_target_pairs={{0,8},{8,0},{1,9},{9,1},{2,10},{10,2},{3,11},{11,3},{4,12},{12,4},... | collective-permute-start | bytes 737288 | tf_op jit(solution)/shard_map/ppermute | solution.py:327
  38.6 26.5 %all-to-all-start.1 = ((f32[32,32,128]{2,1,0:T(8,128)}), f32[32,32,128]{2,1,0:T(8,128)S(1)}, u32[]{:S(2)}, u32[]{:S(2)}) async-start(f32[32,32,128]{2,1,0:T(8,128)} %shard_map.38), calls=%async_computation.1 | async-start | bytes 1048576 | tf_op jit(solution)/shard_map/all_to_all | solution.py:340
  49.6 3.9 %collective-permute-start.4 = (f32[3,16,128]{2,1,0:T(8,128)S(1)}, f32[3,16,128]{2,1,0:T(8,128)S(1)}, u32[]{:S(2)}, u32[]{:S(2)}) collective-permute-start(f32[3,16,128]{2,1,0:T(8,128)S(1)} %get-tuple-element.19.own_ref), channel_id=1, source_target_pairs={{0,8},{8,0},{1,9},{9,1},{2,10},{10,2},{3,11},{11,3},{4,12},{12,4},... | collective-permute-start | bytes 73736 | tf_op jit(solution)/shard_map/ppermute | solution.py:342
  53.6 6.3 %collective-permute-start.5 = (f32[2,3,16,128]{3,2,1,0:T(8,128)S(1)}, f32[2,3,16,128]{3,2,1,0:T(8,128)S(1)}, u32[]{:S(2)}, u32[]{:S(2)}) collective-permute-start(f32[2,3,16,128]{3,2,1,0:T(8,128)S(1)} %pad_maximum_fusion.1), channel_id=1, source_target_pairs={{0,16},{24,8},{16,32},{40,24},{32,48},{56,40},{48,64},{72,56},{64,... | collective-permute-start | bytes 147464 | tf_op jit(solution)/shard_map/ppermute | solution.py:347
  54.9 5.0 %collective-permute-start.6 = (f32[3,16,128]{2,1,0:T(8,128)S(1)}, f32[3,16,128]{2,1,0:T(8,128)S(1)}, u32[]{:S(2)}, u32[]{:S(2)}) collective-permute-start(f32[3,16,128]{2,1,0:T(8,128)S(1)} %get-tuple-element.19.own_ref), channel_id=1, source_target_pairs={{16,0},{8,24},{32,16},{24,40},{48,32},{40,56},{64,48},{56,72},{80,... | collective-permute-start | bytes 73736 | tf_op jit(solution)/shard_map/ppermute | solution.py:348
  65.1 6.7 %collective-permute-start.7 = (f32[32,32,128]{2,1,0:T(8,128)S(1)}, f32[32,32,128]{2,1,0:T(8,128)S(1)}, u32[]{:S(2)}, u32[]{:S(2)}) collective-permute-start(f32[32,32,128]{2,1,0:T(8,128)S(1)} %all-to-all-done.1.got_ref), channel_id=1, source_target_pairs={{0,8},{8,0},{1,9},{9,1},{2,10},{10,2},{3,11},{11,3},{4,12},{12,4},... | collective-permute-start | bytes 1572872 | tf_op jit(solution)/shard_map/ppermute | solution.py:353

commit v3 on v2

--- a/solution.py
+++ b/solution.py
@@ -1,5 +1,3 @@
-import functools
-
 import jax
 import jax.numpy as jnp
 from jax import lax
@@ -12,21 +10,6 @@
 F32 = jnp.float32
 
 
-def dot(a, b):
-    high = a.astype(jnp.bfloat16)
-    rest = a - high.astype(F32)
-    middle = rest.astype(jnp.bfloat16)
-    low = (rest - middle.astype(F32)).astype(jnp.bfloat16)
-    parts = lax.dot_general(
-        jnp.concatenate([high, middle, low], axis=0),
-        b.astype(jnp.bfloat16),
-        (((1,), (0,)), ((), ())),
-        preferred_element_type=F32,
-    )
-    n = a.shape[0]
-    return parts[:n] + parts[n : 2 * n] + parts[2 * n :]
-
-
 def iota(shape, dim):
     return lax.broadcasted_iota(jnp.int32, shape, dim)
 
@@ -41,6 +24,10 @@
     below = jnp.where(lane > 0, pltpu.roll(v, 1, axis), 0.0)
     above = jnp.where(lane < period - 1, pltpu.roll(v, 127, axis), 0.0)
     return v + below + above
+
+
+def gather_lanes(v, index):
+    return jnp.take_along_axis(v, index, axis=1, mode="promise_in_bounds")
 
 
 def relax_weight(scale, shift, level_scale):
@@ -60,18 +47,25 @@
 
 def pair_planes(quads, rows_ref):
     parts = []
-    for k, t in enumerate(quads):
-        halves = []
-        for i in (0, 2):
+    for i in (0, 2):
+        for k, t in enumerate(quads):
             at = 40 * (2 * k + i // 2)
             rows_ref[at : at + 40] = t[i] + t[i + 1]
-            halves.append(
+            parts.append(
                 rows_ref[pl.ds(at + 4, 16, stride=2)] + rows_ref[pl.ds(at + 5, 16, stride=2)]
             )
-        parts.append(jnp.concatenate(halves, axis=1))
-    lane, out = iota((256, 128), 0), iota((256, 128), 1)
-    pack = ones_where(lane // 2 == out, 0.125)
-    return dot(jnp.concatenate(parts, axis=0), pack).reshape(len(quads), 16, 128)
+    both = jnp.concatenate(parts, axis=0)
+    lane = iota(both.shape, 1)
+    both = gather_lanes(both + pltpu.roll(both, 127, 1), 2 * (lane % 64))
+    n = 16 * len(quads)
+    pair = 0.125 * jnp.where(lane[:n] < 64, both[:n], both[n:])
+    return pair.reshape(len(quads), 16, 128)
+
+
+def plane_groups(v):
+    v = v + pltpu.roll(v, 127, 1)
+    v = v + pltpu.roll(v, 64, 1)
+    return 0.125 * gather_lanes(v, 2 * (iota(v.shape, 1) % 32))
 
 
 def fine_kernel(
@@ -103,11 +97,10 @@
     v = w * f
     v = v + w * (f - middle_apply(v, a, s))
     resid = f - middle_apply(v, a, s)
-    spread = ones_where(iota((128, 128), 1) % 32 == (iota((128, 128), 0) % 64) // 2, 0.125)
     own = ones_where(iota((16, 128), 0) // 2 == iota((16, 128), 1) // 32 + 2)
-    mixed = dot(resid.reshape(48, 128), spread).reshape(3, 16, 128)
+    mixed = plane_groups(resid.reshape(48, 128)).reshape(3, 16, 128)
     rows = [mixed[k] * own for k in range(3)]
-    mixed = dot(jnp.concatenate([a[1], s[1]], axis=0), spread).reshape(2, 16, 128)
+    mixed = plane_groups(jnp.concatenate([a[1], s[1]], axis=0)).reshape(2, 16, 128)
     rows += [mixed[k] * own for k in range(2)] + [jnp.zeros((1, 128), F32)] * 3
     piece = jnp.concatenate([jnp.sum(t, axis=0, keepdims=True) for t in rows], axis=0)
     piece_ref[...] = jnp.broadcast_to(piece[None], piece_ref.shape)
@@ -129,15 +122,6 @@
     )
     box = lane_box(box, 64)
     return 0.25 * scale * (27.0 * v - box) + shift * v
-
-
-def quarter_row(shape, dim):
-    i = iota(shape, dim)
-    return 4 * (i % 8) + i // 8
-
-
-def quarter_mask():
-    return ones_where(iota((4, 8, 128), 2) // 32 == iota((4, 8, 128), 0))
 
 
 def gather_kernel(got_ref, piece_ref, rows_ref):
@@ -191,45 +175,48 @@
     return jnp.sum(jnp.sum(plane, axis=0, keepdims=True), axis=1, keepdims=True)
 
 
-def solve_coarse(q_ref, a_ref, d_ref, inverse_ref, z_ref, image_ref, e_ref):
-    planes = q_ref.shape[0]
+def solve_coarse(q_ref, a_ref, d_ref, inverse_ref, w_ref, y_ref, at):
+    planes = a_ref.shape[0]
     chunk = 8 if planes % 8 == 0 else 2
     starts = range(0, planes, chunk)
-    none = jnp.zeros((1, 8, 128), F32)
-    z_ref[:1] = none
-    z_ref[planes + 1 :] = none
-    for i in (0, 1, planes + 2, planes + 3):
-        e_ref[i : i + 1] = none
+    none = jnp.zeros((2, 8, 128), F32)
+    for ref in (q_ref, inverse_ref, w_ref):
+        ref[:2] = none
+        ref[planes + 2 :] = none
     for i in starts:
-        own = slice(i, i + chunk)
-        inverse = 1.0 / (d_ref[own] - a_ref[own])
-        inverse_ref[own] = inverse
-        z_ref[i + 1 : i + chunk + 1] = q_ref[own] * inverse
+        own, padded = slice(i, i + chunk), slice(i + 2, i + chunk + 2)
+        inverse_ref[padded] = 1.0 / (d_ref[own] - a_ref[own])
+
+    def product(ref):
+        for i in starts:
+            own, wide = slice(i, i + chunk), slice(i + 1, i + chunk + 3)
+            z = ref[wide] * inverse_ref[wide]
+            y_ref[own] = d_ref[own] * z[1:-1] - a_ref[own] * coarse_box(z)
+
+    product(q_ref)
+    solution = jnp.zeros((5, 8, 128), F32)
     for step in range(COARSE):
         upper = lower = jnp.zeros((8, 128), F32)
         for i in starts:
-            own = slice(i, i + chunk)
-            z = z_ref[i : i + chunk + 2]
-            image = d_ref[own] * z[1:-1] - a_ref[own] * coarse_box(z)
-            image_ref[own] = image
-            upper = upper + jnp.sum(image * q_ref[own], axis=0)
-            lower = lower + jnp.sum(image * image, axis=0)
+            own, padded = slice(i, i + chunk), slice(i + 2, i + chunk + 2)
+            w, q = y_ref[own], q_ref[padded]
+            if step > 0:
+                old = w_ref[padded]
+                w, q = old - alpha * w, q - alpha * old
+                q_ref[padded] = q
+            w_ref[padded] = w
+            upper = upper + jnp.sum(w * q, axis=0)
+            lower = lower + jnp.sum(w * w, axis=0)
         alpha = (total(upper) / total(lower))[None]
-        for i in starts:
-            own = slice(i, i + chunk)
-            inner = slice(i + 1, i + chunk + 1)
-            outer = slice(i + 2, i + chunk + 2)
-            gain = alpha * z_ref[inner]
-            e_ref[outer] = gain if step == 0 else e_ref[outer] + gain
-            if step < COARSE - 1:
-                q = q_ref[own] - alpha * image_ref[own]
-                q_ref[own] = q
-                z_ref[inner] = q * inverse_ref[own]
+        if step < COARSE - 1:
+            product(w_ref)
+        solution = solution + alpha * q_ref[pl.ds(at, 5)]
+    return solution * inverse_ref[pl.ds(at, 5)]
 
 
 def last_kernel(
     got_ref, mate_ref, field_ref, middle_ref, fine_ref, iter_ref, out_ref,
-    q_ref, a_ref, d_ref, inverse_ref, z_ref, image_ref, coarse_ref, middle_rows, fine_rows,
+    q_ref, a_ref, d_ref, inverse_ref, w_ref, y_ref, middle_rows, fine_rows,
 ):
     nx = lax.axis_size("x")
     chip = lax.axis_index("y") * nx + lax.axis_index("x")
@@ -247,20 +234,16 @@
         return jnp.concatenate([first[:, None], second[:, None]], axis=1).reshape(planes, 8, 128)
 
     edge = jnp.zeros_like(part(0, 0)[:1])
-    q_ref[...] = pairs(
+    q_ref[2 : planes + 2] = pairs(
         part(0, 1) + jnp.concatenate([edge, part(1, 0)[:-1]], axis=0),
         part(1, 1) + jnp.concatenate([part(0, 0)[1:], edge], axis=0),
     )
     a = 0.0625 * pairs(part(0, 2), part(1, 2))
     a_ref[...] = a
     d_ref[...] = 27.0 * a + pairs(part(0, 3), part(1, 3))
-    solve_coarse(q_ref, a_ref, d_ref, inverse_ref, z_ref, image_ref, coarse_ref)
-    near = coarse_ref[pl.ds(chip * 2 + core, 5)]
-
-    mask = quarter_mask()
-    stack = jnp.concatenate([(near[p][None] * mask).reshape(32, 128) for p in range(5)], axis=0)
-    spread = ones_where(iota((128, 128), 0) % 32 == (iota((128, 128), 1) % 64) // 2)
-    mixed = dot(stack, spread)
+    near = solve_coarse(q_ref, a_ref, d_ref, inverse_ref, w_ref, y_ref, chip * 2 + core)
+
+    lane = iota((8, 128), 1) % 64 // 2
     size = (middle_rows.shape[0] - 16) // 5
     edge = jnp.zeros((4, 128), F32)
     window = []
@@ -269,7 +252,7 @@
         middle_rows[at : at + 4] = edge
         middle_rows[at + size - 4 : at + size] = edge
         for k in range(4):
-            t = mixed[32 * p + 8 * k : 32 * p + 8 * k + 8]
+            t = gather_lanes(near[p], 32 * k + lane)
             for i in (4, 5):
                 middle_rows[pl.ds(at + 2 * k + i, 8, stride=8)] = t
         window.append(middle_rows[pl.ds(pl.multiple_of(at + rank * 8, 8), 16)][None])
@@ -278,9 +261,10 @@
     for _ in range(2):
         v = v + w * (f - middle_apply(v, a, s))
 
-    lane, out = iota((128, 256), 0), iota((128, 256), 1)
-    mixed = dot(v[1:4].reshape(48, 128), ones_where(lane == out // 2))
-    halves = [mixed[:16, 128:], mixed[16:32, :128], mixed[16:32, 128:], mixed[32:, :128]]
+    lane = iota((32, 128), 1) // 2
+    low = gather_lanes(v[2:4].reshape(32, 128), lane)
+    high = gather_lanes(v[1:3].reshape(32, 128), 64 + lane)
+    halves = [high[:16], low[:16], high[16:], low[16:]]
     refined = []
     for p, t in enumerate(halves):
         for i in range(2):
@@ -354,8 +338,8 @@
     (result,) = call(
         last_kernel, [source.shape],
         half, half_mate, fields, middle_iter, fine_fields, fine_iter,
-        scratch=[(2 * chips, 8, 128)] * 4
-        + [(2 * chips + 2, 8, 128), (2 * chips, 8, 128), (2 * chips + 4, 8, 128)]
+        scratch=[(2 * chips + 4, 8, 128)] + [(2 * chips, 8, 128)] * 2
+        + [(2 * chips + 4, 8, 128)] * 2 + [(2 * chips, 8, 128)]
         + [(5 * (8 * nz + 8) + 16, 128), (4 * 24 + 16, 128)],
     )
     return result

time: 75.7 us -> 76.5 us (1.011)
  Pallas kernels: 5.41 us -> 6.19 us
    pallas_call x4, Pallas kernels: 5.41 us -> 6.19 us  [call(): pl.pallas_call(kernel, out_shape=[jax.ShapeDtypeStruct(shape, F32) for sh...]
where the time goes in v3:
time: 76.5 us; the launch traced here: 76 us
  starting transfers between devices  40.6 us (53%)
  blocking collectives  16.8 us (22%)
  waiting for transfers between devices  11 us (14%)
  Pallas kernels  6.19 us (8%)
  other arithmetic  0.81 us (1%)
    all_to_all x1, blocking collectives, shards(): got = lax.all_to_all(sent, ('c', 'z'), 0, 0).reshape(16 * nz, 128)  16.8 us
    all_to_all x1, starting transfers between devices, shards(): half = lax.all_to_all(sent, ('y', 'x'), 0, 0)  11.1 us
    pallas_call x4, Pallas kernels, call(): pl.pallas_call(kernel, out_shape=[jax.ShapeDtypeStruct(shape, F32) for sh...  6.19 us
    ppermute x1, starting transfers between devices, shards(): before = lax.ppermute(own[:, :, 6:], 'z', up)  5.46 us
    ppermute x1, starting transfers between devices, shards(): half_mate = lax.ppermute(half, 'c', swap)  5.22 us
    all_to_all x1, waiting for transfers between devices, shards(): half = lax.all_to_all(sent, ('y', 'x'), 0, 0)  5.02 us
    ppermute x1, starting transfers between devices, shards(): mate = lax.ppermute(own, 'c', swap)  4.6 us
    ppermute x1, starting transfers between devices, shards(): face = lax.ppermute(own, ('y', 'x', 'c'), facing)  4.53 us
  transfers between devices with their start and end apart: 9, of which 7 were waited for; matrix products, arithmetic and copies ran while one was open for 0% of the time, Pallas kernels for 0%

profile of v3, /device:TPU:1, one launch (start us, length us, event | category | flops | bytes accessed | tf_op | source)
XLA Modules:
  0.0 76.0 jit_solution(18200741935883790223)
XLA Ops:
  0.0 0.8 %pad_maximum_fusion = f32[3,4,16,128]{3,2,1,0:T(8,128)S(1)} fusion(f32[1,4,16,128]{3,2,1,0:T(8,128)} %bitcast.9, f32[1,4,16,128]{3,2,1,0:T(8,128)} %bitcast.10, f32[1,4,16,128]{3,2,1,0:T(8,128)} %bitcast.11), kind=kLoop, calls=%fused_computation | loop fusion | flops 49152 | bytes 196608 | tf_op jit(solution)/shard_map/stack | solution.py:299
  0.8 1.3 %collective-permute-start.1 = (f32[3,4,10,128]{3,2,1,0:T(8,128)S(1)}, f32[3,4,10,128]{3,2,1,0:T(8,128)S(1)}, u32[]{:S(2)}, u32[]{:S(2)}) collective-permute-start(f32[3,4,10,128]{3,2,1,0:T(8,128)S(1)} %get-tuple-element.27), channel_id=1, source_target_pairs={{1,0},{2,1},{3,2},{4,3},{5,4},{6,5},{7,6},{9,8},{10,9},{11,10},{12... | collective-permute-start | bytes 184328 | tf_op jit(solution)/shard_map/ppermute | solution.py:303
  2.1 5.5 %collective-permute-start = (f32[3,4,10,128]{3,2,1,0:T(8,128)S(1)}, f32[3,4,10,128]{3,2,1,0:T(8,128)S(1)}, u32[]{:S(2)}, u32[]{:S(2)}) collective-permute-start(f32[3,4,10,128]{3,2,1,0:T(8,128)S(1)} %get-tuple-element.28), channel_id=1, source_target_pairs={{0,1},{1,2},{2,3},{3,4},{4,5},{5,6},{6,7},{8,9},{9,10},{10,11},{11... | collective-permute-start | bytes 184328 | tf_op jit(solution)/shard_map/ppermute | solution.py:302
  7.6 0.1 collective-permute-done.1
  7.6 1.6 %collective-permute-done = f32[3,4,10,128]{3,2,1,0:T(8,128)S(1)} collective-permute-done((f32[3,4,10,128]{3,2,1,0:T(8,128)S(1)}, f32[3,4,10,128]{3,2,1,0:T(8,128)S(1)}, u32[]{:S(2)}, u32[]{:S(2)}) %collective-permute-start) | collective-permute-done | bytes 61472 | tf_op jit(solution)/shard_map/ppermute | solution.py:302
  9.2 0.5 concatenate.3.own_ref
  9.7 4.5 %collective-permute-start.3 = (f32[3,4,40,128]{3,2,1,0:T(8,128)S(1)}, f32[3,4,40,128]{3,2,1,0:T(8,128)S(1)}, u32[]{:S(2)}, u32[]{:S(2)}) collective-permute-start(f32[3,4,40,128]{3,2,1,0:T(8,128)S(1)} %concatenate.3.own_ref), channel_id=1, source_target_pairs={{8,16},{16,8},{24,32},{32,24},{40,48},{48,40},{56,64},{64,56},{72,... | collective-permute-start | bytes 737288 | tf_op jit(solution)/shard_map/ppermute | solution.py:310
  14.2 4.6 %collective-permute-start.2 = (f32[3,4,40,128]{3,2,1,0:T(8,128)S(1)}, f32[3,4,40,128]{3,2,1,0:T(8,128)S(1)}, u32[]{:S(2)}, u32[]{:S(2)}) collective-permute-start(f32[3,4,40,128]{3,2,1,0:T(8,128)S(1)} %concatenate.3.own_ref), channel_id=1, source_target_pairs={{0,8},{8,0},{1,9},{9,1},{2,10},{10,2},{3,11},{11,3},{4,12},{12,4},... | collective-permute-start | bytes 737288 | tf_op jit(solution)/shard_map/ppermute | solution.py:311
  18.8 0.0 collective-permute-done.3.face_ref
  18.9 1.1 %collective-permute-done.2.mate_ref = f32[3,4,40,128]{3,2,1,0:T(8,128)S(1)} collective-permute-done((f32[3,4,40,128]{3,2,1,0:T(8,128)S(1)}, f32[3,4,40,128]{3,2,1,0:T(8,128)S(1)}, u32[]{:S(2)}, u32[]{:S(2)}) %collective-permute-start.2) | collective-permute-done | bytes 245792 | tf_op jit(solution)/shard_map/ppermute | solution.py:311
  20.0 1.0 %shard_map.37 = (f32[8,24,128]{2,1,0:T(8,128)S(1)}, f32[4,8,24,128]{3,2,1,0:T(8,128)S(1)}, f32[16,8,128]{2,1,0:T(8,128)S(1)}, f32[3,16,128]{2,1,0:T(8,128)S(1)}) custom-call(f32[3,4,40,128]{3,2,1,0:T(8,128)S(1)} %concatenate.3.own_ref, f32[3,4,40,128]{3,2,1,0:T(8,128)S(1)} %collective-permute-done.2.mate_ref, ...), custom_call_target="tpu_custom_call" | custom-call | tf_op jit(solution)/shard_map/pallas_call | solution.py:284
  21.0 16.8 %all_to_all.10 = f32[16,8,128]{2,1,0:T(8,128)S(1)} all-to-all(f32[16,8,128]{2,1,0:T(8,128)S(1)} %get-tuple-element.17), channel_id=1, replica_groups=mesh['y'=8,'x'=4,'c'=2,'z'=8] {'c','z'}, dimensions={0} | all-to-all | bytes 131072 | tf_op jit(solution)/shard_map/all_to_all | solution.py:319
  37.8 0.9 %shard_map.38 = f32[32,32,128]{2,1,0:T(8,128)} custom-call(f32[128,128]{1,0:T(8,128)S(1)} %bitcast.8), custom_call_target="tpu_custom_call" | custom-call | tf_op jit(solution)/shard_map/pallas_call | solution.py:284
  38.6 11.1 %all-to-all-start.1 = ((f32[32,32,128]{2,1,0:T(8,128)}), f32[32,32,128]{2,1,0:T(8,128)S(1)}, u32[]{:S(2)}, u32[]{:S(2)}) async-start(f32[32,32,128]{2,1,0:T(8,128)} %shard_map.38), calls=%async_computation.1 | async-start | bytes 1048576 | tf_op jit(solution)/shard_map/all_to_all | solution.py:324
  49.7 3.1 %collective-permute-start.4 = (f32[3,16,128]{2,1,0:T(8,128)S(1)}, f32[3,16,128]{2,1,0:T(8,128)S(1)}, u32[]{:S(2)}, u32[]{:S(2)}) collective-permute-start(f32[3,16,128]{2,1,0:T(8,128)S(1)} %get-tuple-element.19.own_ref), channel_id=1, source_target_pairs={{0,8},{8,0},{1,9},{9,1},{2,10},{10,2},{3,11},{11,3},{4,12},{12,4},... | collective-permute-start | bytes 73736 | tf_op jit(solution)/shard_map/ppermute | solution.py:326
  52.8 0.8 %collective-permute-done.4.mate_ref = f32[3,16,128]{2,1,0:T(8,128)S(1)} collective-permute-done((f32[3,16,128]{2,1,0:T(8,128)S(1)}, f32[3,16,128]{2,1,0:T(8,128)S(1)}, u32[]{:S(2)}, u32[]{:S(2)}) %collective-permute-start.4) | collective-permute-done | bytes 24608 | tf_op jit(solution)/shard_map/ppermute | solution.py:326
  53.6 1.3 %collective-permute-start.5 = (f32[2,3,16,128]{3,2,1,0:T(8,128)S(1)}, f32[2,3,16,128]{3,2,1,0:T(8,128)S(1)}, u32[]{:S(2)}, u32[]{:S(2)}) collective-permute-start(f32[2,3,16,128]{3,2,1,0:T(8,128)S(1)} %pad_maximum_fusion.1), channel_id=1, source_target_pairs={{0,16},{24,8},{16,32},{40,24},{32,48},{56,40},{48,64},{72,56},{64,... | collective-permute-start | bytes 147464 | tf_op jit(solution)/shard_map/ppermute | solution.py:331
  54.9 4.0 %collective-permute-start.6 = (f32[3,16,128]{2,1,0:T(8,128)S(1)}, f32[3,16,128]{2,1,0:T(8,128)S(1)}, u32[]{:S(2)}, u32[]{:S(2)}) collective-permute-start(f32[3,16,128]{2,1,0:T(8,128)S(1)} %get-tuple-element.19.own_ref), channel_id=1, source_target_pairs={{16,0},{8,24},{32,16},{24,40},{48,32},{40,56},{64,48},{56,72},{80,... | collective-permute-start | bytes 73736 | tf_op jit(solution)/shard_map/ppermute | solution.py:332
  59.0 0.9 %collective-permute-done.6.inner_ref = f32[3,16,128]{2,1,0:T(8,128)S(1)} collective-permute-done((f32[3,16,128]{2,1,0:T(8,128)S(1)}, f32[3,16,128]{2,1,0:T(8,128)S(1)}, u32[]{:S(2)}, u32[]{:S(2)}) %collective-permute-start.6) | collective-permute-done | bytes 24608 | tf_op jit(solution)/shard_map/ppermute | solution.py:332
  59.9 0.0 collective-permute-done.5.outer_ref
  59.9 0.2 shard_map.39
  60.1 5.0 %all-to-all-done.1.got_ref = f32[32,32,128]{2,1,0:T(8,128)S(1)} async-done(((f32[32,32,128]{2,1,0:T(8,128)}), f32[32,32,128]{2,1,0:T(8,128)S(1)}, u32[]{:S(2)}, u32[]{:S(2)}) %all-to-all-start.1) | async-done | bytes 524320 | tf_op jit(solution)/shard_map/all_to_all | solution.py:324
  65.2 5.2 %collective-permute-start.7 = (f32[32,32,128]{2,1,0:T(8,128)S(1)}, f32[32,32,128]{2,1,0:T(8,128)S(1)}, u32[]{:S(2)}, u32[]{:S(2)}) collective-permute-start(f32[32,32,128]{2,1,0:T(8,128)S(1)} %all-to-all-done.1.got_ref), channel_id=1, source_target_pairs={{0,8},{8,0},{1,9},{9,1},{2,10},{10,2},{3,11},{11,3},{4,12},{12,4},... | collective-permute-start | bytes 1572872 | tf_op jit(solution)/shard_map/ppermute | solution.py:337
  70.4 1.5 %collective-permute-done.7.mate_ref = f32[32,32,128]{2,1,0:T(8,128)S(1)} collective-permute-done((f32[32,32,128]{2,1,0:T(8,128)S(1)}, f32[32,32,128]{2,1,0:T(8,128)S(1)}, u32[]{:S(2)}, u32[]{:S(2)}) %collective-permute-start.7) | collective-permute-done | bytes 524320 | tf_op jit(solution)/shard_map/ppermute | solution.py:337
  71.9 4.1 %shard_map.40 = f32[4,16,128]{2,1,0:T(8,128)} custom-call(f32[32,32,128]{2,1,0:T(8,128)S(1)} %all-to-all-done.1.got_ref, f32[32,32,128]{2,1,0:T(8,128)S(1)} %collective-permute-done.7.mate_ref, f32[4,5,16,128]{3,2,1,0:T(8,128)S(1)} %get-tuple-element.23.field_ref, f32[5,16,128]{2,1,0:T(8,128)S(1)} %get-tuple-element.24.middle_ref, ...), custom_call_target="tpu_custom_call" | custom-call | tf_op jit(solution)/shard_map/pallas_call | solution.py:284
  (4 shorter events, 0.0 us)
Async XLA Ops:
  0.8 6.8 %collective-permute-start.1 = (f32[3,4,10,128]{3,2,1,0:T(8,128)S(1)}, f32[3,4,10,128]{3,2,1,0:T(8,128)S(1)}, u32[]{:S(2)}, u32[]{:S(2)}) collective-permute-start(f32[3,4,10,128]{3,2,1,0:T(8,128)S(1)} %get-tuple-element.27), channel_id=1, source_target_pairs={{1,0},{2,1},{3,2},{4,3},{5,4},{6,5},{7,6},{9,8},{10,9},{11,10},{12... | collective-permute-start | bytes 184328 | tf_op jit(solution)/shard_map/ppermute | solution.py:303
  2.1 7.1 %collective-permute-start = (f32[3,4,10,128]{3,2,1,0:T(8,128)S(1)}, f32[3,4,10,128]{3,2,1,0:T(8,128)S(1)}, u32[]{:S(2)}, u32[]{:S(2)}) collective-permute-start(f32[3,4,10,128]{3,2,1,0:T(8,128)S(1)} %get-tuple-element.28), channel_id=1, source_target_pairs={{0,1},{1,2},{2,3},{3,4},{4,5},{5,6},{6,7},{8,9},{9,10},{10,11},{11... | collective-permute-start | bytes 184328 | tf_op jit(solution)/shard_map/ppermute | solution.py:302
  9.7 9.1 %collective-permute-start.3 = (f32[3,4,40,128]{3,2,1,0:T(8,128)S(1)}, f32[3,4,40,128]{3,2,1,0:T(8,128)S(1)}, u32[]{:S(2)}, u32[]{:S(2)}) collective-permute-start(f32[3,4,40,128]{3,2,1,0:T(8,128)S(1)} %concatenate.3.own_ref), channel_id=1, source_target_pairs={{8,16},{16,8},{24,32},{32,24},{40,48},{48,40},{56,64},{64,56},{72,... | collective-permute-start | bytes 737288 | tf_op jit(solution)/shard_map/ppermute | solution.py:310
  14.2 5.7 %collective-permute-start.2 = (f32[3,4,40,128]{3,2,1,0:T(8,128)S(1)}, f32[3,4,40,128]{3,2,1,0:T(8,128)S(1)}, u32[]{:S(2)}, u32[]{:S(2)}) collective-permute-start(f32[3,4,40,128]{3,2,1,0:T(8,128)S(1)} %concatenate.3.own_ref), channel_id=1, source_target_pairs={{0,8},{8,0},{1,9},{9,1},{2,10},{10,2},{3,11},{11,3},{4,12},{12,4},... | collective-permute-start | bytes 737288 | tf_op jit(solution)/shard_map/ppermute | solution.py:311
  38.6 26.5 %all-to-all-start.1 = ((f32[32,32,128]{2,1,0:T(8,128)}), f32[32,32,128]{2,1,0:T(8,128)S(1)}, u32[]{:S(2)}, u32[]{:S(2)}) async-start(f32[32,32,128]{2,1,0:T(8,128)} %shard_map.38), calls=%async_computation.1 | async-start | bytes 1048576 | tf_op jit(solution)/shard_map/all_to_all | solution.py:324
  49.7 3.9 %collective-permute-start.4 = (f32[3,16,128]{2,1,0:T(8,128)S(1)}, f32[3,16,128]{2,1,0:T(8,128)S(1)}, u32[]{:S(2)}, u32[]{:S(2)}) collective-permute-start(f32[3,16,128]{2,1,0:T(8,128)S(1)} %get-tuple-element.19.own_ref), channel_id=1, source_target_pairs={{0,8},{8,0},{1,9},{9,1},{2,10},{10,2},{3,11},{11,3},{4,12},{12,4},... | collective-permute-start | bytes 73736 | tf_op jit(solution)/shard_map/ppermute | solution.py:326
  53.6 6.3 %collective-permute-start.5 = (f32[2,3,16,128]{3,2,1,0:T(8,128)S(1)}, f32[2,3,16,128]{3,2,1,0:T(8,128)S(1)}, u32[]{:S(2)}, u32[]{:S(2)}) collective-permute-start(f32[2,3,16,128]{3,2,1,0:T(8,128)S(1)} %pad_maximum_fusion.1), channel_id=1, source_target_pairs={{0,16},{24,8},{16,32},{40,24},{32,48},{56,40},{48,64},{72,56},{64,... | collective-permute-start | bytes 147464 | tf_op jit(solution)/shard_map/ppermute | solution.py:331
  54.9 5.0 %collective-permute-start.6 = (f32[3,16,128]{2,1,0:T(8,128)S(1)}, f32[3,16,128]{2,1,0:T(8,128)S(1)}, u32[]{:S(2)}, u32[]{:S(2)}) collective-permute-start(f32[3,16,128]{2,1,0:T(8,128)S(1)} %get-tuple-element.19.own_ref), channel_id=1, source_target_pairs={{16,0},{8,24},{32,16},{24,40},{48,32},{40,56},{64,48},{56,72},{80,... | collective-permute-start | bytes 73736 | tf_op jit(solution)/shard_map/ppermute | solution.py:332
  65.2 6.7 %collective-permute-start.7 = (f32[32,32,128]{2,1,0:T(8,128)S(1)}, f32[32,32,128]{2,1,0:T(8,128)S(1)}, u32[]{:S(2)}, u32[]{:S(2)}) collective-permute-start(f32[32,32,128]{2,1,0:T(8,128)S(1)} %all-to-all-done.1.got_ref), channel_id=1, source_target_pairs={{0,8},{8,0},{1,9},{9,1},{2,10},{10,2},{3,11},{11,3},{4,12},{12,4},... | collective-permute-start | bytes 1572872 | tf_op jit(solution)/shard_map/ppermute | solution.py:337

commit v4 on v2

--- a/solution.py
+++ b/solution.py
@@ -1,5 +1,3 @@
-import functools
-
 import jax
 import jax.numpy as jnp
 from jax import lax
@@ -74,14 +72,51 @@
     return dot(jnp.concatenate(parts, axis=0), pack).reshape(len(quads), 16, 128)
 
 
+def edge_kernel(own_ref, first_ref, last_ref):
+    for k in range(3):
+        for p in range(4):
+            at = 10 * (4 * k + p)
+            first_ref[at : at + 10] = own_ref[k, p, :10]
+            last_ref[at : at + 10] = own_ref[k, p, 6:]
+
+
+def block_kernel(own_ref, before_ref, after_ref, block_ref, face_ref):
+    left = lax.axis_index("c") == 0
+    none = jnp.zeros((2, 128), F32)
+    for k in range(3):
+        for p in range(4):
+            at = 10 * (4 * k + p)
+            block_ref[k, p, 12:28] = own_ref[k, p]
+            block_ref[k, p, 2:12] = before_ref[at : at + 10]
+            block_ref[k, p, 28:38] = after_ref[at : at + 10]
+            block_ref[k, p, :2] = none
+            block_ref[k, p, 38:] = none
+    for k in range(3):
+        for p in range(2):
+            at = 40 * (2 * k + p)
+            face_ref[at : at + 40] = jnp.where(left, block_ref[k, p], block_ref[k, p + 2])
+        at = 240 + 24 * k
+        rows = slice(8, 32)
+        face_ref[at : at + 24] = jnp.where(left, block_ref[k, 2, rows], block_ref[k, 1, rows])
+    face_ref[312:] = jnp.where(left, block_ref[1, 3, rows], block_ref[1, 0, rows])
+
+
 def fine_kernel(
     own_ref, mate_ref, face_ref, iter_ref, field_ref, piece_ref, one_ref, coef_rows, rows_ref
 ):
     left = lax.axis_index("c") == 0
     blocks = []
     for k in range(3):
-        face, mate = face_ref[k], mate_ref[k]
-        before, after = jnp.where(left, face, mate), jnp.where(left, mate, face)
+        mate = mate_ref[k]
+        near = face_ref[80 * k : 80 * k + 80].reshape(2, 40, 128)
+        pad = jnp.zeros((1, 8, 128), F32)
+        third = face_ref[240 + 24 * k : 264 + 24 * k][None]
+        fourth = face_ref[312:][None] if k == 1 else jnp.zeros_like(third)
+        third, fourth = (
+            jnp.concatenate([pad, t, pad], axis=1) for t in (third, fourth)
+        )
+        before = jnp.where(left, jnp.concatenate([fourth, third, near], axis=0), mate)
+        after = jnp.where(left, mate, jnp.concatenate([near, third, fourth], axis=0))
         blocks.append(jnp.concatenate([before, own_ref[k], after], axis=0))
     f, a, s = blocks
     coefs = pair_planes([t[4 * p : 4 * p + 4] for t in (a, s) for p in range(3)], coef_rows)
@@ -161,7 +196,9 @@
     piece_ref[...] = jnp.broadcast_to(piece[None], piece_ref.shape)
 
 
-def smooth_kernel(own_ref, mate_ref, outer_ref, inner_ref, field_ref, iter_ref):
+def smooth_kernel(
+    own_ref, mate_ref, outer_ref, inner_ref, field_ref, iter_ref, matrix_ref
+):
     left = lax.axis_index("c") == 0
     for k in range(3):
         mate, outer, inner = mate_ref[k], outer_ref[:, k], inner_ref[k]
@@ -175,25 +212,42 @@
     field_ref[3] = w
     v = w * f
     iter_ref[...] = v + w * (f - middle_apply(v, a, s))
-
-
-def coarse_box(v):
-    box = v[:-2] + v[1:-1] + v[2:]
+    matrix_ref[...] = box_matrix()
+
+
+def box_matrix():
+    lane, out = iota((256, 256), 0) % 128, iota((256, 256), 1)
+    group, to = lane // 32, out % 128 // 32
+    near = jnp.abs(lane % 32 - out % 32) <= 1
+    same = (out < 128) & (jnp.abs(group - to) <= 1)
+    wrap = (out >= 128) & (jnp.abs(group - to) == 3)
+    return ones_where(near & (same | wrap)).astype(jnp.bfloat16)
+
+
+def coarse_box(v, matrix):
+    rows = (v[:-2] + v[1:-1] + v[2:]).reshape(-1, 128)
+    high = rows.astype(jnp.bfloat16)
+    low = (rows - high.astype(F32)).astype(jnp.bfloat16)
+    both = lax.dot_general(
+        jnp.concatenate([high, low], axis=1),
+        matrix,
+        (((1,), (0,)), ((), ())),
+        preferred_element_type=F32,
+    )
+    box, wrap = (both[:, k : k + 128].reshape(-1, 8, 128) for k in (0, 128))
     lane, row = iota((8, 128), 1), iota((8, 128), 0)
-    up = pltpu.roll(box, 32, 2)
-    up = jnp.where(lane >= 32, up, jnp.where(row > 0, pltpu.roll(up, 1, 1), 0.0))
-    down = pltpu.roll(box, 96, 2)
-    down = jnp.where(lane < 96, down, jnp.where(row < 7, pltpu.roll(down, 7, 1), 0.0))
-    return lane_box(box + up + down, 32)
+    up = jnp.where((lane < 32) & (row > 0), pltpu.roll(wrap, 1, 1), 0.0)
+    down = jnp.where((lane >= 96) & (row < 7), pltpu.roll(wrap, 7, 1), 0.0)
+    return box + up + down
 
 
 def total(plane):
     return jnp.sum(jnp.sum(plane, axis=0, keepdims=True), axis=1, keepdims=True)
 
 
-def solve_coarse(q_ref, a_ref, d_ref, inverse_ref, z_ref, image_ref, e_ref):
+def solve_coarse(q_ref, a_ref, d_ref, inverse_ref, z_ref, image_ref, e_ref, matrix):
     planes = q_ref.shape[0]
-    chunk = 8 if planes % 8 == 0 else 2
+    chunk = 16 if planes % 16 == 0 else 2
     starts = range(0, planes, chunk)
     none = jnp.zeros((1, 8, 128), F32)
     z_ref[:1] = none
@@ -210,7 +264,7 @@
         for i in starts:
             own = slice(i, i + chunk)
             z = z_ref[i : i + chunk + 2]
-            image = d_ref[own] * z[1:-1] - a_ref[own] * coarse_box(z)
+            image = d_ref[own] * z[1:-1] - a_ref[own] * coarse_box(z, matrix)
             image_ref[own] = image
             upper = upper + jnp.sum(image * q_ref[own], axis=0)
             lower = lower + jnp.sum(image * image, axis=0)
@@ -228,7 +282,7 @@
 
 
 def last_kernel(
-    got_ref, mate_ref, field_ref, middle_ref, fine_ref, iter_ref, out_ref,
+    got_ref, mate_ref, matrix_ref, field_ref, middle_ref, fine_ref, iter_ref, out_ref,
     q_ref, a_ref, d_ref, inverse_ref, z_ref, image_ref, coarse_ref, middle_rows, fine_rows,
 ):
     nx = lax.axis_size("x")
@@ -254,7 +308,9 @@
     a = 0.0625 * pairs(part(0, 2), part(1, 2))
     a_ref[...] = a
     d_ref[...] = 27.0 * a + pairs(part(0, 3), part(1, 3))
-    solve_coarse(q_ref, a_ref, d_ref, inverse_ref, z_ref, image_ref, coarse_ref)
+    solve_coarse(
+        q_ref, a_ref, d_ref, inverse_ref, z_ref, image_ref, coarse_ref, matrix_ref[...]
+    )
     near = coarse_ref[pl.ds(chip * 2 + core, 5)]
 
     mask = quarter_mask()
@@ -299,7 +355,10 @@
 def call(kernel, outs, *args, scratch=()):
     return pl.pallas_call(
         kernel,
-        out_shape=[jax.ShapeDtypeStruct(shape, F32) for shape in outs],
+        out_shape=[
+            jax.ShapeDtypeStruct(*(out if isinstance(out[0], tuple) else (out, F32)))
+            for out in outs
+        ],
         in_specs=[pl.BlockSpec(memory_space=pltpu.VMEM)] * len(args),
         out_specs=[pl.BlockSpec(memory_space=pltpu.VMEM)] * len(outs),
         scratch_shapes=[pltpu.VMEM(shape, F32) for shape in scratch],
@@ -313,17 +372,17 @@
     first = lax.axis_index("c") == 0
 
     own = jnp.stack([source, row_scale, shift_field])
+    head, tail = call(edge_kernel, [(120, 128), (120, 128)], own)
     up = [(i, i + 1) for i in range(nz - 1)]
     down = [(i + 1, i) for i in range(nz - 1)]
-    before = lax.ppermute(own[:, :, 6:], "z", up)
-    after = lax.ppermute(own[:, :, :10], "z", down)
-    fill = jnp.zeros((3, 4, 2, 128), F32)
-    own = jnp.concatenate([fill, before, own, after, fill], axis=2)
+    before = lax.ppermute(tail, "z", up)
+    after = lax.ppermute(head, "z", down)
+    own, face = call(block_kernel, [(3, 4, 40, 128), (336, 128)], own, before, after)
     facing = []
     for i in range(chips - 1):
         facing += [(2 * i + 1, 2 * i + 2), (2 * i + 2, 2 * i + 1)]
     swap = [(0, 1), (1, 0)]
-    face = lax.ppermute(own, ("y", "x", "c"), facing)
+    face = lax.ppermute(face, ("y", "x", "c"), facing)
     mate = lax.ppermute(own, "c", swap)
     fine_iter, fine_fields, sent, one = call(
         fine_kernel,
@@ -346,14 +405,16 @@
         ring += [(2 * i, 2 * i + 2), (2 * i + 3, 2 * i + 1)]
     outer = lax.ppermute(pairs, ("y", "x", "c"), ring)
     inner = lax.ppermute(one, ("y", "x", "c"), [(j, i) for i, j in ring])
-    fields, middle_iter = call(
-        smooth_kernel, [(4, 5, 16, 128), (5, 16, 128)], one, mate, outer, inner
+    fields, middle_iter, matrix = call(
+        smooth_kernel,
+        [(4, 5, 16, 128), (5, 16, 128), ((256, 256), jnp.bfloat16)],
+        one, mate, outer, inner,
     )
     half, fields, middle_iter = lax.optimization_barrier((half, fields, middle_iter))
     half_mate = lax.ppermute(half, "c", swap)
     (result,) = call(
         last_kernel, [source.shape],
-        half, half_mate, fields, middle_iter, fine_fields, fine_iter,
+        half, half_mate, matrix, fields, middle_iter, fine_fields, fine_iter,
         scratch=[(2 * chips, 8, 128)] * 4
         + [(2 * chips + 2, 8, 128), (2 * chips, 8, 128), (2 * chips + 4, 8, 128)]
         + [(5 * (8 * nz + 8) + 16, 128), (4 * 24 + 16, 128)],

time: 75.7 us -> 77.3 us (1.021)
  waiting for transfers between devices: 11 us -> 17.3 us
  blocking collectives: 16.8 us -> 14.4 us
  starting transfers between devices: 40.6 us -> 39 us
    ppermute x3, waiting for transfers between devices: 1.62 us -> 9.09 us  [the longest x1 4.8 us: shards(): face = lax.ppermute(face, ('y', 'x', 'c'), facing)]
    ppermute x3, starting transfers between devices: 11.3 us -> 8.04 us  [the longest x1 4.83 us: shards(): before = lax.ppermute(tail, 'z', up)]
    all_to_all x1, blocking collectives: 16.8 us -> 14.4 us  [shards(): got = lax.all_to_all(sent, ('c', 'z'), 0, 0).reshape(16 * nz, 128)]
    ppermute x1, starting transfers between devices: 4.6 us -> 5.76 us  [shards(): mate = lax.ppermute(own, 'c', swap)]
    ppermute x1, waiting for transfers between devices: 1.11 us -> 0.01 us  [shards(): mate = lax.ppermute(own, 'c', swap)]
    pallas_call x4 -> x6, Pallas kernels: 5.41 us -> 5.21 us  [call(): pl.pallas_call(kernel, out_shape=[jax.ShapeDtypeStruct(*(out if isinstanc...]
  transfers between devices with their start and end apart: 9 -> 9, of which waited for: 7 -> 6; matrix products, arithmetic and copies ran while one was open for 0% -> 0% of each run, Pallas kernels for 0% -> 0%
where the time goes in v4:
time: 77.3 us; the launch traced here: 76.8 us
  starting transfers between devices  39 us (50%)
  waiting for transfers between devices  17.3 us (22%)
  blocking collectives  14.4 us (19%)
  Pallas kernels  5.21 us (7%)
  other arithmetic  0.81 us (1%)
    all_to_all x1, blocking collectives, shards(): got = lax.all_to_all(sent, ('c', 'z'), 0, 0).reshape(16 * nz, 128)  14.4 us
    all_to_all x1, starting transfers between devices, shards(): half = lax.all_to_all(sent, ('y', 'x'), 0, 0)  11.5 us
    ppermute x1, starting transfers between devices, shards(): mate = lax.ppermute(own, 'c', swap)  5.76 us
    ppermute x1, starting transfers between devices, shards(): half_mate = lax.ppermute(half, 'c', swap)  5.22 us
    pallas_call x6, Pallas kernels, call(): pl.pallas_call(kernel, out_shape=[jax.ShapeDtypeStruct(*(out if isinstanc...  5.21 us
    all_to_all x1, waiting for transfers between devices, shards(): half = lax.all_to_all(sent, ('y', 'x'), 0, 0)  4.97 us
    ppermute x1, starting transfers between devices, shards(): before = lax.ppermute(tail, 'z', up)  4.83 us
    ppermute x1, waiting for transfers between devices, shards(): face = lax.ppermute(face, ('y', 'x', 'c'), facing)  4.8 us
  transfers between devices with their start and end apart: 9, of which 6 were waited for; matrix products, arithmetic and copies ran while one was open for 0% of the time, Pallas kernels for 0%

profile of v4, /device:TPU:1, one launch (start us, length us, event | category | flops | bytes accessed | tf_op | source)
XLA Modules:
  0.0 76.8 jit_solution(14873772715514869878)
XLA Ops:
  0.0 0.8 %pad_maximum_fusion.own_ref = f32[3,4,16,128]{3,2,1,0:T(8,128)S(1)} fusion(f32[1,4,16,128]{3,2,1,0:T(8,128)} %bitcast.9, f32[1,4,16,128]{3,2,1,0:T(8,128)} %bitcast.10, f32[1,4,16,128]{3,2,1,0:T(8,128)} %bitcast.11), kind=kLoop, calls=%fused_computation | loop fusion | flops 49152 | bytes 196608 | tf_op jit(solution)/shard_map/stack | solution.py:374
  0.8 4.8 %collective-permute-start = (f32[120,128]{1,0:T(8,128)S(1)}, f32[120,128]{1,0:T(8,128)S(1)}, u32[]{:S(2)}, u32[]{:S(2)}) collective-permute-start(f32[120,128]{1,0:T(8,128)S(1)} %get-tuple-element.21), channel_id=1, source_target_pairs={{0,1},{1,2},{2,3},{3,4},{4,5},{5,6},{6,7},{8,9},{9,10},{10,11},{11... | collective-permute-start | bytes 184328 | tf_op jit(solution)/shard_map/ppermute | solution.py:378
  5.7 1.3 %collective-permute-start.1 = (f32[120,128]{1,0:T(8,128)S(1)}, f32[120,128]{1,0:T(8,128)S(1)}, u32[]{:S(2)}, u32[]{:S(2)}) collective-permute-start(f32[120,128]{1,0:T(8,128)S(1)} %get-tuple-element.22), channel_id=1, source_target_pairs={{1,0},{2,1},{3,2},{4,3},{5,4},{6,5},{7,6},{9,8},{10,9},{11,10},{12... | collective-permute-start | bytes 184328 | tf_op jit(solution)/shard_map/ppermute | solution.py:379
  7.0 0.0 collective-permute-done.before_ref
  7.0 4.3 %collective-permute-done.1.after_ref = f32[120,128]{1,0:T(8,128)S(1)} collective-permute-done((f32[120,128]{1,0:T(8,128)S(1)}, f32[120,128]{1,0:T(8,128)S(1)}, u32[]{:S(2)}, u32[]{:S(2)}) %collective-permute-start.1) | collective-permute-done | bytes 61472 | tf_op jit(solution)/shard_map/ppermute | solution.py:379
  11.3 5.8 %collective-permute-start.2 = (f32[3,4,40,128]{3,2,1,0:T(8,128)S(1)}, f32[3,4,40,128]{3,2,1,0:T(8,128)S(1)}, u32[]{:S(2)}, u32[]{:S(2)}) collective-permute-start(f32[3,4,40,128]{3,2,1,0:T(8,128)S(1)} %get-tuple-element.23.own_ref), channel_id=1, source_target_pairs={{0,8},{8,0},{1,9},{9,1},{2,10},{10,2},{3,11},{11,3},{4,12},{12,4},... | collective-permute-start | bytes 737288 | tf_op jit(solution)/shard_map/ppermute | solution.py:386
  17.1 1.9 %collective-permute-start.3 = (f32[336,128]{1,0:T(8,128)S(1)}, f32[336,128]{1,0:T(8,128)S(1)}, u32[]{:S(2)}, u32[]{:S(2)}) collective-permute-start(f32[336,128]{1,0:T(8,128)S(1)} %get-tuple-element.24), channel_id=1, source_target_pairs={{8,16},{16,8},{24,32},{32,24},{40,48},{48,40},{56,64},{64,56},{72,... | collective-permute-start | bytes 516104 | tf_op jit(solution)/shard_map/ppermute | solution.py:385
  19.0 4.8 %collective-permute-done.3.face_ref = f32[336,128]{1,0:T(8,128)S(1)} collective-permute-done((f32[336,128]{1,0:T(8,128)S(1)}, f32[336,128]{1,0:T(8,128)S(1)}, u32[]{:S(2)}, u32[]{:S(2)}) %collective-permute-start.3) | collective-permute-done | bytes 172064 | tf_op jit(solution)/shard_map/ppermute | solution.py:385
  23.8 0.0 collective-permute-done.2.mate_ref
  23.8 1.0 %shard_map.39 = (f32[8,24,128]{2,1,0:T(8,128)S(1)}, f32[4,8,24,128]{3,2,1,0:T(8,128)S(1)}, f32[16,8,128]{2,1,0:T(8,128)S(1)}, f32[3,16,128]{2,1,0:T(8,128)S(1)}) custom-call(f32[3,4,40,128]{3,2,1,0:T(8,128)S(1)} %get-tuple-element.23.own_ref, f32[3,4,40,128]{3,2,1,0:T(8,128)S(1)} %collective-permute-done.2.mate_ref, ...), custom_call_target="tpu_custom_call" | custom-call | tf_op jit(solution)/shard_map/pallas_call | solution.py:356
  24.8 14.4 %all_to_all.10 = f32[16,8,128]{2,1,0:T(8,128)S(1)} all-to-all(f32[16,8,128]{2,1,0:T(8,128)S(1)} %get-tuple-element.26), channel_id=1, replica_groups=mesh['y'=8,'x'=4,'c'=2,'z'=8] {'c','z'}, dimensions={0} | all-to-all | bytes 131072 | tf_op jit(solution)/shard_map/all_to_all | solution.py:394
  39.2 0.9 %shard_map.40 = f32[32,32,128]{2,1,0:T(8,128)} custom-call(f32[128,128]{1,0:T(8,128)S(1)} %bitcast.8), custom_call_target="tpu_custom_call" | custom-call | tf_op jit(solution)/shard_map/pallas_call | solution.py:356
  40.0 11.5 %all-to-all-start.1 = ((f32[32,32,128]{2,1,0:T(8,128)}), f32[32,32,128]{2,1,0:T(8,128)S(1)}, u32[]{:S(2)}, u32[]{:S(2)}) async-start(f32[32,32,128]{2,1,0:T(8,128)} %shard_map.40), calls=%async_computation.1 | async-start | bytes 1048576 | tf_op jit(solution)/shard_map/all_to_all | solution.py:399
  51.6 3.1 %collective-permute-start.4 = (f32[3,16,128]{2,1,0:T(8,128)S(1)}, f32[3,16,128]{2,1,0:T(8,128)S(1)}, u32[]{:S(2)}, u32[]{:S(2)}) collective-permute-start(f32[3,16,128]{2,1,0:T(8,128)S(1)} %get-tuple-element.28.own_ref), channel_id=1, source_target_pairs={{0,8},{8,0},{1,9},{9,1},{2,10},{10,2},{3,11},{11,3},{4,12},{12,4},... | collective-permute-start | bytes 73736 | tf_op jit(solution)/shard_map/ppermute | solution.py:401
  54.7 0.8 %collective-permute-done.4.mate_ref = f32[3,16,128]{2,1,0:T(8,128)S(1)} collective-permute-done((f32[3,16,128]{2,1,0:T(8,128)S(1)}, f32[3,16,128]{2,1,0:T(8,128)S(1)}, u32[]{:S(2)}, u32[]{:S(2)}) %collective-permute-start.4) | collective-permute-done | bytes 24608 | tf_op jit(solution)/shard_map/ppermute | solution.py:401
  55.5 1.3 %collective-permute-start.5 = (f32[2,3,16,128]{3,2,1,0:T(8,128)S(1)}, f32[2,3,16,128]{3,2,1,0:T(8,128)S(1)}, u32[]{:S(2)}, u32[]{:S(2)}) collective-permute-start(f32[2,3,16,128]{3,2,1,0:T(8,128)S(1)} %pad_maximum_fusion.1), channel_id=1, source_target_pairs={{0,16},{24,8},{16,32},{40,24},{32,48},{56,40},{48,64},{72,56},{64,... | collective-permute-start | bytes 147464 | tf_op jit(solution)/shard_map/ppermute | solution.py:406
  56.8 4.0 %collective-permute-start.6 = (f32[3,16,128]{2,1,0:T(8,128)S(1)}, f32[3,16,128]{2,1,0:T(8,128)S(1)}, u32[]{:S(2)}, u32[]{:S(2)}) collective-permute-start(f32[3,16,128]{2,1,0:T(8,128)S(1)} %get-tuple-element.28.own_ref), channel_id=1, source_target_pairs={{16,0},{8,24},{32,16},{24,40},{48,32},{40,56},{64,48},{56,72},{80,... | collective-permute-start | bytes 73736 | tf_op jit(solution)/shard_map/ppermute | solution.py:407
  60.9 0.9 %collective-permute-done.6.inner_ref = f32[3,16,128]{2,1,0:T(8,128)S(1)} collective-permute-done((f32[3,16,128]{2,1,0:T(8,128)S(1)}, f32[3,16,128]{2,1,0:T(8,128)S(1)}, u32[]{:S(2)}, u32[]{:S(2)}) %collective-permute-start.6) | collective-permute-done | bytes 24608 | tf_op jit(solution)/shard_map/ppermute | solution.py:407
  61.8 0.0 collective-permute-done.5.outer_ref
  61.8 0.2 shard_map.41
  62.0 5.0 %all-to-all-done.1.got_ref = f32[32,32,128]{2,1,0:T(8,128)S(1)} async-done(((f32[32,32,128]{2,1,0:T(8,128)}), f32[32,32,128]{2,1,0:T(8,128)S(1)}, u32[]{:S(2)}, u32[]{:S(2)}) %all-to-all-start.1) | async-done | bytes 524320 | tf_op jit(solution)/shard_map/all_to_all | solution.py:399
  67.0 5.2 %collective-permute-start.7 = (f32[32,32,128]{2,1,0:T(8,128)S(1)}, f32[32,32,128]{2,1,0:T(8,128)S(1)}, u32[]{:S(2)}, u32[]{:S(2)}) collective-permute-start(f32[32,32,128]{2,1,0:T(8,128)S(1)} %all-to-all-done.1.got_ref), channel_id=1, source_target_pairs={{0,8},{8,0},{1,9},{9,1},{2,10},{10,2},{3,11},{11,3},{4,12},{12,4},... | collective-permute-start | bytes 1572872 | tf_op jit(solution)/shard_map/ppermute | solution.py:414
  72.2 1.5 %collective-permute-done.7.mate_ref = f32[32,32,128]{2,1,0:T(8,128)S(1)} collective-permute-done((f32[32,32,128]{2,1,0:T(8,128)S(1)}, f32[32,32,128]{2,1,0:T(8,128)S(1)}, u32[]{:S(2)}, u32[]{:S(2)}) %collective-permute-start.7) | collective-permute-done | bytes 524320 | tf_op jit(solution)/shard_map/ppermute | solution.py:414
  73.7 3.1 %shard_map.42 = f32[4,16,128]{2,1,0:T(8,128)} custom-call(f32[32,32,128]{2,1,0:T(8,128)S(1)} %all-to-all-done.1.got_ref, f32[32,32,128]{2,1,0:T(8,128)S(1)} %collective-permute-done.7.mate_ref, bf16[256,256]{1,0:T(8,128)(2,1)S(1)} %get-tuple-element.32.matrix_ref, f32[4,5,16,128]{3,2,1,0:T(8,128)S(1)} %get-tuple-element.33.field_ref, ...), custom_call_target="tpu_custom_call" | custom-call | tf_op jit(solution)/shard_map/pallas_call | solution.py:356
  (4 shorter events, 0.1 us)
Async XLA Ops:
  0.8 6.1 %collective-permute-start = (f32[120,128]{1,0:T(8,128)S(1)}, f32[120,128]{1,0:T(8,128)S(1)}, u32[]{:S(2)}, u32[]{:S(2)}) collective-permute-start(f32[120,128]{1,0:T(8,128)S(1)} %get-tuple-element.21), channel_id=1, source_target_pairs={{0,1},{1,2},{2,3},{3,4},{4,5},{5,6},{6,7},{8,9},{9,10},{10,11},{11... | collective-permute-start | bytes 184328 | tf_op jit(solution)/shard_map/ppermute | solution.py:378
  5.7 5.6 %collective-permute-start.1 = (f32[120,128]{1,0:T(8,128)S(1)}, f32[120,128]{1,0:T(8,128)S(1)}, u32[]{:S(2)}, u32[]{:S(2)}) collective-permute-start(f32[120,128]{1,0:T(8,128)S(1)} %get-tuple-element.22), channel_id=1, source_target_pairs={{1,0},{2,1},{3,2},{4,3},{5,4},{6,5},{7,6},{9,8},{10,9},{11,10},{12... | collective-permute-start | bytes 184328 | tf_op jit(solution)/shard_map/ppermute | solution.py:379
  11.3 12.5 %collective-permute-start.2 = (f32[3,4,40,128]{3,2,1,0:T(8,128)S(1)}, f32[3,4,40,128]{3,2,1,0:T(8,128)S(1)}, u32[]{:S(2)}, u32[]{:S(2)}) collective-permute-start(f32[3,4,40,128]{3,2,1,0:T(8,128)S(1)} %get-tuple-element.23.own_ref), channel_id=1, source_target_pairs={{0,8},{8,0},{1,9},{9,1},{2,10},{10,2},{3,11},{11,3},{4,12},{12,4},... | collective-permute-start | bytes 737288 | tf_op jit(solution)/shard_map/ppermute | solution.py:386
  17.1 6.7 %collective-permute-start.3 = (f32[336,128]{1,0:T(8,128)S(1)}, f32[336,128]{1,0:T(8,128)S(1)}, u32[]{:S(2)}, u32[]{:S(2)}) collective-permute-start(f32[336,128]{1,0:T(8,128)S(1)} %get-tuple-element.24), channel_id=1, source_target_pairs={{8,16},{16,8},{24,32},{32,24},{40,48},{48,40},{56,64},{64,56},{72,... | collective-permute-start | bytes 516104 | tf_op jit(solution)/shard_map/ppermute | solution.py:385
  40.0 27.0 %all-to-all-start.1 = ((f32[32,32,128]{2,1,0:T(8,128)}), f32[32,32,128]{2,1,0:T(8,128)S(1)}, u32[]{:S(2)}, u32[]{:S(2)}) async-start(f32[32,32,128]{2,1,0:T(8,128)} %shard_map.40), calls=%async_computation.1 | async-start | bytes 1048576 | tf_op jit(solution)/shard_map/all_to_all | solution.py:399
  51.6 3.9 %collective-permute-start.4 = (f32[3,16,128]{2,1,0:T(8,128)S(1)}, f32[3,16,128]{2,1,0:T(8,128)S(1)}, u32[]{:S(2)}, u32[]{:S(2)}) collective-permute-start(f32[3,16,128]{2,1,0:T(8,128)S(1)} %get-tuple-element.28.own_ref), channel_id=1, source_target_pairs={{0,8},{8,0},{1,9},{9,1},{2,10},{10,2},{3,11},{11,3},{4,12},{12,4},... | collective-permute-start | bytes 73736 | tf_op jit(solution)/shard_map/ppermute | solution.py:401
  55.5 6.3 %collective-permute-start.5 = (f32[2,3,16,128]{3,2,1,0:T(8,128)S(1)}, f32[2,3,16,128]{3,2,1,0:T(8,128)S(1)}, u32[]{:S(2)}, u32[]{:S(2)}) collective-permute-start(f32[2,3,16,128]{3,2,1,0:T(8,128)S(1)} %pad_maximum_fusion.1), channel_id=1, source_target_pairs={{0,16},{24,8},{16,32},{40,24},{32,48},{56,40},{48,64},{72,56},{64,... | collective-permute-start | bytes 147464 | tf_op jit(solution)/shard_map/ppermute | solution.py:406
  56.8 5.0 %collective-permute-start.6 = (f32[3,16,128]{2,1,0:T(8,128)S(1)}, f32[3,16,128]{2,1,0:T(8,128)S(1)}, u32[]{:S(2)}, u32[]{:S(2)}) collective-permute-start(f32[3,16,128]{2,1,0:T(8,128)S(1)} %get-tuple-element.28.own_ref), channel_id=1, source_target_pairs={{16,0},{8,24},{32,16},{24,40},{48,32},{40,56},{64,48},{56,72},{80,... | collective-permute-start | bytes 73736 | tf_op jit(solution)/shard_map/ppermute | solution.py:407
  67.0 6.7 %collective-permute-start.7 = (f32[32,32,128]{2,1,0:T(8,128)S(1)}, f32[32,32,128]{2,1,0:T(8,128)S(1)}, u32[]{:S(2)}, u32[]{:S(2)}) collective-permute-start(f32[32,32,128]{2,1,0:T(8,128)S(1)} %all-to-all-done.1.got_ref), channel_id=1, source_target_pairs={{0,8},{8,0},{1,9},{9,1},{2,10},{10,2},{3,11},{11,3},{4,12},{12,4},... | collective-permute-start | bytes 1572872 | tf_op jit(solution)/shard_map/ppermute | solution.py:414

commit v5 on v4

--- a/solution.py
+++ b/solution.py
@@ -80,7 +80,7 @@
             last_ref[at : at + 10] = own_ref[k, p, 6:]
 
 
-def block_kernel(own_ref, before_ref, after_ref, block_ref, face_ref):
+def block_kernel(own_ref, before_ref, after_ref, block_ref, face_ref, mate_ref):
     left = lax.axis_index("c") == 0
     none = jnp.zeros((2, 128), F32)
     for k in range(3):
@@ -91,33 +91,38 @@
             block_ref[k, p, 28:38] = after_ref[at : at + 10]
             block_ref[k, p, :2] = none
             block_ref[k, p, 38:] = none
+
+    def send(at, k, low, high, rows):
+        low, high = block_ref[k, low, rows], block_ref[k, high, rows]
+        size = low.shape[0]
+        face_ref[at : at + size] = jnp.where(left, low, high)
+        mate_ref[at : at + size] = jnp.where(left, high, low)
+
     for k in range(3):
         for p in range(2):
-            at = 40 * (2 * k + p)
-            face_ref[at : at + 40] = jnp.where(left, block_ref[k, p], block_ref[k, p + 2])
-        at = 240 + 24 * k
-        rows = slice(8, 32)
-        face_ref[at : at + 24] = jnp.where(left, block_ref[k, 2, rows], block_ref[k, 1, rows])
-    face_ref[312:] = jnp.where(left, block_ref[1, 3, rows], block_ref[1, 0, rows])
+            send(40 * (2 * k + p), k, p, p + 2, slice(0, 40))
+        send(240 + 24 * k, k, 2, 1, slice(8, 32))
+    send(312, 1, 3, 0, slice(8, 32))
+    face_ref[336:] = jnp.zeros((8, 128), F32)
 
 
 def fine_kernel(
     own_ref, mate_ref, face_ref, iter_ref, field_ref, piece_ref, one_ref, coef_rows, rows_ref
 ):
     left = lax.axis_index("c") == 0
+    face, mate = face_ref[:336], mate_ref[...]
+    low, high = jnp.where(left, face, mate), jnp.where(left, mate, face)
+    pad = jnp.zeros((1, 8, 128), F32)
     blocks = []
     for k in range(3):
-        mate = mate_ref[k]
-        near = face_ref[80 * k : 80 * k + 80].reshape(2, 40, 128)
-        pad = jnp.zeros((1, 8, 128), F32)
-        third = face_ref[240 + 24 * k : 264 + 24 * k][None]
-        fourth = face_ref[312:][None] if k == 1 else jnp.zeros_like(third)
-        third, fourth = (
-            jnp.concatenate([pad, t, pad], axis=1) for t in (third, fourth)
-        )
-        before = jnp.where(left, jnp.concatenate([fourth, third, near], axis=0), mate)
-        after = jnp.where(left, mate, jnp.concatenate([near, third, fourth], axis=0))
-        blocks.append(jnp.concatenate([before, own_ref[k], after], axis=0))
+        sides = []
+        for t in (low, high):
+            far = [t[240 + 24 * k : 264 + 24 * k], t[312:]]
+            if k != 1:
+                far[1] = jnp.zeros_like(far[1])
+            far = [jnp.concatenate([pad, u[None], pad], axis=1) for u in far]
+            sides.append([t[80 * k : 80 * k + 80].reshape(2, 40, 128)] + far)
+        blocks.append(jnp.concatenate(sides[0][::-1] + [own_ref[k]] + sides[1], axis=0))
     f, a, s = blocks
     coefs = pair_planes([t[4 * p : 4 * p + 4] for t in (a, s) for p in range(3)], coef_rows)
     w = relax_weight(a[1:11], s[1:11], 1.0)
@@ -245,45 +250,48 @@
     return jnp.sum(jnp.sum(plane, axis=0, keepdims=True), axis=1, keepdims=True)
 
 
-def solve_coarse(q_ref, a_ref, d_ref, inverse_ref, z_ref, image_ref, e_ref, matrix):
-    planes = q_ref.shape[0]
+def solve_coarse(q_ref, a_ref, d_ref, inverse_ref, w_ref, y_ref, at, matrix):
+    planes = a_ref.shape[0]
     chunk = 16 if planes % 16 == 0 else 2
     starts = range(0, planes, chunk)
-    none = jnp.zeros((1, 8, 128), F32)
-    z_ref[:1] = none
-    z_ref[planes + 1 :] = none
-    for i in (0, 1, planes + 2, planes + 3):
-        e_ref[i : i + 1] = none
+    none = jnp.zeros((2, 8, 128), F32)
+    for ref in (q_ref, inverse_ref, w_ref):
+        ref[:2] = none
+        ref[planes + 2 :] = none
     for i in starts:
-        own = slice(i, i + chunk)
-        inverse = 1.0 / (d_ref[own] - a_ref[own])
-        inverse_ref[own] = inverse
-        z_ref[i + 1 : i + chunk + 1] = q_ref[own] * inverse
+        own, padded = slice(i, i + chunk), slice(i + 2, i + chunk + 2)
+        inverse_ref[padded] = 1.0 / (d_ref[own] - a_ref[own])
+
+    def product(ref):
+        for i in starts:
+            own, wide = slice(i, i + chunk), slice(i + 1, i + chunk + 3)
+            z = ref[wide] * inverse_ref[wide]
+            y_ref[own] = d_ref[own] * z[1:-1] - a_ref[own] * coarse_box(z, matrix)
+
+    product(q_ref)
+    solution = jnp.zeros((5, 8, 128), F32)
     for step in range(COARSE):
         upper = lower = jnp.zeros((8, 128), F32)
         for i in starts:
-            own = slice(i, i + chunk)
-            z = z_ref[i : i + chunk + 2]
-            image = d_ref[own] * z[1:-1] - a_ref[own] * coarse_box(z, matrix)
-            image_ref[own] = image
-            upper = upper + jnp.sum(image * q_ref[own], axis=0)
-            lower = lower + jnp.sum(image * image, axis=0)
+            own, padded = slice(i, i + chunk), slice(i + 2, i + chunk + 2)
+            w, q = y_ref[own], q_ref[padded]
+            if step > 0:
+                old = w_ref[padded]
+                w, q = old - alpha * w, q - alpha * old
+                q_ref[padded] = q
+            w_ref[padded] = w
+            upper = upper + jnp.sum(w * q, axis=0)
+            lower = lower + jnp.sum(w * w, axis=0)
         alpha = (total(upper) / total(lower))[None]
-        for i in starts:
-            own = slice(i, i + chunk)
-            inner = slice(i + 1, i + chunk + 1)
-            outer = slice(i + 2, i + chunk + 2)
-            gain = alpha * z_ref[inner]
-            e_ref[outer] = gain if step == 0 else e_ref[outer] + gain
-            if step < COARSE - 1:
-                q = q_ref[own] - alpha * image_ref[own]
-                q_ref[own] = q
-                z_ref[inner] = q * inverse_ref[own]
+        if step < COARSE - 1:
+            product(w_ref)
+        solution = solution + alpha * q_ref[pl.ds(at, 5)]
+    return solution * inverse_ref[pl.ds(at, 5)]
 
 
 def last_kernel(
     got_ref, mate_ref, matrix_ref, field_ref, middle_ref, fine_ref, iter_ref, out_ref,
-    q_ref, a_ref, d_ref, inverse_ref, z_ref, image_ref, coarse_ref, middle_rows, fine_rows,
+    q_ref, a_ref, d_ref, inverse_ref, w_ref, y_ref, middle_rows, fine_rows,
 ):
     nx = lax.axis_size("x")
     chip = lax.axis_index("y") * nx + lax.axis_index("x")
@@ -301,17 +309,16 @@
         return jnp.concatenate([first[:, None], second[:, None]], axis=1).reshape(planes, 8, 128)
 
     edge = jnp.zeros_like(part(0, 0)[:1])
-    q_ref[...] = pairs(
+    q_ref[2 : planes + 2] = pairs(
         part(0, 1) + jnp.concatenate([edge, part(1, 0)[:-1]], axis=0),
         part(1, 1) + jnp.concatenate([part(0, 0)[1:], edge], axis=0),
     )
     a = 0.0625 * pairs(part(0, 2), part(1, 2))
     a_ref[...] = a
     d_ref[...] = 27.0 * a + pairs(part(0, 3), part(1, 3))
-    solve_coarse(
-        q_ref, a_ref, d_ref, inverse_ref, z_ref, image_ref, coarse_ref, matrix_ref[...]
-    )
-    near = coarse_ref[pl.ds(chip * 2 + core, 5)]
+    near = solve_coarse(
+        q_ref, a_ref, d_ref, inverse_ref, w_ref, y_ref, chip * 2 + core, matrix_ref[...]
+    )
 
     mask = quarter_mask()
     stack = jnp.concatenate([(near[p][None] * mask).reshape(32, 128) for p in range(5)], axis=0)
@@ -377,13 +384,15 @@
     down = [(i + 1, i) for i in range(nz - 1)]
     before = lax.ppermute(tail, "z", up)
     after = lax.ppermute(head, "z", down)
-    own, face = call(block_kernel, [(3, 4, 40, 128), (336, 128)], own, before, after)
+    own, face, mate = call(
+        block_kernel, [(3, 4, 40, 128), (344, 128), (336, 128)], own, before, after
+    )
     facing = []
     for i in range(chips - 1):
         facing += [(2 * i + 1, 2 * i + 2), (2 * i + 2, 2 * i + 1)]
     swap = [(0, 1), (1, 0)]
     face = lax.ppermute(face, ("y", "x", "c"), facing)
-    mate = lax.ppermute(own, "c", swap)
+    mate = lax.ppermute(mate, "c", swap)
     fine_iter, fine_fields, sent, one = call(
         fine_kernel,
         [(8, 24, 128), (4, 8, 24, 128), (2 * nz, 8, 128), (3, 16, 128)],
@@ -415,8 +424,8 @@
     (result,) = call(
         last_kernel, [source.shape],
         half, half_mate, matrix, fields, middle_iter, fine_fields, fine_iter,
-        scratch=[(2 * chips, 8, 128)] * 4
-        + [(2 * chips + 2, 8, 128), (2 * chips, 8, 128), (2 * chips + 4, 8, 128)]
+        scratch=[(2 * chips + 4, 8, 128)] + [(2 * chips, 8, 128)] * 2
+        + [(2 * chips + 4, 8, 128)] * 2 + [(2 * chips, 8, 128)]
         + [(5 * (8 * nz + 8) + 16, 128), (4 * 24 + 16, 128)],
     )
     return result

time: 77.3 us -> 73.9 us (0.956)
  waiting for transfers between devices: 17.3 us -> 13.9 us
  blocking collectives: 14.4 us -> 16.5 us
  starting transfers between devices: 39 us -> 37.3 us
    ppermute x1, waiting for transfers between devices: 4.8 us -> 0.01 us  [shards(): face = lax.ppermute(face, ('y', 'x', 'c'), facing)]
    ppermute x1, starting transfers between devices: 5.76 us -> 1.92 us  [shards(): mate = lax.ppermute(mate, 'c', swap)]
    ppermute x1, starting transfers between devices: 1.92 us -> 4.83 us  [shards(): face = lax.ppermute(face, ('y', 'x', 'c'), facing)]
    all_to_all x1, blocking collectives: 14.4 us -> 16.5 us  [shards(): got = lax.all_to_all(sent, ('c', 'z'), 0, 0).reshape(16 * nz, 128)]
    ppermute x1, waiting for transfers between devices: 0.01 us -> 1.37 us  [shards(): mate = lax.ppermute(mate, 'c', swap)]
where the time goes in v5:
time: 73.9 us; the launch traced here: 73.4 us
  starting transfers between devices  37.3 us (50%)
  blocking collectives  16.5 us (22%)
  waiting for transfers between devices  13.9 us (19%)
  Pallas kernels  4.81 us (7%)
  other arithmetic  0.81 us (1%)
    all_to_all x1, blocking collectives, shards(): got = lax.all_to_all(sent, ('c', 'z'), 0, 0).reshape(16 * nz, 128)  16.5 us
    all_to_all x1, starting transfers between devices, shards(): half = lax.all_to_all(sent, ('y', 'x'), 0, 0)  10.8 us
    ppermute x1, starting transfers between devices, shards(): half_mate = lax.ppermute(half, 'c', swap)  5.22 us
    all_to_all x1, waiting for transfers between devices, shards(): half = lax.all_to_all(sent, ('y', 'x'), 0, 0)  4.97 us
    ppermute x1, starting transfers between devices, shards(): face = lax.ppermute(face, ('y', 'x', 'c'), facing)  4.83 us
    ppermute x1, starting transfers between devices, shards(): before = lax.ppermute(tail, 'z', up)  4.83 us
    pallas_call x6, Pallas kernels, call(): pl.pallas_call(kernel, out_shape=[jax.ShapeDtypeStruct(*(out if isinstanc...  4.81 us
    ppermute x1, waiting for transfers between devices, shards(): after = lax.ppermute(head, 'z', down)  4.29 us
  transfers between devices with their start and end apart: 9, of which 6 were waited for; matrix products, arithmetic and copies ran while one was open for 0% of the time, Pallas kernels for 0%

profile of v5, /device:TPU:1, one launch (start us, length us, event | category | flops | bytes accessed | tf_op | source)
XLA Modules:
  0.0 73.4 jit_solution(8038119142588995203)
XLA Ops:
  0.0 0.8 %pad_maximum_fusion.own_ref = f32[3,4,16,128]{3,2,1,0:T(8,128)S(1)} fusion(f32[1,4,16,128]{3,2,1,0:T(8,128)} %bitcast.9, f32[1,4,16,128]{3,2,1,0:T(8,128)} %bitcast.10, f32[1,4,16,128]{3,2,1,0:T(8,128)} %bitcast.11), kind=kLoop, calls=%fused_computation | loop fusion | flops 49152 | bytes 196608 | tf_op jit(solution)/shard_map/stack | solution.py:381
  0.8 4.8 %collective-permute-start = (f32[120,128]{1,0:T(8,128)S(1)}, f32[120,128]{1,0:T(8,128)S(1)}, u32[]{:S(2)}, u32[]{:S(2)}) collective-permute-start(f32[120,128]{1,0:T(8,128)S(1)} %get-tuple-element.22), channel_id=1, source_target_pairs={{0,1},{1,2},{2,3},{3,4},{4,5},{5,6},{6,7},{8,9},{9,10},{10,11},{11... | collective-permute-start | bytes 184328 | tf_op jit(solution)/shard_map/ppermute | solution.py:385
  5.7 1.3 %collective-permute-start.1 = (f32[120,128]{1,0:T(8,128)S(1)}, f32[120,128]{1,0:T(8,128)S(1)}, u32[]{:S(2)}, u32[]{:S(2)}) collective-permute-start(f32[120,128]{1,0:T(8,128)S(1)} %get-tuple-element.23), channel_id=1, source_target_pairs={{1,0},{2,1},{3,2},{4,3},{5,4},{6,5},{7,6},{9,8},{10,9},{11,10},{12... | collective-permute-start | bytes 184328 | tf_op jit(solution)/shard_map/ppermute | solution.py:386
  7.0 0.0 collective-permute-done.before_ref
  7.0 4.3 %collective-permute-done.1.after_ref = f32[120,128]{1,0:T(8,128)S(1)} collective-permute-done((f32[120,128]{1,0:T(8,128)S(1)}, f32[120,128]{1,0:T(8,128)S(1)}, u32[]{:S(2)}, u32[]{:S(2)}) %collective-permute-start.1) | collective-permute-done | bytes 61472 | tf_op jit(solution)/shard_map/ppermute | solution.py:386
  11.3 4.8 %collective-permute-start.3 = (f32[344,128]{1,0:T(8,128)S(1)}, f32[344,128]{1,0:T(8,128)S(1)}, u32[]{:S(2)}, u32[]{:S(2)}) collective-permute-start(f32[344,128]{1,0:T(8,128)S(1)} %get-tuple-element.26), channel_id=1, source_target_pairs={{8,16},{16,8},{24,32},{32,24},{40,48},{48,40},{56,64},{64,56},{72,... | collective-permute-start | bytes 528392 | tf_op jit(solution)/shard_map/ppermute | solution.py:394
  16.1 1.9 %collective-permute-start.2 = (f32[336,128]{1,0:T(8,128)S(1)}, f32[336,128]{1,0:T(8,128)S(1)}, u32[]{:S(2)}, u32[]{:S(2)}) collective-permute-start(f32[336,128]{1,0:T(8,128)S(1)} %get-tuple-element.25), channel_id=1, source_target_pairs={{0,8},{8,0},{1,9},{9,1},{2,10},{10,2},{3,11},{11,3},{4,12},{12,4},... | collective-permute-start | bytes 516104 | tf_op jit(solution)/shard_map/ppermute | solution.py:395
  18.1 1.4 %collective-permute-done.2.mate_ref = f32[336,128]{1,0:T(8,128)S(1)} collective-permute-done((f32[336,128]{1,0:T(8,128)S(1)}, f32[336,128]{1,0:T(8,128)S(1)}, u32[]{:S(2)}, u32[]{:S(2)}) %collective-permute-start.2) | collective-permute-done | bytes 172064 | tf_op jit(solution)/shard_map/ppermute | solution.py:395
  19.4 0.0 collective-permute-done.3.face_ref
  19.5 1.0 %shard_map.39 = (f32[8,24,128]{2,1,0:T(8,128)S(1)}, f32[4,8,24,128]{3,2,1,0:T(8,128)S(1)}, f32[16,8,128]{2,1,0:T(8,128)S(1)}, f32[3,16,128]{2,1,0:T(8,128)S(1)}) custom-call(f32[3,4,40,128]{3,2,1,0:T(8,128)S(1)} %get-tuple-element.24.own_ref, f32[336,128]{1,0:T(8,128)S(1)} %collective-permute-done.2.mate_ref, f32[344,128]{1,0:T(8,128)S(1)} %collective-permute-done.3.face_ref), custom_call_target="tpu_custom_call" | custom-call | tf_op jit(solution)/shard_map/pallas_call | solution.py:363
  20.4 16.5 %all_to_all.10 = f32[16,8,128]{2,1,0:T(8,128)S(1)} all-to-all(f32[16,8,128]{2,1,0:T(8,128)S(1)} %get-tuple-element.28), channel_id=1, replica_groups=mesh['y'=8,'x'=4,'c'=2,'z'=8] {'c','z'}, dimensions={0} | all-to-all | bytes 131072 | tf_op jit(solution)/shard_map/all_to_all | solution.py:403
  36.9 0.9 %shard_map.40 = f32[32,32,128]{2,1,0:T(8,128)} custom-call(f32[128,128]{1,0:T(8,128)S(1)} %bitcast.8), custom_call_target="tpu_custom_call" | custom-call | tf_op jit(solution)/shard_map/pallas_call | solution.py:363
  37.8 10.8 %all-to-all-start.1 = ((f32[32,32,128]{2,1,0:T(8,128)}), f32[32,32,128]{2,1,0:T(8,128)S(1)}, u32[]{:S(2)}, u32[]{:S(2)}) async-start(f32[32,32,128]{2,1,0:T(8,128)} %shard_map.40), calls=%async_computation.1 | async-start | bytes 1048576 | tf_op jit(solution)/shard_map/all_to_all | solution.py:408
  48.6 3.1 %collective-permute-start.4 = (f32[3,16,128]{2,1,0:T(8,128)S(1)}, f32[3,16,128]{2,1,0:T(8,128)S(1)}, u32[]{:S(2)}, u32[]{:S(2)}) collective-permute-start(f32[3,16,128]{2,1,0:T(8,128)S(1)} %get-tuple-element.30.own_ref), channel_id=1, source_target_pairs={{0,8},{8,0},{1,9},{9,1},{2,10},{10,2},{3,11},{11,3},{4,12},{12,4},... | collective-permute-start | bytes 73736 | tf_op jit(solution)/shard_map/ppermute | solution.py:410
  51.7 0.8 %collective-permute-done.4.mate_ref = f32[3,16,128]{2,1,0:T(8,128)S(1)} collective-permute-done((f32[3,16,128]{2,1,0:T(8,128)S(1)}, f32[3,16,128]{2,1,0:T(8,128)S(1)}, u32[]{:S(2)}, u32[]{:S(2)}) %collective-permute-start.4) | collective-permute-done | bytes 24608 | tf_op jit(solution)/shard_map/ppermute | solution.py:410
  52.5 1.3 %collective-permute-start.5 = (f32[2,3,16,128]{3,2,1,0:T(8,128)S(1)}, f32[2,3,16,128]{3,2,1,0:T(8,128)S(1)}, u32[]{:S(2)}, u32[]{:S(2)}) collective-permute-start(f32[2,3,16,128]{3,2,1,0:T(8,128)S(1)} %pad_maximum_fusion.1), channel_id=1, source_target_pairs={{0,16},{24,8},{16,32},{40,24},{32,48},{56,40},{48,64},{72,56},{64,... | collective-permute-start | bytes 147464 | tf_op jit(solution)/shard_map/ppermute | solution.py:415
  53.8 4.0 %collective-permute-start.6 = (f32[3,16,128]{2,1,0:T(8,128)S(1)}, f32[3,16,128]{2,1,0:T(8,128)S(1)}, u32[]{:S(2)}, u32[]{:S(2)}) collective-permute-start(f32[3,16,128]{2,1,0:T(8,128)S(1)} %get-tuple-element.30.own_ref), channel_id=1, source_target_pairs={{16,0},{8,24},{32,16},{24,40},{48,32},{40,56},{64,48},{56,72},{80,... | collective-permute-start | bytes 73736 | tf_op jit(solution)/shard_map/ppermute | solution.py:416
  57.9 0.9 %collective-permute-done.6.inner_ref = f32[3,16,128]{2,1,0:T(8,128)S(1)} collective-permute-done((f32[3,16,128]{2,1,0:T(8,128)S(1)}, f32[3,16,128]{2,1,0:T(8,128)S(1)}, u32[]{:S(2)}, u32[]{:S(2)}) %collective-permute-start.6) | collective-permute-done | bytes 24608 | tf_op jit(solution)/shard_map/ppermute | solution.py:416
  58.8 0.0 collective-permute-done.5.outer_ref
  58.8 0.2 shard_map.41
  59.1 5.0 %all-to-all-done.1.got_ref = f32[32,32,128]{2,1,0:T(8,128)S(1)} async-done(((f32[32,32,128]{2,1,0:T(8,128)}), f32[32,32,128]{2,1,0:T(8,128)S(1)}, u32[]{:S(2)}, u32[]{:S(2)}) %all-to-all-start.1) | async-done | bytes 524320 | tf_op jit(solution)/shard_map/all_to_all | solution.py:408
  64.0 5.2 %collective-permute-start.7 = (f32[32,32,128]{2,1,0:T(8,128)S(1)}, f32[32,32,128]{2,1,0:T(8,128)S(1)}, u32[]{:S(2)}, u32[]{:S(2)}) collective-permute-start(f32[32,32,128]{2,1,0:T(8,128)S(1)} %all-to-all-done.1.got_ref), channel_id=1, source_target_pairs={{0,8},{8,0},{1,9},{9,1},{2,10},{10,2},{3,11},{11,3},{4,12},{12,4},... | collective-permute-start | bytes 1572872 | tf_op jit(solution)/shard_map/ppermute | solution.py:423
  69.3 1.5 %collective-permute-done.7.mate_ref = f32[32,32,128]{2,1,0:T(8,128)S(1)} collective-permute-done((f32[32,32,128]{2,1,0:T(8,128)S(1)}, f32[32,32,128]{2,1,0:T(8,128)S(1)}, u32[]{:S(2)}, u32[]{:S(2)}) %collective-permute-start.7) | collective-permute-done | bytes 524320 | tf_op jit(solution)/shard_map/ppermute | solution.py:423
  70.8 2.7 %shard_map.42 = f32[4,16,128]{2,1,0:T(8,128)} custom-call(f32[32,32,128]{2,1,0:T(8,128)S(1)} %all-to-all-done.1.got_ref, f32[32,32,128]{2,1,0:T(8,128)S(1)} %collective-permute-done.7.mate_ref, bf16[256,256]{1,0:T(8,128)(2,1)S(1)} %get-tuple-element.34.matrix_ref, f32[4,5,16,128]{3,2,1,0:T(8,128)S(1)} %get-tuple-element.35.field_ref, ...), custom_call_target="tpu_custom_call" | custom-call | tf_op jit(solution)/shard_map/pallas_call | solution.py:363
  (4 shorter events, 0.1 us)
Async XLA Ops:
  0.8 6.1 %collective-permute-start = (f32[120,128]{1,0:T(8,128)S(1)}, f32[120,128]{1,0:T(8,128)S(1)}, u32[]{:S(2)}, u32[]{:S(2)}) collective-permute-start(f32[120,128]{1,0:T(8,128)S(1)} %get-tuple-element.22), channel_id=1, source_target_pairs={{0,1},{1,2},{2,3},{3,4},{4,5},{5,6},{6,7},{8,9},{9,10},{10,11},{11... | collective-permute-start | bytes 184328 | tf_op jit(solution)/shard_map/ppermute | solution.py:385
  5.7 5.6 %collective-permute-start.1 = (f32[120,128]{1,0:T(8,128)S(1)}, f32[120,128]{1,0:T(8,128)S(1)}, u32[]{:S(2)}, u32[]{:S(2)}) collective-permute-start(f32[120,128]{1,0:T(8,128)S(1)} %get-tuple-element.23), channel_id=1, source_target_pairs={{1,0},{2,1},{3,2},{4,3},{5,4},{6,5},{7,6},{9,8},{10,9},{11,10},{12... | collective-permute-start | bytes 184328 | tf_op jit(solution)/shard_map/ppermute | solution.py:386
  11.3 8.1 %collective-permute-start.3 = (f32[344,128]{1,0:T(8,128)S(1)}, f32[344,128]{1,0:T(8,128)S(1)}, u32[]{:S(2)}, u32[]{:S(2)}) collective-permute-start(f32[344,128]{1,0:T(8,128)S(1)} %get-tuple-element.26), channel_id=1, source_target_pairs={{8,16},{16,8},{24,32},{32,24},{40,48},{48,40},{56,64},{64,56},{72,... | collective-permute-start | bytes 528392 | tf_op jit(solution)/shard_map/ppermute | solution.py:394
  16.1 3.3 %collective-permute-start.2 = (f32[336,128]{1,0:T(8,128)S(1)}, f32[336,128]{1,0:T(8,128)S(1)}, u32[]{:S(2)}, u32[]{:S(2)}) collective-permute-start(f32[336,128]{1,0:T(8,128)S(1)} %get-tuple-element.25), channel_id=1, source_target_pairs={{0,8},{8,0},{1,9},{9,1},{2,10},{10,2},{3,11},{11,3},{4,12},{12,4},... | collective-permute-start | bytes 516104 | tf_op jit(solution)/shard_map/ppermute | solution.py:395
  37.8 26.3 %all-to-all-start.1 = ((f32[32,32,128]{2,1,0:T(8,128)}), f32[32,32,128]{2,1,0:T(8,128)S(1)}, u32[]{:S(2)}, u32[]{:S(2)}) async-start(f32[32,32,128]{2,1,0:T(8,128)} %shard_map.40), calls=%async_computation.1 | async-start | bytes 1048576 | tf_op jit(solution)/shard_map/all_to_all | solution.py:408
  48.6 3.9 %collective-permute-start.4 = (f32[3,16,128]{2,1,0:T(8,128)S(1)}, f32[3,16,128]{2,1,0:T(8,128)S(1)}, u32[]{:S(2)}, u32[]{:S(2)}) collective-permute-start(f32[3,16,128]{2,1,0:T(8,128)S(1)} %get-tuple-element.30.own_ref), channel_id=1, source_target_pairs={{0,8},{8,0},{1,9},{9,1},{2,10},{10,2},{3,11},{11,3},{4,12},{12,4},... | collective-permute-start | bytes 73736 | tf_op jit(solution)/shard_map/ppermute | solution.py:410
  52.5 6.3 %collective-permute-start.5 = (f32[2,3,16,128]{3,2,1,0:T(8,128)S(1)}, f32[2,3,16,128]{3,2,1,0:T(8,128)S(1)}, u32[]{:S(2)}, u32[]{:S(2)}) collective-permute-start(f32[2,3,16,128]{3,2,1,0:T(8,128)S(1)} %pad_maximum_fusion.1), channel_id=1, source_target_pairs={{0,16},{24,8},{16,32},{40,24},{32,48},{56,40},{48,64},{72,56},{64,... | collective-permute-start | bytes 147464 | tf_op jit(solution)/shard_map/ppermute | solution.py:415
  53.8 5.0 %collective-permute-start.6 = (f32[3,16,128]{2,1,0:T(8,128)S(1)}, f32[3,16,128]{2,1,0:T(8,128)S(1)}, u32[]{:S(2)}, u32[]{:S(2)}) collective-permute-start(f32[3,16,128]{2,1,0:T(8,128)S(1)} %get-tuple-element.30.own_ref), channel_id=1, source_target_pairs={{16,0},{8,24},{32,16},{24,40},{48,32},{40,56},{64,48},{56,72},{80,... | collective-permute-start | bytes 73736 | tf_op jit(solution)/shard_map/ppermute | solution.py:416
  64.0 6.7 %collective-permute-start.7 = (f32[32,32,128]{2,1,0:T(8,128)S(1)}, f32[32,32,128]{2,1,0:T(8,128)S(1)}, u32[]{:S(2)}, u32[]{:S(2)}) collective-permute-start(f32[32,32,128]{2,1,0:T(8,128)S(1)} %all-to-all-done.1.got_ref), channel_id=1, source_target_pairs={{0,8},{8,0},{1,9},{9,1},{2,10},{10,2},{3,11},{11,3},{4,12},{12,4},... | collective-permute-start | bytes 1572872 | tf_op jit(solution)/shard_map/ppermute | solution.py:423

commit v6 on v5

--- a/solution.py
+++ b/solution.py
@@ -262,9 +262,11 @@
         own, padded = slice(i, i + chunk), slice(i + 2, i + chunk + 2)
         inverse_ref[padded] = 1.0 / (d_ref[own] - a_ref[own])
 
+    span = 2 * chunk if planes % (2 * chunk) == 0 else chunk
+
     def product(ref):
-        for i in starts:
-            own, wide = slice(i, i + chunk), slice(i + 1, i + chunk + 3)
+        for i in range(0, planes, span):
+            own, wide = slice(i, i + span), slice(i + 1, i + span + 3)
             z = ref[wide] * inverse_ref[wide]
             y_ref[own] = d_ref[own] * z[1:-1] - a_ref[own] * coarse_box(z, matrix)
 
@@ -291,31 +293,29 @@
 
 def last_kernel(
     got_ref, mate_ref, matrix_ref, field_ref, middle_ref, fine_ref, iter_ref, out_ref,
-    q_ref, a_ref, d_ref, inverse_ref, w_ref, y_ref, middle_rows, fine_rows,
+    q_ref, a_ref, d_ref, inverse_ref, w_ref, y_ref, mine_out, mate_out, middle_rows, fine_rows,
 ):
     nx = lax.axis_size("x")
     chip = lax.axis_index("y") * nx + lax.axis_index("x")
     core = lax.axis_index("c")
     rank = lax.axis_index("z")
-    planes = 2 * got_ref.shape[0]
-
-    got, mate = got_ref[...], mate_ref[...]
-    halves = jnp.where(core == 0, got, mate), jnp.where(core == 0, mate, got)
-
-    def part(half, k):
-        return halves[half][:, 8 * k : 8 * k + 8]
-
-    def pairs(first, second):
-        return jnp.concatenate([first[:, None], second[:, None]], axis=1).reshape(planes, 8, 128)
-
-    edge = jnp.zeros_like(part(0, 0)[:1])
-    q_ref[2 : planes + 2] = pairs(
-        part(0, 1) + jnp.concatenate([edge, part(1, 0)[:-1]], axis=0),
-        part(1, 1) + jnp.concatenate([part(0, 0)[1:], edge], axis=0),
-    )
-    a = 0.0625 * pairs(part(0, 2), part(1, 2))
-    a_ref[...] = a
-    d_ref[...] = 27.0 * a + pairs(part(0, 3), part(1, 3))
+
+    chips = got_ref.shape[0]
+    order = [i % nx * (chips // nx) + i // nx for i in range(chips)]
+    none = jnp.zeros((1, 8, 128), F32)
+    for ref, outward_ref in ((got_ref, mine_out), (mate_ref, mate_out)):
+        outward_ref[:1] = none
+        outward_ref[chips + 1 :] = none
+        for i in range(chips):
+            outward_ref[i + 1] = ref[order[i], :8]
+    for ref, outward_ref, side in ((got_ref, mate_out, core), (mate_ref, mine_out, 1 - core)):
+        for i in range(chips):
+            piece = ref.at[order[i]]
+            q = piece[8:16][None] + outward_ref[pl.ds(i + 2 * side, 1)]
+            a = 0.0625 * piece[16:24][None]
+            q_ref[pl.ds(2 * i + 2 + side, 1)] = q
+            a_ref[pl.ds(2 * i + side, 1)] = a
+            d_ref[pl.ds(2 * i + side, 1)] = 27.0 * a + piece[24:32][None]
     near = solve_coarse(
         q_ref, a_ref, d_ref, inverse_ref, w_ref, y_ref, chip * 2 + core, matrix_ref[...]
     )
@@ -405,7 +405,7 @@
         gather_kernel, [(chips, 32, 128)], got, scratch=[(16 * nz + 16, 128)]
     )
     one, sent = lax.optimization_barrier((one, sent))
-    half = lax.all_to_all(sent, ("y", "x"), 0, 0)
+    half = lax.all_to_all(sent, ("x", "y"), 0, 0)
 
     mate = lax.ppermute(one, "c", swap)
     pairs = jnp.stack([jnp.where(first, one, mate), jnp.where(first, mate, one)])
@@ -425,7 +425,7 @@
         last_kernel, [source.shape],
         half, half_mate, matrix, fields, middle_iter, fine_fields, fine_iter,
         scratch=[(2 * chips + 4, 8, 128)] + [(2 * chips, 8, 128)] * 2
-        + [(2 * chips + 4, 8, 128)] * 2 + [(2 * chips, 8, 128)]
+        + [(2 * chips + 4, 8, 128)] * 2 + [(2 * chips, 8, 128)] + [(chips + 2, 8, 128)] * 2
         + [(5 * (8 * nz + 8) + 16, 128), (4 * 24 + 16, 128)],
     )
     return result

time: 73.9 us -> 73.3 us (level)
  waiting for transfers between devices: 13.9 us -> 12.5 us
    all_to_all x1, waiting for transfers between devices: 4.97 us -> 3.59 us  [shards(): half = lax.all_to_all(sent, ('x', 'y'), 0, 0)]
where the time goes in v6:
time: 73.3 us; the launch traced here: 72.9 us
  starting transfers between devices  38 us (52%)
  blocking collectives  16.5 us (23%)
  waiting for transfers between devices  12.5 us (17%)
  Pallas kernels  4.9 us (7%)
  other arithmetic  0.81 us (1%)
    all_to_all x1, blocking collectives, shards(): got = lax.all_to_all(sent, ('c', 'z'), 0, 0).reshape(16 * nz, 128)  16.5 us
    all_to_all x1, starting transfers between devices, shards(): half = lax.all_to_all(sent, ('x', 'y'), 0, 0)  10.8 us
    ppermute x1, starting transfers between devices, shards(): half_mate = lax.ppermute(half, 'c', swap)  5.93 us
    pallas_call x6, Pallas kernels, call(): pl.pallas_call(kernel, out_shape=[jax.ShapeDtypeStruct(*(out if isinstanc...  4.9 us
    ppermute x1, starting transfers between devices, shards(): face = lax.ppermute(face, ('y', 'x', 'c'), facing)  4.83 us
    ppermute x1, starting transfers between devices, shards(): before = lax.ppermute(tail, 'z', up)  4.83 us
    ppermute x1, waiting for transfers between devices, shards(): after = lax.ppermute(head, 'z', down)  4.29 us
    ppermute x1, starting transfers between devices, shards(): inner = lax.ppermute(one, ('y', 'x', 'c'), [(j, i) for i, j in ring])  4.05 us
  transfers between devices with their start and end apart: 9, of which 6 were waited for; matrix products, arithmetic and copies ran while one was open for 0% of the time, Pallas kernels for 0%

profile of v6, /device:TPU:1, one launch (start us, length us, event | category | flops | bytes accessed | tf_op | source)
XLA Modules:
  0.0 72.9 jit_solution(17106702182987306944)
XLA Ops:
  0.0 0.8 %pad_maximum_fusion.own_ref = f32[3,4,16,128]{3,2,1,0:T(8,128)S(1)} fusion(f32[1,4,16,128]{3,2,1,0:T(8,128)} %bitcast.9, f32[1,4,16,128]{3,2,1,0:T(8,128)} %bitcast.10, f32[1,4,16,128]{3,2,1,0:T(8,128)} %bitcast.11), kind=kLoop, calls=%fused_computation | loop fusion | flops 49152 | bytes 196608 | tf_op jit(solution)/shard_map/stack | solution.py:381
  0.8 4.8 %collective-permute-start = (f32[120,128]{1,0:T(8,128)S(1)}, f32[120,128]{1,0:T(8,128)S(1)}, u32[]{:S(2)}, u32[]{:S(2)}) collective-permute-start(f32[120,128]{1,0:T(8,128)S(1)} %get-tuple-element.22), channel_id=1, source_target_pairs={{0,1},{1,2},{2,3},{3,4},{4,5},{5,6},{6,7},{8,9},{9,10},{10,11},{11... | collective-permute-start | bytes 184328 | tf_op jit(solution)/shard_map/ppermute | solution.py:385
  5.7 1.3 %collective-permute-start.1 = (f32[120,128]{1,0:T(8,128)S(1)}, f32[120,128]{1,0:T(8,128)S(1)}, u32[]{:S(2)}, u32[]{:S(2)}) collective-permute-start(f32[120,128]{1,0:T(8,128)S(1)} %get-tuple-element.23), channel_id=1, source_target_pairs={{1,0},{2,1},{3,2},{4,3},{5,4},{6,5},{7,6},{9,8},{10,9},{11,10},{12... | collective-permute-start | bytes 184328 | tf_op jit(solution)/shard_map/ppermute | solution.py:386
  7.0 0.0 collective-permute-done.before_ref
  7.0 4.3 %collective-permute-done.1.after_ref = f32[120,128]{1,0:T(8,128)S(1)} collective-permute-done((f32[120,128]{1,0:T(8,128)S(1)}, f32[120,128]{1,0:T(8,128)S(1)}, u32[]{:S(2)}, u32[]{:S(2)}) %collective-permute-start.1) | collective-permute-done | bytes 61472 | tf_op jit(solution)/shard_map/ppermute | solution.py:386
  11.3 4.8 %collective-permute-start.3 = (f32[344,128]{1,0:T(8,128)S(1)}, f32[344,128]{1,0:T(8,128)S(1)}, u32[]{:S(2)}, u32[]{:S(2)}) collective-permute-start(f32[344,128]{1,0:T(8,128)S(1)} %get-tuple-element.26), channel_id=1, source_target_pairs={{8,16},{16,8},{24,32},{32,24},{40,48},{48,40},{56,64},{64,56},{72,... | collective-permute-start | bytes 528392 | tf_op jit(solution)/shard_map/ppermute | solution.py:394
  16.1 1.9 %collective-permute-start.2 = (f32[336,128]{1,0:T(8,128)S(1)}, f32[336,128]{1,0:T(8,128)S(1)}, u32[]{:S(2)}, u32[]{:S(2)}) collective-permute-start(f32[336,128]{1,0:T(8,128)S(1)} %get-tuple-element.25), channel_id=1, source_target_pairs={{0,8},{8,0},{1,9},{9,1},{2,10},{10,2},{3,11},{11,3},{4,12},{12,4},... | collective-permute-start | bytes 516104 | tf_op jit(solution)/shard_map/ppermute | solution.py:395
  18.1 1.4 %collective-permute-done.2.mate_ref = f32[336,128]{1,0:T(8,128)S(1)} collective-permute-done((f32[336,128]{1,0:T(8,128)S(1)}, f32[336,128]{1,0:T(8,128)S(1)}, u32[]{:S(2)}, u32[]{:S(2)}) %collective-permute-start.2) | collective-permute-done | bytes 172064 | tf_op jit(solution)/shard_map/ppermute | solution.py:395
  19.4 0.0 collective-permute-done.3.face_ref
  19.5 1.0 %shard_map.39 = (f32[8,24,128]{2,1,0:T(8,128)S(1)}, f32[4,8,24,128]{3,2,1,0:T(8,128)S(1)}, f32[16,8,128]{2,1,0:T(8,128)S(1)}, f32[3,16,128]{2,1,0:T(8,128)S(1)}) custom-call(f32[3,4,40,128]{3,2,1,0:T(8,128)S(1)} %get-tuple-element.24.own_ref, f32[336,128]{1,0:T(8,128)S(1)} %collective-permute-done.2.mate_ref, f32[344,128]{1,0:T(8,128)S(1)} %collective-permute-done.3.face_ref), custom_call_target="tpu_custom_call" | custom-call | tf_op jit(solution)/shard_map/pallas_call | solution.py:363
  20.4 16.5 %all_to_all.10 = f32[16,8,128]{2,1,0:T(8,128)S(1)} all-to-all(f32[16,8,128]{2,1,0:T(8,128)S(1)} %get-tuple-element.28), channel_id=1, replica_groups=mesh['y'=8,'x'=4,'c'=2,'z'=8] {'c','z'}, dimensions={0} | all-to-all | bytes 131072 | tf_op jit(solution)/shard_map/all_to_all | solution.py:403
  36.9 0.9 %shard_map.40 = f32[32,32,128]{2,1,0:T(8,128)} custom-call(f32[128,128]{1,0:T(8,128)S(1)} %bitcast.8), custom_call_target="tpu_custom_call" | custom-call | tf_op jit(solution)/shard_map/pallas_call | solution.py:363
  37.8 10.8 %all-to-all-start.1 = ((f32[32,32,128]{2,1,0:T(8,128)}), f32[32,32,128]{2,1,0:T(8,128)S(1)}, u32[]{:S(2)}, u32[]{:S(2)}) async-start(f32[32,32,128]{2,1,0:T(8,128)} %shard_map.40), calls=%async_computation.1 | async-start | bytes 1048576 | tf_op jit(solution)/shard_map/all_to_all | solution.py:408
  48.6 3.1 %collective-permute-start.4 = (f32[3,16,128]{2,1,0:T(8,128)S(1)}, f32[3,16,128]{2,1,0:T(8,128)S(1)}, u32[]{:S(2)}, u32[]{:S(2)}) collective-permute-start(f32[3,16,128]{2,1,0:T(8,128)S(1)} %get-tuple-element.30.own_ref), channel_id=1, source_target_pairs={{0,8},{8,0},{1,9},{9,1},{2,10},{10,2},{3,11},{11,3},{4,12},{12,4},... | collective-permute-start | bytes 73736 | tf_op jit(solution)/shard_map/ppermute | solution.py:410
  51.7 0.8 %collective-permute-done.4.mate_ref = f32[3,16,128]{2,1,0:T(8,128)S(1)} collective-permute-done((f32[3,16,128]{2,1,0:T(8,128)S(1)}, f32[3,16,128]{2,1,0:T(8,128)S(1)}, u32[]{:S(2)}, u32[]{:S(2)}) %collective-permute-start.4) | collective-permute-done | bytes 24608 | tf_op jit(solution)/shard_map/ppermute | solution.py:410
  52.5 1.3 %collective-permute-start.5 = (f32[2,3,16,128]{3,2,1,0:T(8,128)S(1)}, f32[2,3,16,128]{3,2,1,0:T(8,128)S(1)}, u32[]{:S(2)}, u32[]{:S(2)}) collective-permute-start(f32[2,3,16,128]{3,2,1,0:T(8,128)S(1)} %pad_maximum_fusion.1), channel_id=1, source_target_pairs={{0,16},{24,8},{16,32},{40,24},{32,48},{56,40},{48,64},{72,56},{64,... | collective-permute-start | bytes 147464 | tf_op jit(solution)/shard_map/ppermute | solution.py:415
  53.8 4.0 %collective-permute-start.6 = (f32[3,16,128]{2,1,0:T(8,128)S(1)}, f32[3,16,128]{2,1,0:T(8,128)S(1)}, u32[]{:S(2)}, u32[]{:S(2)}) collective-permute-start(f32[3,16,128]{2,1,0:T(8,128)S(1)} %get-tuple-element.30.own_ref), channel_id=1, source_target_pairs={{16,0},{8,24},{32,16},{24,40},{48,32},{40,56},{64,48},{56,72},{80,... | collective-permute-start | bytes 73736 | tf_op jit(solution)/shard_map/ppermute | solution.py:416
  57.9 0.9 %collective-permute-done.6.inner_ref = f32[3,16,128]{2,1,0:T(8,128)S(1)} collective-permute-done((f32[3,16,128]{2,1,0:T(8,128)S(1)}, f32[3,16,128]{2,1,0:T(8,128)S(1)}, u32[]{:S(2)}, u32[]{:S(2)}) %collective-permute-start.6) | collective-permute-done | bytes 24608 | tf_op jit(solution)/shard_map/ppermute | solution.py:416
  58.8 0.0 collective-permute-done.5.outer_ref
  58.8 0.2 shard_map.41
  59.1 3.6 %all-to-all-done.1.got_ref = f32[32,32,128]{2,1,0:T(8,128)S(1)} async-done(((f32[32,32,128]{2,1,0:T(8,128)}), f32[32,32,128]{2,1,0:T(8,128)S(1)}, u32[]{:S(2)}, u32[]{:S(2)}) %all-to-all-start.1) | async-done | bytes 524320 | tf_op jit(solution)/shard_map/all_to_all | solution.py:408
  62.7 5.9 %collective-permute-start.7 = (f32[32,32,128]{2,1,0:T(8,128)S(1)}, f32[32,32,128]{2,1,0:T(8,128)S(1)}, u32[]{:S(2)}, u32[]{:S(2)}) collective-permute-start(f32[32,32,128]{2,1,0:T(8,128)S(1)} %all-to-all-done.1.got_ref), channel_id=1, source_target_pairs={{0,8},{8,0},{1,9},{9,1},{2,10},{10,2},{3,11},{11,3},{4,12},{12,4},... | collective-permute-start | bytes 1572872 | tf_op jit(solution)/shard_map/ppermute | solution.py:423
  68.6 1.5 %collective-permute-done.7.mate_ref = f32[32,32,128]{2,1,0:T(8,128)S(1)} collective-permute-done((f32[32,32,128]{2,1,0:T(8,128)S(1)}, f32[32,32,128]{2,1,0:T(8,128)S(1)}, u32[]{:S(2)}, u32[]{:S(2)}) %collective-permute-start.7) | collective-permute-done | bytes 524320 | tf_op jit(solution)/shard_map/ppermute | solution.py:423
  70.1 2.7 %shard_map.42 = f32[4,16,128]{2,1,0:T(8,128)} custom-call(f32[32,32,128]{2,1,0:T(8,128)S(1)} %all-to-all-done.1.got_ref, f32[32,32,128]{2,1,0:T(8,128)S(1)} %collective-permute-done.7.mate_ref, bf16[256,256]{1,0:T(8,128)(2,1)S(1)} %get-tuple-element.34.matrix_ref, f32[4,5,16,128]{3,2,1,0:T(8,128)S(1)} %get-tuple-element.35.field_ref, ...), custom_call_target="tpu_custom_call" | custom-call | tf_op jit(solution)/shard_map/pallas_call | solution.py:363
  (4 shorter events, 0.1 us)
Async XLA Ops:
  0.8 6.1 %collective-permute-start = (f32[120,128]{1,0:T(8,128)S(1)}, f32[120,128]{1,0:T(8,128)S(1)}, u32[]{:S(2)}, u32[]{:S(2)}) collective-permute-start(f32[120,128]{1,0:T(8,128)S(1)} %get-tuple-element.22), channel_id=1, source_target_pairs={{0,1},{1,2},{2,3},{3,4},{4,5},{5,6},{6,7},{8,9},{9,10},{10,11},{11... | collective-permute-start | bytes 184328 | tf_op jit(solution)/shard_map/ppermute | solution.py:385
  5.7 5.6 %collective-permute-start.1 = (f32[120,128]{1,0:T(8,128)S(1)}, f32[120,128]{1,0:T(8,128)S(1)}, u32[]{:S(2)}, u32[]{:S(2)}) collective-permute-start(f32[120,128]{1,0:T(8,128)S(1)} %get-tuple-element.23), channel_id=1, source_target_pairs={{1,0},{2,1},{3,2},{4,3},{5,4},{6,5},{7,6},{9,8},{10,9},{11,10},{12... | collective-permute-start | bytes 184328 | tf_op jit(solution)/shard_map/ppermute | solution.py:386
  11.3 8.1 %collective-permute-start.3 = (f32[344,128]{1,0:T(8,128)S(1)}, f32[344,128]{1,0:T(8,128)S(1)}, u32[]{:S(2)}, u32[]{:S(2)}) collective-permute-start(f32[344,128]{1,0:T(8,128)S(1)} %get-tuple-element.26), channel_id=1, source_target_pairs={{8,16},{16,8},{24,32},{32,24},{40,48},{48,40},{56,64},{64,56},{72,... | collective-permute-start | bytes 528392 | tf_op jit(solution)/shard_map/ppermute | solution.py:394
  16.1 3.3 %collective-permute-start.2 = (f32[336,128]{1,0:T(8,128)S(1)}, f32[336,128]{1,0:T(8,128)S(1)}, u32[]{:S(2)}, u32[]{:S(2)}) collective-permute-start(f32[336,128]{1,0:T(8,128)S(1)} %get-tuple-element.25), channel_id=1, source_target_pairs={{0,8},{8,0},{1,9},{9,1},{2,10},{10,2},{3,11},{11,3},{4,12},{12,4},... | collective-permute-start | bytes 516104 | tf_op jit(solution)/shard_map/ppermute | solution.py:395
  37.8 24.9 %all-to-all-start.1 = ((f32[32,32,128]{2,1,0:T(8,128)}), f32[32,32,128]{2,1,0:T(8,128)S(1)}, u32[]{:S(2)}, u32[]{:S(2)}) async-start(f32[32,32,128]{2,1,0:T(8,128)} %shard_map.40), calls=%async_computation.1 | async-start | bytes 1048576 | tf_op jit(solution)/shard_map/all_to_all | solution.py:408
  48.6 3.9 %collective-permute-start.4 = (f32[3,16,128]{2,1,0:T(8,128)S(1)}, f32[3,16,128]{2,1,0:T(8,128)S(1)}, u32[]{:S(2)}, u32[]{:S(2)}) collective-permute-start(f32[3,16,128]{2,1,0:T(8,128)S(1)} %get-tuple-element.30.own_ref), channel_id=1, source_target_pairs={{0,8},{8,0},{1,9},{9,1},{2,10},{10,2},{3,11},{11,3},{4,12},{12,4},... | collective-permute-start | bytes 73736 | tf_op jit(solution)/shard_map/ppermute | solution.py:410
  52.5 6.3 %collective-permute-start.5 = (f32[2,3,16,128]{3,2,1,0:T(8,128)S(1)}, f32[2,3,16,128]{3,2,1,0:T(8,128)S(1)}, u32[]{:S(2)}, u32[]{:S(2)}) collective-permute-start(f32[2,3,16,128]{3,2,1,0:T(8,128)S(1)} %pad_maximum_fusion.1), channel_id=1, source_target_pairs={{0,16},{24,8},{16,32},{40,24},{32,48},{56,40},{48,64},{72,56},{64,... | collective-permute-start | bytes 147464 | tf_op jit(solution)/shard_map/ppermute | solution.py:415
  53.8 5.0 %collective-permute-start.6 = (f32[3,16,128]{2,1,0:T(8,128)S(1)}, f32[3,16,128]{2,1,0:T(8,128)S(1)}, u32[]{:S(2)}, u32[]{:S(2)}) collective-permute-start(f32[3,16,128]{2,1,0:T(8,128)S(1)} %get-tuple-element.30.own_ref), channel_id=1, source_target_pairs={{16,0},{8,24},{32,16},{24,40},{48,32},{40,56},{64,48},{56,72},{80,... | collective-permute-start | bytes 73736 | tf_op jit(solution)/shard_map/ppermute | solution.py:416
  62.7 7.4 %collective-permute-start.7 = (f32[32,32,128]{2,1,0:T(8,128)S(1)}, f32[32,32,128]{2,1,0:T(8,128)S(1)}, u32[]{:S(2)}, u32[]{:S(2)}) collective-permute-start(f32[32,32,128]{2,1,0:T(8,128)S(1)} %all-to-all-done.1.got_ref), channel_id=1, source_target_pairs={{0,8},{8,0},{1,9},{9,1},{2,10},{10,2},{3,11},{11,3},{4,12},{12,4},... | collective-permute-start | bytes 1572872 | tf_op jit(solution)/shard_map/ppermute | solution.py:423

commit v7 on v5

--- a/solution.py
+++ b/solution.py
@@ -10,13 +10,17 @@
 F32 = jnp.float32
 
 
-def dot(a, b):
+def split(a):
     high = a.astype(jnp.bfloat16)
     rest = a - high.astype(F32)
     middle = rest.astype(jnp.bfloat16)
     low = (rest - middle.astype(F32)).astype(jnp.bfloat16)
+    return [high, middle, low]
+
+
+def dot(a, b):
     parts = lax.dot_general(
-        jnp.concatenate([high, middle, low], axis=0),
+        jnp.concatenate(split(a), axis=0),
         b.astype(jnp.bfloat16),
         (((1,), (0,)), ((), ())),
         preferred_element_type=F32,
@@ -221,7 +225,7 @@
 
 
 def box_matrix():
-    lane, out = iota((256, 256), 0) % 128, iota((256, 256), 1)
+    lane, out = iota((384, 256), 0) % 128, iota((384, 256), 1)
     group, to = lane // 32, out % 128 // 32
     near = jnp.abs(lane % 32 - out % 32) <= 1
     same = (out < 128) & (jnp.abs(group - to) <= 1)
@@ -231,10 +235,8 @@
 
 def coarse_box(v, matrix):
     rows = (v[:-2] + v[1:-1] + v[2:]).reshape(-1, 128)
-    high = rows.astype(jnp.bfloat16)
-    low = (rows - high.astype(F32)).astype(jnp.bfloat16)
     both = lax.dot_general(
-        jnp.concatenate([high, low], axis=1),
+        jnp.concatenate(split(rows), axis=1),
         matrix,
         (((1,), (0,)), ((), ())),
         preferred_element_type=F32,
@@ -416,7 +418,7 @@
     inner = lax.ppermute(one, ("y", "x", "c"), [(j, i) for i, j in ring])
     fields, middle_iter, matrix = call(
         smooth_kernel,
-        [(4, 5, 16, 128), (5, 16, 128), ((256, 256), jnp.bfloat16)],
+        [(4, 5, 16, 128), (5, 16, 128), ((384, 256), jnp.bfloat16)],
         one, mate, outer, inner,
     )
     half, fields, middle_iter = lax.optimization_barrier((half, fields, middle_iter))

time: 73.9 us -> 74.1 us (level)
  no operation moved by 1% of the time
where the time goes in v7:
time: 74.1 us; the launch traced here: 73.6 us
  starting transfers between devices  37.3 us (50%)
  blocking collectives  16.5 us (22%)
  waiting for transfers between devices  13.8 us (19%)
  Pallas kernels  5.06 us (7%)
  other arithmetic  0.81 us (1%)
    all_to_all x1, blocking collectives, shards(): got = lax.all_to_all(sent, ('c', 'z'), 0, 0).reshape(16 * nz, 128)  16.5 us
    all_to_all x1, starting transfers between devices, shards(): half = lax.all_to_all(sent, ('y', 'x'), 0, 0)  10.8 us
    ppermute x1, starting transfers between devices, shards(): half_mate = lax.ppermute(half, 'c', swap)  5.22 us
    pallas_call x6, Pallas kernels, call(): pl.pallas_call(kernel, out_shape=[jax.ShapeDtypeStruct(*(out if isinstanc...  5.06 us
    all_to_all x1, waiting for transfers between devices, shards(): half = lax.all_to_all(sent, ('y', 'x'), 0, 0)  4.89 us
    ppermute x1, starting transfers between devices, shards(): face = lax.ppermute(face, ('y', 'x', 'c'), facing)  4.83 us
    ppermute x1, starting transfers between devices, shards(): before = lax.ppermute(tail, 'z', up)  4.83 us
    ppermute x1, waiting for transfers between devices, shards(): after = lax.ppermute(head, 'z', down)  4.29 us
  transfers between devices with their start and end apart: 9, of which 6 were waited for; matrix products, arithmetic and copies ran while one was open for 0% of the time, Pallas kernels for 0%

profile of v7, /device:TPU:1, one launch (start us, length us, event | category | flops | bytes accessed | tf_op | source)
XLA Modules:
  0.0 73.6 jit_solution(10170733542677690742)
XLA Ops:
  0.0 0.8 %pad_maximum_fusion.own_ref = f32[3,4,16,128]{3,2,1,0:T(8,128)S(1)} fusion(f32[1,4,16,128]{3,2,1,0:T(8,128)} %bitcast.9, f32[1,4,16,128]{3,2,1,0:T(8,128)} %bitcast.10, f32[1,4,16,128]{3,2,1,0:T(8,128)} %bitcast.11), kind=kLoop, calls=%fused_computation | loop fusion | flops 49152 | bytes 196608 | tf_op jit(solution)/shard_map/stack | solution.py:383
  0.8 4.8 %collective-permute-start = (f32[120,128]{1,0:T(8,128)S(1)}, f32[120,128]{1,0:T(8,128)S(1)}, u32[]{:S(2)}, u32[]{:S(2)}) collective-permute-start(f32[120,128]{1,0:T(8,128)S(1)} %get-tuple-element.22), channel_id=1, source_target_pairs={{0,1},{1,2},{2,3},{3,4},{4,5},{5,6},{6,7},{8,9},{9,10},{10,11},{11... | collective-permute-start | bytes 184328 | tf_op jit(solution)/shard_map/ppermute | solution.py:387
  5.7 1.3 %collective-permute-start.1 = (f32[120,128]{1,0:T(8,128)S(1)}, f32[120,128]{1,0:T(8,128)S(1)}, u32[]{:S(2)}, u32[]{:S(2)}) collective-permute-start(f32[120,128]{1,0:T(8,128)S(1)} %get-tuple-element.23), channel_id=1, source_target_pairs={{1,0},{2,1},{3,2},{4,3},{5,4},{6,5},{7,6},{9,8},{10,9},{11,10},{12... | collective-permute-start | bytes 184328 | tf_op jit(solution)/shard_map/ppermute | solution.py:388
  7.0 0.0 collective-permute-done.before_ref
  7.0 4.3 %collective-permute-done.1.after_ref = f32[120,128]{1,0:T(8,128)S(1)} collective-permute-done((f32[120,128]{1,0:T(8,128)S(1)}, f32[120,128]{1,0:T(8,128)S(1)}, u32[]{:S(2)}, u32[]{:S(2)}) %collective-permute-start.1) | collective-permute-done | bytes 61472 | tf_op jit(solution)/shard_map/ppermute | solution.py:388
  11.3 4.8 %collective-permute-start.3 = (f32[344,128]{1,0:T(8,128)S(1)}, f32[344,128]{1,0:T(8,128)S(1)}, u32[]{:S(2)}, u32[]{:S(2)}) collective-permute-start(f32[344,128]{1,0:T(8,128)S(1)} %get-tuple-element.26), channel_id=1, source_target_pairs={{8,16},{16,8},{24,32},{32,24},{40,48},{48,40},{56,64},{64,56},{72,... | collective-permute-start | bytes 528392 | tf_op jit(solution)/shard_map/ppermute | solution.py:396
  16.1 1.9 %collective-permute-start.2 = (f32[336,128]{1,0:T(8,128)S(1)}, f32[336,128]{1,0:T(8,128)S(1)}, u32[]{:S(2)}, u32[]{:S(2)}) collective-permute-start(f32[336,128]{1,0:T(8,128)S(1)} %get-tuple-element.25), channel_id=1, source_target_pairs={{0,8},{8,0},{1,9},{9,1},{2,10},{10,2},{3,11},{11,3},{4,12},{12,4},... | collective-permute-start | bytes 516104 | tf_op jit(solution)/shard_map/ppermute | solution.py:397
  18.1 1.4 %collective-permute-done.2.mate_ref = f32[336,128]{1,0:T(8,128)S(1)} collective-permute-done((f32[336,128]{1,0:T(8,128)S(1)}, f32[336,128]{1,0:T(8,128)S(1)}, u32[]{:S(2)}, u32[]{:S(2)}) %collective-permute-start.2) | collective-permute-done | bytes 172064 | tf_op jit(solution)/shard_map/ppermute | solution.py:397
  19.4 0.0 collective-permute-done.3.face_ref
  19.5 1.0 %shard_map.39 = (f32[8,24,128]{2,1,0:T(8,128)S(1)}, f32[4,8,24,128]{3,2,1,0:T(8,128)S(1)}, f32[16,8,128]{2,1,0:T(8,128)S(1)}, f32[3,16,128]{2,1,0:T(8,128)S(1)}) custom-call(f32[3,4,40,128]{3,2,1,0:T(8,128)S(1)} %get-tuple-element.24.own_ref, f32[336,128]{1,0:T(8,128)S(1)} %collective-permute-done.2.mate_ref, f32[344,128]{1,0:T(8,128)S(1)} %collective-permute-done.3.face_ref), custom_call_target="tpu_custom_call" | custom-call | tf_op jit(solution)/shard_map/pallas_call | solution.py:365
  20.4 16.5 %all_to_all.10 = f32[16,8,128]{2,1,0:T(8,128)S(1)} all-to-all(f32[16,8,128]{2,1,0:T(8,128)S(1)} %get-tuple-element.28), channel_id=1, replica_groups=mesh['y'=8,'x'=4,'c'=2,'z'=8] {'c','z'}, dimensions={0} | all-to-all | bytes 131072 | tf_op jit(solution)/shard_map/all_to_all | solution.py:405
  36.9 0.9 %shard_map.40 = f32[32,32,128]{2,1,0:T(8,128)} custom-call(f32[128,128]{1,0:T(8,128)S(1)} %bitcast.8), custom_call_target="tpu_custom_call" | custom-call | tf_op jit(solution)/shard_map/pallas_call | solution.py:365
  37.8 10.8 %all-to-all-start.1 = ((f32[32,32,128]{2,1,0:T(8,128)}), f32[32,32,128]{2,1,0:T(8,128)S(1)}, u32[]{:S(2)}, u32[]{:S(2)}) async-start(f32[32,32,128]{2,1,0:T(8,128)} %shard_map.40), calls=%async_computation.1 | async-start | bytes 1048576 | tf_op jit(solution)/shard_map/all_to_all | solution.py:410
  48.6 3.1 %collective-permute-start.4 = (f32[3,16,128]{2,1,0:T(8,128)S(1)}, f32[3,16,128]{2,1,0:T(8,128)S(1)}, u32[]{:S(2)}, u32[]{:S(2)}) collective-permute-start(f32[3,16,128]{2,1,0:T(8,128)S(1)} %get-tuple-element.30.own_ref), channel_id=1, source_target_pairs={{0,8},{8,0},{1,9},{9,1},{2,10},{10,2},{3,11},{11,3},{4,12},{12,4},... | collective-permute-start | bytes 73736 | tf_op jit(solution)/shard_map/ppermute | solution.py:412
  51.7 0.8 %collective-permute-done.4.mate_ref = f32[3,16,128]{2,1,0:T(8,128)S(1)} collective-permute-done((f32[3,16,128]{2,1,0:T(8,128)S(1)}, f32[3,16,128]{2,1,0:T(8,128)S(1)}, u32[]{:S(2)}, u32[]{:S(2)}) %collective-permute-start.4) | collective-permute-done | bytes 24608 | tf_op jit(solution)/shard_map/ppermute | solution.py:412
  52.5 1.3 %collective-permute-start.5 = (f32[2,3,16,128]{3,2,1,0:T(8,128)S(1)}, f32[2,3,16,128]{3,2,1,0:T(8,128)S(1)}, u32[]{:S(2)}, u32[]{:S(2)}) collective-permute-start(f32[2,3,16,128]{3,2,1,0:T(8,128)S(1)} %pad_maximum_fusion.1), channel_id=1, source_target_pairs={{0,16},{24,8},{16,32},{40,24},{32,48},{56,40},{48,64},{72,56},{64,... | collective-permute-start | bytes 147464 | tf_op jit(solution)/shard_map/ppermute | solution.py:417
  53.8 4.0 %collective-permute-start.6 = (f32[3,16,128]{2,1,0:T(8,128)S(1)}, f32[3,16,128]{2,1,0:T(8,128)S(1)}, u32[]{:S(2)}, u32[]{:S(2)}) collective-permute-start(f32[3,16,128]{2,1,0:T(8,128)S(1)} %get-tuple-element.30.own_ref), channel_id=1, source_target_pairs={{16,0},{8,24},{32,16},{24,40},{48,32},{40,56},{64,48},{56,72},{80,... | collective-permute-start | bytes 73736 | tf_op jit(solution)/shard_map/ppermute | solution.py:418
  57.9 0.9 %collective-permute-done.6.inner_ref = f32[3,16,128]{2,1,0:T(8,128)S(1)} collective-permute-done((f32[3,16,128]{2,1,0:T(8,128)S(1)}, f32[3,16,128]{2,1,0:T(8,128)S(1)}, u32[]{:S(2)}, u32[]{:S(2)}) %collective-permute-start.6) | collective-permute-done | bytes 24608 | tf_op jit(solution)/shard_map/ppermute | solution.py:418
  58.8 0.0 collective-permute-done.5.outer_ref
  58.8 0.3 shard_map.41
  59.1 4.9 %all-to-all-done.1.got_ref = f32[32,32,128]{2,1,0:T(8,128)S(1)} async-done(((f32[32,32,128]{2,1,0:T(8,128)}), f32[32,32,128]{2,1,0:T(8,128)S(1)}, u32[]{:S(2)}, u32[]{:S(2)}) %all-to-all-start.1) | async-done | bytes 524320 | tf_op jit(solution)/shard_map/all_to_all | solution.py:410
  64.0 5.2 %collective-permute-start.7 = (f32[32,32,128]{2,1,0:T(8,128)S(1)}, f32[32,32,128]{2,1,0:T(8,128)S(1)}, u32[]{:S(2)}, u32[]{:S(2)}) collective-permute-start(f32[32,32,128]{2,1,0:T(8,128)S(1)} %all-to-all-done.1.got_ref), channel_id=1, source_target_pairs={{0,8},{8,0},{1,9},{9,1},{2,10},{10,2},{3,11},{11,3},{4,12},{12,4},... | collective-permute-start | bytes 1572872 | tf_op jit(solution)/shard_map/ppermute | solution.py:425
  69.3 1.5 %collective-permute-done.7.mate_ref = f32[32,32,128]{2,1,0:T(8,128)S(1)} collective-permute-done((f32[32,32,128]{2,1,0:T(8,128)S(1)}, f32[32,32,128]{2,1,0:T(8,128)S(1)}, u32[]{:S(2)}, u32[]{:S(2)}) %collective-permute-start.7) | collective-permute-done | bytes 524320 | tf_op jit(solution)/shard_map/ppermute | solution.py:425
  70.8 2.8 %shard_map.42 = f32[4,16,128]{2,1,0:T(8,128)} custom-call(f32[32,32,128]{2,1,0:T(8,128)S(1)} %all-to-all-done.1.got_ref, f32[32,32,128]{2,1,0:T(8,128)S(1)} %collective-permute-done.7.mate_ref, bf16[384,256]{1,0:T(8,128)(2,1)S(1)} %get-tuple-element.34.matrix_ref, f32[4,5,16,128]{3,2,1,0:T(8,128)S(1)} %get-tuple-element.35.field_ref, ...), custom_call_target="tpu_custom_call" | custom-call | tf_op jit(solution)/shard_map/pallas_call | solution.py:365
  (4 shorter events, 0.1 us)
Async XLA Ops:
  0.8 6.1 %collective-permute-start = (f32[120,128]{1,0:T(8,128)S(1)}, f32[120,128]{1,0:T(8,128)S(1)}, u32[]{:S(2)}, u32[]{:S(2)}) collective-permute-start(f32[120,128]{1,0:T(8,128)S(1)} %get-tuple-element.22), channel_id=1, source_target_pairs={{0,1},{1,2},{2,3},{3,4},{4,5},{5,6},{6,7},{8,9},{9,10},{10,11},{11... | collective-permute-start | bytes 184328 | tf_op jit(solution)/shard_map/ppermute | solution.py:387
  5.7 5.6 %collective-permute-start.1 = (f32[120,128]{1,0:T(8,128)S(1)}, f32[120,128]{1,0:T(8,128)S(1)}, u32[]{:S(2)}, u32[]{:S(2)}) collective-permute-start(f32[120,128]{1,0:T(8,128)S(1)} %get-tuple-element.23), channel_id=1, source_target_pairs={{1,0},{2,1},{3,2},{4,3},{5,4},{6,5},{7,6},{9,8},{10,9},{11,10},{12... | collective-permute-start | bytes 184328 | tf_op jit(solution)/shard_map/ppermute | solution.py:388
  11.3 8.1 %collective-permute-start.3 = (f32[344,128]{1,0:T(8,128)S(1)}, f32[344,128]{1,0:T(8,128)S(1)}, u32[]{:S(2)}, u32[]{:S(2)}) collective-permute-start(f32[344,128]{1,0:T(8,128)S(1)} %get-tuple-element.26), channel_id=1, source_target_pairs={{8,16},{16,8},{24,32},{32,24},{40,48},{48,40},{56,64},{64,56},{72,... | collective-permute-start | bytes 528392 | tf_op jit(solution)/shard_map/ppermute | solution.py:396
  16.1 3.3 %collective-permute-start.2 = (f32[336,128]{1,0:T(8,128)S(1)}, f32[336,128]{1,0:T(8,128)S(1)}, u32[]{:S(2)}, u32[]{:S(2)}) collective-permute-start(f32[336,128]{1,0:T(8,128)S(1)} %get-tuple-element.25), channel_id=1, source_target_pairs={{0,8},{8,0},{1,9},{9,1},{2,10},{10,2},{3,11},{11,3},{4,12},{12,4},... | collective-permute-start | bytes 516104 | tf_op jit(solution)/shard_map/ppermute | solution.py:397
  37.8 26.3 %all-to-all-start.1 = ((f32[32,32,128]{2,1,0:T(8,128)}), f32[32,32,128]{2,1,0:T(8,128)S(1)}, u32[]{:S(2)}, u32[]{:S(2)}) async-start(f32[32,32,128]{2,1,0:T(8,128)} %shard_map.40), calls=%async_computation.1 | async-start | bytes 1048576 | tf_op jit(solution)/shard_map/all_to_all | solution.py:410
  48.6 3.9 %collective-permute-start.4 = (f32[3,16,128]{2,1,0:T(8,128)S(1)}, f32[3,16,128]{2,1,0:T(8,128)S(1)}, u32[]{:S(2)}, u32[]{:S(2)}) collective-permute-start(f32[3,16,128]{2,1,0:T(8,128)S(1)} %get-tuple-element.30.own_ref), channel_id=1, source_target_pairs={{0,8},{8,0},{1,9},{9,1},{2,10},{10,2},{3,11},{11,3},{4,12},{12,4},... | collective-permute-start | bytes 73736 | tf_op jit(solution)/shard_map/ppermute | solution.py:412
  52.5 6.3 %collective-permute-start.5 = (f32[2,3,16,128]{3,2,1,0:T(8,128)S(1)}, f32[2,3,16,128]{3,2,1,0:T(8,128)S(1)}, u32[]{:S(2)}, u32[]{:S(2)}) collective-permute-start(f32[2,3,16,128]{3,2,1,0:T(8,128)S(1)} %pad_maximum_fusion.1), channel_id=1, source_target_pairs={{0,16},{24,8},{16,32},{40,24},{32,48},{56,40},{48,64},{72,56},{64,... | collective-permute-start | bytes 147464 | tf_op jit(solution)/shard_map/ppermute | solution.py:417
  53.8 5.0 %collective-permute-start.6 = (f32[3,16,128]{2,1,0:T(8,128)S(1)}, f32[3,16,128]{2,1,0:T(8,128)S(1)}, u32[]{:S(2)}, u32[]{:S(2)}) collective-permute-start(f32[3,16,128]{2,1,0:T(8,128)S(1)} %get-tuple-element.30.own_ref), channel_id=1, source_target_pairs={{16,0},{8,24},{32,16},{24,40},{48,32},{40,56},{64,48},{56,72},{80,... | collective-permute-start | bytes 73736 | tf_op jit(solution)/shard_map/ppermute | solution.py:418
  64.0 6.7 %collective-permute-start.7 = (f32[32,32,128]{2,1,0:T(8,128)S(1)}, f32[32,32,128]{2,1,0:T(8,128)S(1)}, u32[]{:S(2)}, u32[]{:S(2)}) collective-permute-start(f32[32,32,128]{2,1,0:T(8,128)S(1)} %all-to-all-done.1.got_ref), channel_id=1, source_target_pairs={{0,8},{8,0},{1,9},{9,1},{2,10},{10,2},{3,11},{11,3},{4,12},{12,4},... | collective-permute-start | bytes 1572872 | tf_op jit(solution)/shard_map/ppermute | solution.py:425

commit v8 on v7

--- a/solution.py
+++ b/solution.py
@@ -270,24 +270,34 @@
             z = ref[wide] * inverse_ref[wide]
             y_ref[own] = d_ref[own] * z[1:-1] - a_ref[own] * coarse_box(z, matrix)
 
-    product(q_ref)
-    solution = jnp.zeros((5, 8, 128), F32)
-    for step in range(COARSE):
+    def update(alpha):
         upper = lower = jnp.zeros((8, 128), F32)
         for i in starts:
             own, padded = slice(i, i + chunk), slice(i + 2, i + chunk + 2)
             w, q = y_ref[own], q_ref[padded]
-            if step > 0:
+            if alpha is not None:
                 old = w_ref[padded]
                 w, q = old - alpha * w, q - alpha * old
                 q_ref[padded] = q
             w_ref[padded] = w
             upper = upper + jnp.sum(w * q, axis=0)
             lower = lower + jnp.sum(w * w, axis=0)
+        return upper, lower
+
+    def gain(upper, lower):
         alpha = (total(upper) / total(lower))[None]
-        if step < COARSE - 1:
-            product(w_ref)
-        solution = solution + alpha * q_ref[pl.ds(at, 5)]
+        return alpha, alpha * q_ref[pl.ds(at, 5)]
+
+    def step(_, carry):
+        solution, upper, lower = carry
+        alpha, part = gain(upper, lower)
+        product(w_ref)
+        return (solution + part, *update(alpha))
+
+    product(q_ref)
+    carry = (jnp.zeros((5, 8, 128), F32), *update(None))
+    solution, upper, lower = lax.fori_loop(0, COARSE - 1, step, carry)
+    solution = solution + gain(upper, lower)[1]
     return solution * inverse_ref[pl.ds(at, 5)]
 
 

time: 74.1 us -> 74.3 us (level)
  no operation moved by 1% of the time
where the time goes in v8:
time: 74.3 us; the launch traced here: 73.8 us
  starting transfers between devices  37.3 us (50%)
  blocking collectives  16.5 us (22%)
  waiting for transfers between devices  13.8 us (19%)
  Pallas kernels  5.27 us (7%)
  other arithmetic  0.81 us (1%)
    all_to_all x1, blocking collectives, shards(): got = lax.all_to_all(sent, ('c', 'z'), 0, 0).reshape(16 * nz, 128)  16.5 us
    all_to_all x1, starting transfers between devices, shards(): half = lax.all_to_all(sent, ('y', 'x'), 0, 0)  10.8 us
    pallas_call x6, Pallas kernels, call(): pl.pallas_call(kernel, out_shape=[jax.ShapeDtypeStruct(*(out if isinstanc...  5.27 us
    ppermute x1, starting transfers between devices, shards(): half_mate = lax.ppermute(half, 'c', swap)  5.22 us
    all_to_all x1, waiting for transfers between devices, shards(): half = lax.all_to_all(sent, ('y', 'x'), 0, 0)  4.89 us
    ppermute x1, starting transfers between devices, shards(): face = lax.ppermute(face, ('y', 'x', 'c'), facing)  4.83 us
    ppermute x1, starting transfers between devices, shards(): before = lax.ppermute(tail, 'z', up)  4.83 us
    ppermute x1, waiting for transfers between devices, shards(): after = lax.ppermute(head, 'z', down)  4.29 us
  transfers between devices with their start and end apart: 9, of which 6 were waited for; matrix products, arithmetic and copies ran while one was open for 0% of the time, Pallas kernels for 0%

profile of v8, /device:TPU:1, one launch (start us, length us, event | category | flops | bytes accessed | tf_op | source)
XLA Modules:
  0.0 73.8 jit_solution(14747328044483483858)
XLA Ops:
  0.0 0.8 %pad_maximum_fusion.own_ref = f32[3,4,16,128]{3,2,1,0:T(8,128)S(1)} fusion(f32[1,4,16,128]{3,2,1,0:T(8,128)} %bitcast.9, f32[1,4,16,128]{3,2,1,0:T(8,128)} %bitcast.10, f32[1,4,16,128]{3,2,1,0:T(8,128)} %bitcast.11), kind=kLoop, calls=%fused_computation | loop fusion | flops 49152 | bytes 196608 | tf_op jit(solution)/shard_map/stack | solution.py:393
  0.8 4.8 %collective-permute-start = (f32[120,128]{1,0:T(8,128)S(1)}, f32[120,128]{1,0:T(8,128)S(1)}, u32[]{:S(2)}, u32[]{:S(2)}) collective-permute-start(f32[120,128]{1,0:T(8,128)S(1)} %get-tuple-element.22), channel_id=1, source_target_pairs={{0,1},{1,2},{2,3},{3,4},{4,5},{5,6},{6,7},{8,9},{9,10},{10,11},{11... | collective-permute-start | bytes 184328 | tf_op jit(solution)/shard_map/ppermute | solution.py:397
  5.7 1.3 %collective-permute-start.1 = (f32[120,128]{1,0:T(8,128)S(1)}, f32[120,128]{1,0:T(8,128)S(1)}, u32[]{:S(2)}, u32[]{:S(2)}) collective-permute-start(f32[120,128]{1,0:T(8,128)S(1)} %get-tuple-element.23), channel_id=1, source_target_pairs={{1,0},{2,1},{3,2},{4,3},{5,4},{6,5},{7,6},{9,8},{10,9},{11,10},{12... | collective-permute-start | bytes 184328 | tf_op jit(solution)/shard_map/ppermute | solution.py:398
  7.0 0.0 collective-permute-done.before_ref
  7.0 4.3 %collective-permute-done.1.after_ref = f32[120,128]{1,0:T(8,128)S(1)} collective-permute-done((f32[120,128]{1,0:T(8,128)S(1)}, f32[120,128]{1,0:T(8,128)S(1)}, u32[]{:S(2)}, u32[]{:S(2)}) %collective-permute-start.1) | collective-permute-done | bytes 61472 | tf_op jit(solution)/shard_map/ppermute | solution.py:398
  11.3 4.8 %collective-permute-start.3 = (f32[344,128]{1,0:T(8,128)S(1)}, f32[344,128]{1,0:T(8,128)S(1)}, u32[]{:S(2)}, u32[]{:S(2)}) collective-permute-start(f32[344,128]{1,0:T(8,128)S(1)} %get-tuple-element.26), channel_id=1, source_target_pairs={{8,16},{16,8},{24,32},{32,24},{40,48},{48,40},{56,64},{64,56},{72,... | collective-permute-start | bytes 528392 | tf_op jit(solution)/shard_map/ppermute | solution.py:406
  16.1 1.9 %collective-permute-start.2 = (f32[336,128]{1,0:T(8,128)S(1)}, f32[336,128]{1,0:T(8,128)S(1)}, u32[]{:S(2)}, u32[]{:S(2)}) collective-permute-start(f32[336,128]{1,0:T(8,128)S(1)} %get-tuple-element.25), channel_id=1, source_target_pairs={{0,8},{8,0},{1,9},{9,1},{2,10},{10,2},{3,11},{11,3},{4,12},{12,4},... | collective-permute-start | bytes 516104 | tf_op jit(solution)/shard_map/ppermute | solution.py:407
  18.1 1.4 %collective-permute-done.2.mate_ref = f32[336,128]{1,0:T(8,128)S(1)} collective-permute-done((f32[336,128]{1,0:T(8,128)S(1)}, f32[336,128]{1,0:T(8,128)S(1)}, u32[]{:S(2)}, u32[]{:S(2)}) %collective-permute-start.2) | collective-permute-done | bytes 172064 | tf_op jit(solution)/shard_map/ppermute | solution.py:407
  19.4 0.0 collective-permute-done.3.face_ref
  19.5 1.0 %shard_map.39 = (f32[8,24,128]{2,1,0:T(8,128)S(1)}, f32[4,8,24,128]{3,2,1,0:T(8,128)S(1)}, f32[16,8,128]{2,1,0:T(8,128)S(1)}, f32[3,16,128]{2,1,0:T(8,128)S(1)}) custom-call(f32[3,4,40,128]{3,2,1,0:T(8,128)S(1)} %get-tuple-element.24.own_ref, f32[336,128]{1,0:T(8,128)S(1)} %collective-permute-done.2.mate_ref, f32[344,128]{1,0:T(8,128)S(1)} %collective-permute-done.3.face_ref), custom_call_target="tpu_custom_call" | custom-call | tf_op jit(solution)/shard_map/pallas_call | solution.py:375
  20.4 16.5 %all_to_all.10 = f32[16,8,128]{2,1,0:T(8,128)S(1)} all-to-all(f32[16,8,128]{2,1,0:T(8,128)S(1)} %get-tuple-element.28), channel_id=1, replica_groups=mesh['y'=8,'x'=4,'c'=2,'z'=8] {'c','z'}, dimensions={0} | all-to-all | bytes 131072 | tf_op jit(solution)/shard_map/all_to_all | solution.py:415
  36.9 0.9 %shard_map.40 = f32[32,32,128]{2,1,0:T(8,128)} custom-call(f32[128,128]{1,0:T(8,128)S(1)} %bitcast.8), custom_call_target="tpu_custom_call" | custom-call | tf_op jit(solution)/shard_map/pallas_call | solution.py:375
  37.8 10.8 %all-to-all-start.1 = ((f32[32,32,128]{2,1,0:T(8,128)}), f32[32,32,128]{2,1,0:T(8,128)S(1)}, u32[]{:S(2)}, u32[]{:S(2)}) async-start(f32[32,32,128]{2,1,0:T(8,128)} %shard_map.40), calls=%async_computation.1 | async-start | bytes 1048576 | tf_op jit(solution)/shard_map/all_to_all | solution.py:420
  48.6 3.1 %collective-permute-start.4 = (f32[3,16,128]{2,1,0:T(8,128)S(1)}, f32[3,16,128]{2,1,0:T(8,128)S(1)}, u32[]{:S(2)}, u32[]{:S(2)}) collective-permute-start(f32[3,16,128]{2,1,0:T(8,128)S(1)} %get-tuple-element.30.own_ref), channel_id=1, source_target_pairs={{0,8},{8,0},{1,9},{9,1},{2,10},{10,2},{3,11},{11,3},{4,12},{12,4},... | collective-permute-start | bytes 73736 | tf_op jit(solution)/shard_map/ppermute | solution.py:422
  51.7 0.8 %collective-permute-done.4.mate_ref = f32[3,16,128]{2,1,0:T(8,128)S(1)} collective-permute-done((f32[3,16,128]{2,1,0:T(8,128)S(1)}, f32[3,16,128]{2,1,0:T(8,128)S(1)}, u32[]{:S(2)}, u32[]{:S(2)}) %collective-permute-start.4) | collective-permute-done | bytes 24608 | tf_op jit(solution)/shard_map/ppermute | solution.py:422
  52.5 1.3 %collective-permute-start.5 = (f32[2,3,16,128]{3,2,1,0:T(8,128)S(1)}, f32[2,3,16,128]{3,2,1,0:T(8,128)S(1)}, u32[]{:S(2)}, u32[]{:S(2)}) collective-permute-start(f32[2,3,16,128]{3,2,1,0:T(8,128)S(1)} %pad_maximum_fusion.1), channel_id=1, source_target_pairs={{0,16},{24,8},{16,32},{40,24},{32,48},{56,40},{48,64},{72,56},{64,... | collective-permute-start | bytes 147464 | tf_op jit(solution)/shard_map/ppermute | solution.py:427
  53.8 4.0 %collective-permute-start.6 = (f32[3,16,128]{2,1,0:T(8,128)S(1)}, f32[3,16,128]{2,1,0:T(8,128)S(1)}, u32[]{:S(2)}, u32[]{:S(2)}) collective-permute-start(f32[3,16,128]{2,1,0:T(8,128)S(1)} %get-tuple-element.30.own_ref), channel_id=1, source_target_pairs={{16,0},{8,24},{32,16},{24,40},{48,32},{40,56},{64,48},{56,72},{80,... | collective-permute-start | bytes 73736 | tf_op jit(solution)/shard_map/ppermute | solution.py:428
  57.9 0.9 %collective-permute-done.6.inner_ref = f32[3,16,128]{2,1,0:T(8,128)S(1)} collective-permute-done((f32[3,16,128]{2,1,0:T(8,128)S(1)}, f32[3,16,128]{2,1,0:T(8,128)S(1)}, u32[]{:S(2)}, u32[]{:S(2)}) %collective-permute-start.6) | collective-permute-done | bytes 24608 | tf_op jit(solution)/shard_map/ppermute | solution.py:428
  58.8 0.0 collective-permute-done.5.outer_ref
  58.8 0.3 shard_map.41
  59.1 4.9 %all-to-all-done.1.got_ref = f32[32,32,128]{2,1,0:T(8,128)S(1)} async-done(((f32[32,32,128]{2,1,0:T(8,128)}), f32[32,32,128]{2,1,0:T(8,128)S(1)}, u32[]{:S(2)}, u32[]{:S(2)}) %all-to-all-start.1) | async-done | bytes 524320 | tf_op jit(solution)/shard_map/all_to_all | solution.py:420
  64.0 5.2 %collective-permute-start.7 = (f32[32,32,128]{2,1,0:T(8,128)S(1)}, f32[32,32,128]{2,1,0:T(8,128)S(1)}, u32[]{:S(2)}, u32[]{:S(2)}) collective-permute-start(f32[32,32,128]{2,1,0:T(8,128)S(1)} %all-to-all-done.1.got_ref), channel_id=1, source_target_pairs={{0,8},{8,0},{1,9},{9,1},{2,10},{10,2},{3,11},{11,3},{4,12},{12,4},... | collective-permute-start | bytes 1572872 | tf_op jit(solution)/shard_map/ppermute | solution.py:435
  69.3 1.5 %collective-permute-done.7.mate_ref = f32[32,32,128]{2,1,0:T(8,128)S(1)} collective-permute-done((f32[32,32,128]{2,1,0:T(8,128)S(1)}, f32[32,32,128]{2,1,0:T(8,128)S(1)}, u32[]{:S(2)}, u32[]{:S(2)}) %collective-permute-start.7) | collective-permute-done | bytes 524320 | tf_op jit(solution)/shard_map/ppermute | solution.py:435
  70.8 3.0 %shard_map.42 = f32[4,16,128]{2,1,0:T(8,128)} custom-call(f32[32,32,128]{2,1,0:T(8,128)S(1)} %all-to-all-done.1.got_ref, f32[32,32,128]{2,1,0:T(8,128)S(1)} %collective-permute-done.7.mate_ref, bf16[384,256]{1,0:T(8,128)(2,1)S(1)} %get-tuple-element.34.matrix_ref, f32[4,5,16,128]{3,2,1,0:T(8,128)S(1)} %get-tuple-element.35.field_ref, ...), custom_call_target="tpu_custom_call" | custom-call | tf_op jit(solution)/shard_map/pallas_call | solution.py:375
  (4 shorter events, 0.1 us)
Async XLA Ops:
  0.8 6.1 %collective-permute-start = (f32[120,128]{1,0:T(8,128)S(1)}, f32[120,128]{1,0:T(8,128)S(1)}, u32[]{:S(2)}, u32[]{:S(2)}) collective-permute-start(f32[120,128]{1,0:T(8,128)S(1)} %get-tuple-element.22), channel_id=1, source_target_pairs={{0,1},{1,2},{2,3},{3,4},{4,5},{5,6},{6,7},{8,9},{9,10},{10,11},{11... | collective-permute-start | bytes 184328 | tf_op jit(solution)/shard_map/ppermute | solution.py:397
  5.7 5.6 %collective-permute-start.1 = (f32[120,128]{1,0:T(8,128)S(1)}, f32[120,128]{1,0:T(8,128)S(1)}, u32[]{:S(2)}, u32[]{:S(2)}) collective-permute-start(f32[120,128]{1,0:T(8,128)S(1)} %get-tuple-element.23), channel_id=1, source_target_pairs={{1,0},{2,1},{3,2},{4,3},{5,4},{6,5},{7,6},{9,8},{10,9},{11,10},{12... | collective-permute-start | bytes 184328 | tf_op jit(solution)/shard_map/ppermute | solution.py:398
  11.3 8.1 %collective-permute-start.3 = (f32[344,128]{1,0:T(8,128)S(1)}, f32[344,128]{1,0:T(8,128)S(1)}, u32[]{:S(2)}, u32[]{:S(2)}) collective-permute-start(f32[344,128]{1,0:T(8,128)S(1)} %get-tuple-element.26), channel_id=1, source_target_pairs={{8,16},{16,8},{24,32},{32,24},{40,48},{48,40},{56,64},{64,56},{72,... | collective-permute-start | bytes 528392 | tf_op jit(solution)/shard_map/ppermute | solution.py:406
  16.1 3.3 %collective-permute-start.2 = (f32[336,128]{1,0:T(8,128)S(1)}, f32[336,128]{1,0:T(8,128)S(1)}, u32[]{:S(2)}, u32[]{:S(2)}) collective-permute-start(f32[336,128]{1,0:T(8,128)S(1)} %get-tuple-element.25), channel_id=1, source_target_pairs={{0,8},{8,0},{1,9},{9,1},{2,10},{10,2},{3,11},{11,3},{4,12},{12,4},... | collective-permute-start | bytes 516104 | tf_op jit(solution)/shard_map/ppermute | solution.py:407
  37.8 26.3 %all-to-all-start.1 = ((f32[32,32,128]{2,1,0:T(8,128)}), f32[32,32,128]{2,1,0:T(8,128)S(1)}, u32[]{:S(2)}, u32[]{:S(2)}) async-start(f32[32,32,128]{2,1,0:T(8,128)} %shard_map.40), calls=%async_computation.1 | async-start | bytes 1048576 | tf_op jit(solution)/shard_map/all_to_all | solution.py:420
  48.6 3.9 %collective-permute-start.4 = (f32[3,16,128]{2,1,0:T(8,128)S(1)}, f32[3,16,128]{2,1,0:T(8,128)S(1)}, u32[]{:S(2)}, u32[]{:S(2)}) collective-permute-start(f32[3,16,128]{2,1,0:T(8,128)S(1)} %get-tuple-element.30.own_ref), channel_id=1, source_target_pairs={{0,8},{8,0},{1,9},{9,1},{2,10},{10,2},{3,11},{11,3},{4,12},{12,4},... | collective-permute-start | bytes 73736 | tf_op jit(solution)/shard_map/ppermute | solution.py:422
  52.5 6.3 %collective-permute-start.5 = (f32[2,3,16,128]{3,2,1,0:T(8,128)S(1)}, f32[2,3,16,128]{3,2,1,0:T(8,128)S(1)}, u32[]{:S(2)}, u32[]{:S(2)}) collective-permute-start(f32[2,3,16,128]{3,2,1,0:T(8,128)S(1)} %pad_maximum_fusion.1), channel_id=1, source_target_pairs={{0,16},{24,8},{16,32},{40,24},{32,48},{56,40},{48,64},{72,56},{64,... | collective-permute-start | bytes 147464 | tf_op jit(solution)/shard_map/ppermute | solution.py:427
  53.8 5.0 %collective-permute-start.6 = (f32[3,16,128]{2,1,0:T(8,128)S(1)}, f32[3,16,128]{2,1,0:T(8,128)S(1)}, u32[]{:S(2)}, u32[]{:S(2)}) collective-permute-start(f32[3,16,128]{2,1,0:T(8,128)S(1)} %get-tuple-element.30.own_ref), channel_id=1, source_target_pairs={{16,0},{8,24},{32,16},{24,40},{48,32},{40,56},{64,48},{56,72},{80,... | collective-permute-start | bytes 73736 | tf_op jit(solution)/shard_map/ppermute | solution.py:428
  64.0 6.7 %collective-permute-start.7 = (f32[32,32,128]{2,1,0:T(8,128)S(1)}, f32[32,32,128]{2,1,0:T(8,128)S(1)}, u32[]{:S(2)}, u32[]{:S(2)}) collective-permute-start(f32[32,32,128]{2,1,0:T(8,128)S(1)} %all-to-all-done.1.got_ref), channel_id=1, source_target_pairs={{0,8},{8,0},{1,9},{9,1},{2,10},{10,2},{3,11},{11,3},{4,12},{12,4},... | collective-permute-start | bytes 1572872 | tf_op jit(solution)/shard_map/ppermute | solution.py:435

commit v9 on v7

--- a/solution.py
+++ b/solution.py
@@ -302,7 +302,9 @@
     planes = 2 * got_ref.shape[0]
 
     got, mate = got_ref[...], mate_ref[...]
-    halves = jnp.where(core == 0, got, mate), jnp.where(core == 0, mate, got)
+    second = jnp.where(core == 0, mate, got)
+    second = jnp.concatenate([second[i : i + 1] for i in reversed(range(planes // 2))], axis=0)
+    halves = jnp.where(core == 0, got, mate), second
 
     def part(half, k):
         return halves[half][:, 8 * k : 8 * k + 8]
@@ -407,7 +409,11 @@
         gather_kernel, [(chips, 32, 128)], got, scratch=[(16 * nz + 16, 128)]
     )
     one, sent = lax.optimization_barrier((one, sent))
-    half = lax.all_to_all(sent, ("y", "x"), 0, 0)
+    evens = list(range(0, 2 * chips, 2))
+    odds = [i + 1 for i in reversed(evens)]
+    half = lax.all_to_all(
+        sent, ("y", "x", "c"), 0, 0, axis_index_groups=[evens, odds]
+    )
 
     mate = lax.ppermute(one, "c", swap)
     pairs = jnp.stack([jnp.where(first, one, mate), jnp.where(first, mate, one)])

time: 74.1 us -> 73.1 us (0.987)
  waiting for transfers between devices: 13.8 us -> 13 us
    all_to_all x1, starting transfers between devices: 10.8 us -> 13.1 us  [shards(): lax.all_to_all(sent, ('y', 'x', 'c'), 0, 0, axis_index_groups=[evens, odds])]
    all_to_all x1, waiting for transfers between devices: 4.89 us -> 3.7 us  [shards(): lax.all_to_all(sent, ('y', 'x', 'c'), 0, 0, axis_index_groups=[evens, odds])]
    ppermute x1, starting transfers between devices: 5.22 us -> 4.04 us  [shards(): half_mate = lax.ppermute(half, 'c', swap)]
    ppermute x1, starting transfers between devices: 3.08 us -> 1.92 us  [shards(): mate = lax.ppermute(one, 'c', swap)]
where the time goes in v9:
time: 73.1 us; the launch traced here: 72.6 us
  starting transfers between devices  37.2 us (51%)
  blocking collectives  16.5 us (23%)
  waiting for transfers between devices  13 us (18%)
  Pallas kernels  5.08 us (7%)
  other arithmetic  0.81 us (1%)
    all_to_all x1, blocking collectives, shards(): got = lax.all_to_all(sent, ('c', 'z'), 0, 0).reshape(16 * nz, 128)  16.5 us
    all_to_all x1, starting transfers between devices, shards(): lax.all_to_all(sent, ('y', 'x', 'c'), 0, 0, axis_index_groups=[evens, odds])  13.1 us
    pallas_call x6, Pallas kernels, call(): pl.pallas_call(kernel, out_shape=[jax.ShapeDtypeStruct(*(out if isinstanc...  5.08 us
    ppermute x1, starting transfers between devices, shards(): face = lax.ppermute(face, ('y', 'x', 'c'), facing)  4.83 us
    ppermute x1, starting transfers between devices, shards(): before = lax.ppermute(tail, 'z', up)  4.83 us
    ppermute x1, waiting for transfers between devices, shards(): after = lax.ppermute(head, 'z', down)  4.29 us
    ppermute x1, starting transfers between devices, shards(): half_mate = lax.ppermute(half, 'c', swap)  4.04 us
    ppermute x1, starting transfers between devices, shards(): inner = lax.ppermute(one, ('y', 'x', 'c'), [(j, i) for i, j in ring])  3.99 us
  transfers between devices with their start and end apart: 9, of which 6 were waited for; matrix products, arithmetic and copies ran while one was open for 0% of the time, Pallas kernels for 0%

profile of v9, /device:TPU:1, one launch (start us, length us, event | category | flops | bytes accessed | tf_op | source)
XLA Modules:
  0.0 72.6 jit_solution(16843618780568442201)
XLA Ops:
  0.0 0.8 %pad_maximum_fusion.own_ref = f32[3,4,16,128]{3,2,1,0:T(8,128)S(1)} fusion(f32[1,4,16,128]{3,2,1,0:T(8,128)} %bitcast.9, f32[1,4,16,128]{3,2,1,0:T(8,128)} %bitcast.10, f32[1,4,16,128]{3,2,1,0:T(8,128)} %bitcast.11), kind=kLoop, calls=%fused_computation | loop fusion | flops 49152 | bytes 196608 | tf_op jit(solution)/shard_map/stack | solution.py:385
  0.8 4.8 %collective-permute-start = (f32[120,128]{1,0:T(8,128)S(1)}, f32[120,128]{1,0:T(8,128)S(1)}, u32[]{:S(2)}, u32[]{:S(2)}) collective-permute-start(f32[120,128]{1,0:T(8,128)S(1)} %get-tuple-element.22), channel_id=1, source_target_pairs={{0,1},{1,2},{2,3},{3,4},{4,5},{5,6},{6,7},{8,9},{9,10},{10,11},{11... | collective-permute-start | bytes 184328 | tf_op jit(solution)/shard_map/ppermute | solution.py:389
  5.7 1.3 %collective-permute-start.1 = (f32[120,128]{1,0:T(8,128)S(1)}, f32[120,128]{1,0:T(8,128)S(1)}, u32[]{:S(2)}, u32[]{:S(2)}) collective-permute-start(f32[120,128]{1,0:T(8,128)S(1)} %get-tuple-element.23), channel_id=1, source_target_pairs={{1,0},{2,1},{3,2},{4,3},{5,4},{6,5},{7,6},{9,8},{10,9},{11,10},{12... | collective-permute-start | bytes 184328 | tf_op jit(solution)/shard_map/ppermute | solution.py:390
  7.0 0.0 collective-permute-done.before_ref
  7.0 4.3 %collective-permute-done.1.after_ref = f32[120,128]{1,0:T(8,128)S(1)} collective-permute-done((f32[120,128]{1,0:T(8,128)S(1)}, f32[120,128]{1,0:T(8,128)S(1)}, u32[]{:S(2)}, u32[]{:S(2)}) %collective-permute-start.1) | collective-permute-done | bytes 61472 | tf_op jit(solution)/shard_map/ppermute | solution.py:390
  11.3 4.8 %collective-permute-start.3 = (f32[344,128]{1,0:T(8,128)S(1)}, f32[344,128]{1,0:T(8,128)S(1)}, u32[]{:S(2)}, u32[]{:S(2)}) collective-permute-start(f32[344,128]{1,0:T(8,128)S(1)} %get-tuple-element.26), channel_id=1, source_target_pairs={{8,16},{16,8},{24,32},{32,24},{40,48},{48,40},{56,64},{64,56},{72,... | collective-permute-start | bytes 528392 | tf_op jit(solution)/shard_map/ppermute | solution.py:398
  16.1 1.9 %collective-permute-start.2 = (f32[336,128]{1,0:T(8,128)S(1)}, f32[336,128]{1,0:T(8,128)S(1)}, u32[]{:S(2)}, u32[]{:S(2)}) collective-permute-start(f32[336,128]{1,0:T(8,128)S(1)} %get-tuple-element.25), channel_id=1, source_target_pairs={{0,8},{8,0},{1,9},{9,1},{2,10},{10,2},{3,11},{11,3},{4,12},{12,4},... | collective-permute-start | bytes 516104 | tf_op jit(solution)/shard_map/ppermute | solution.py:399
  18.1 1.4 %collective-permute-done.2.mate_ref = f32[336,128]{1,0:T(8,128)S(1)} collective-permute-done((f32[336,128]{1,0:T(8,128)S(1)}, f32[336,128]{1,0:T(8,128)S(1)}, u32[]{:S(2)}, u32[]{:S(2)}) %collective-permute-start.2) | collective-permute-done | bytes 172064 | tf_op jit(solution)/shard_map/ppermute | solution.py:399
  19.4 0.0 collective-permute-done.3.face_ref
  19.5 1.0 %shard_map.39 = (f32[8,24,128]{2,1,0:T(8,128)S(1)}, f32[4,8,24,128]{3,2,1,0:T(8,128)S(1)}, f32[16,8,128]{2,1,0:T(8,128)S(1)}, f32[3,16,128]{2,1,0:T(8,128)S(1)}) custom-call(f32[3,4,40,128]{3,2,1,0:T(8,128)S(1)} %get-tuple-element.24.own_ref, f32[336,128]{1,0:T(8,128)S(1)} %collective-permute-done.2.mate_ref, f32[344,128]{1,0:T(8,128)S(1)} %collective-permute-done.3.face_ref), custom_call_target="tpu_custom_call" | custom-call | tf_op jit(solution)/shard_map/pallas_call | solution.py:367
  20.4 16.5 %all_to_all.10 = f32[16,8,128]{2,1,0:T(8,128)S(1)} all-to-all(f32[16,8,128]{2,1,0:T(8,128)S(1)} %get-tuple-element.28), channel_id=1, replica_groups=mesh['y'=8,'x'=4,'c'=2,'z'=8] {'c','z'}, dimensions={0} | all-to-all | bytes 131072 | tf_op jit(solution)/shard_map/all_to_all | solution.py:407
  36.9 0.9 %shard_map.40 = f32[32,32,128]{2,1,0:T(8,128)} custom-call(f32[128,128]{1,0:T(8,128)S(1)} %bitcast.8), custom_call_target="tpu_custom_call" | custom-call | tf_op jit(solution)/shard_map/pallas_call | solution.py:367
  37.8 13.1 %all-to-all-start.1 = ((f32[32,32,128]{2,1,0:T(8,128)}), f32[32,32,128]{2,1,0:T(8,128)S(1)}, u32[]{:S(2)}, u32[]{:S(2)}) async-start(f32[32,32,128]{2,1,0:T(8,128)} %shard_map.40), calls=%async_computation.1 | async-start | bytes 1048576 | tf_op jit(solution)/shard_map/all_to_all | solution.py:414
  50.8 1.9 %collective-permute-start.4 = (f32[3,16,128]{2,1,0:T(8,128)S(1)}, f32[3,16,128]{2,1,0:T(8,128)S(1)}, u32[]{:S(2)}, u32[]{:S(2)}) collective-permute-start(f32[3,16,128]{2,1,0:T(8,128)S(1)} %get-tuple-element.30.own_ref), channel_id=1, source_target_pairs={{0,8},{8,0},{1,9},{9,1},{2,10},{10,2},{3,11},{11,3},{4,12},{12,4},... | collective-permute-start | bytes 73736 | tf_op jit(solution)/shard_map/ppermute | solution.py:418
  52.8 1.2 %collective-permute-done.4.mate_ref = f32[3,16,128]{2,1,0:T(8,128)S(1)} collective-permute-done((f32[3,16,128]{2,1,0:T(8,128)S(1)}, f32[3,16,128]{2,1,0:T(8,128)S(1)}, u32[]{:S(2)}, u32[]{:S(2)}) %collective-permute-start.4) | collective-permute-done | bytes 24608 | tf_op jit(solution)/shard_map/ppermute | solution.py:418
  53.9 1.3 %collective-permute-start.5 = (f32[2,3,16,128]{3,2,1,0:T(8,128)S(1)}, f32[2,3,16,128]{3,2,1,0:T(8,128)S(1)}, u32[]{:S(2)}, u32[]{:S(2)}) collective-permute-start(f32[2,3,16,128]{3,2,1,0:T(8,128)S(1)} %pad_maximum_fusion.1), channel_id=1, source_target_pairs={{0,16},{24,8},{16,32},{40,24},{32,48},{56,40},{48,64},{72,56},{64,... | collective-permute-start | bytes 147464 | tf_op jit(solution)/shard_map/ppermute | solution.py:423
  55.2 4.0 %collective-permute-start.6 = (f32[3,16,128]{2,1,0:T(8,128)S(1)}, f32[3,16,128]{2,1,0:T(8,128)S(1)}, u32[]{:S(2)}, u32[]{:S(2)}) collective-permute-start(f32[3,16,128]{2,1,0:T(8,128)S(1)} %get-tuple-element.30.own_ref), channel_id=1, source_target_pairs={{16,0},{8,24},{32,16},{24,40},{48,32},{40,56},{64,48},{56,72},{80,... | collective-permute-start | bytes 73736 | tf_op jit(solution)/shard_map/ppermute | solution.py:424
  59.2 0.9 %collective-permute-done.6.inner_ref = f32[3,16,128]{2,1,0:T(8,128)S(1)} collective-permute-done((f32[3,16,128]{2,1,0:T(8,128)S(1)}, f32[3,16,128]{2,1,0:T(8,128)S(1)}, u32[]{:S(2)}, u32[]{:S(2)}) %collective-permute-start.6) | collective-permute-done | bytes 24608 | tf_op jit(solution)/shard_map/ppermute | solution.py:424
  60.2 0.0 collective-permute-done.5.outer_ref
  60.2 0.3 shard_map.41
  60.5 3.7 %all-to-all-done.1.got_ref = f32[32,32,128]{2,1,0:T(8,128)S(1)} async-done(((f32[32,32,128]{2,1,0:T(8,128)}), f32[32,32,128]{2,1,0:T(8,128)S(1)}, u32[]{:S(2)}, u32[]{:S(2)}) %all-to-all-start.1) | async-done | bytes 524320 | tf_op jit(solution)/shard_map/all_to_all | solution.py:414
  64.2 4.0 %collective-permute-start.7 = (f32[32,32,128]{2,1,0:T(8,128)S(1)}, f32[32,32,128]{2,1,0:T(8,128)S(1)}, u32[]{:S(2)}, u32[]{:S(2)}) collective-permute-start(f32[32,32,128]{2,1,0:T(8,128)S(1)} %all-to-all-done.1.got_ref), channel_id=1, source_target_pairs={{0,8},{8,0},{1,9},{9,1},{2,10},{10,2},{3,11},{11,3},{4,12},{12,4},... | collective-permute-start | bytes 1572872 | tf_op jit(solution)/shard_map/ppermute | solution.py:431
  68.3 1.5 %collective-permute-done.7.mate_ref = f32[32,32,128]{2,1,0:T(8,128)S(1)} collective-permute-done((f32[32,32,128]{2,1,0:T(8,128)S(1)}, f32[32,32,128]{2,1,0:T(8,128)S(1)}, u32[]{:S(2)}, u32[]{:S(2)}) %collective-permute-start.7) | collective-permute-done | bytes 524320 | tf_op jit(solution)/shard_map/ppermute | solution.py:431
  69.8 2.9 %shard_map.42 = f32[4,16,128]{2,1,0:T(8,128)} custom-call(f32[32,32,128]{2,1,0:T(8,128)S(1)} %all-to-all-done.1.got_ref, f32[32,32,128]{2,1,0:T(8,128)S(1)} %collective-permute-done.7.mate_ref, bf16[384,256]{1,0:T(8,128)(2,1)S(1)} %get-tuple-element.34.matrix_ref, f32[4,5,16,128]{3,2,1,0:T(8,128)S(1)} %get-tuple-element.35.field_ref, ...), custom_call_target="tpu_custom_call" | custom-call | tf_op jit(solution)/shard_map/pallas_call | solution.py:367
  (4 shorter events, 0.1 us)
Async XLA Ops:
  0.8 6.1 %collective-permute-start = (f32[120,128]{1,0:T(8,128)S(1)}, f32[120,128]{1,0:T(8,128)S(1)}, u32[]{:S(2)}, u32[]{:S(2)}) collective-permute-start(f32[120,128]{1,0:T(8,128)S(1)} %get-tuple-element.22), channel_id=1, source_target_pairs={{0,1},{1,2},{2,3},{3,4},{4,5},{5,6},{6,7},{8,9},{9,10},{10,11},{11... | collective-permute-start | bytes 184328 | tf_op jit(solution)/shard_map/ppermute | solution.py:389
  5.7 5.6 %collective-permute-start.1 = (f32[120,128]{1,0:T(8,128)S(1)}, f32[120,128]{1,0:T(8,128)S(1)}, u32[]{:S(2)}, u32[]{:S(2)}) collective-permute-start(f32[120,128]{1,0:T(8,128)S(1)} %get-tuple-element.23), channel_id=1, source_target_pairs={{1,0},{2,1},{3,2},{4,3},{5,4},{6,5},{7,6},{9,8},{10,9},{11,10},{12... | collective-permute-start | bytes 184328 | tf_op jit(solution)/shard_map/ppermute | solution.py:390
  11.3 8.1 %collective-permute-start.3 = (f32[344,128]{1,0:T(8,128)S(1)}, f32[344,128]{1,0:T(8,128)S(1)}, u32[]{:S(2)}, u32[]{:S(2)}) collective-permute-start(f32[344,128]{1,0:T(8,128)S(1)} %get-tuple-element.26), channel_id=1, source_target_pairs={{8,16},{16,8},{24,32},{32,24},{40,48},{48,40},{56,64},{64,56},{72,... | collective-permute-start | bytes 528392 | tf_op jit(solution)/shard_map/ppermute | solution.py:398
  16.1 3.3 %collective-permute-start.2 = (f32[336,128]{1,0:T(8,128)S(1)}, f32[336,128]{1,0:T(8,128)S(1)}, u32[]{:S(2)}, u32[]{:S(2)}) collective-permute-start(f32[336,128]{1,0:T(8,128)S(1)} %get-tuple-element.25), channel_id=1, source_target_pairs={{0,8},{8,0},{1,9},{9,1},{2,10},{10,2},{3,11},{11,3},{4,12},{12,4},... | collective-permute-start | bytes 516104 | tf_op jit(solution)/shard_map/ppermute | solution.py:399
  37.8 26.5 %all-to-all-start.1 = ((f32[32,32,128]{2,1,0:T(8,128)}), f32[32,32,128]{2,1,0:T(8,128)S(1)}, u32[]{:S(2)}, u32[]{:S(2)}) async-start(f32[32,32,128]{2,1,0:T(8,128)} %shard_map.40), calls=%async_computation.1 | async-start | bytes 1048576 | tf_op jit(solution)/shard_map/all_to_all | solution.py:414
  50.8 3.1 %collective-permute-start.4 = (f32[3,16,128]{2,1,0:T(8,128)S(1)}, f32[3,16,128]{2,1,0:T(8,128)S(1)}, u32[]{:S(2)}, u32[]{:S(2)}) collective-permute-start(f32[3,16,128]{2,1,0:T(8,128)S(1)} %get-tuple-element.30.own_ref), channel_id=1, source_target_pairs={{0,8},{8,0},{1,9},{9,1},{2,10},{10,2},{3,11},{11,3},{4,12},{12,4},... | collective-permute-start | bytes 73736 | tf_op jit(solution)/shard_map/ppermute | solution.py:418
  53.9 6.2 %collective-permute-start.5 = (f32[2,3,16,128]{3,2,1,0:T(8,128)S(1)}, f32[2,3,16,128]{3,2,1,0:T(8,128)S(1)}, u32[]{:S(2)}, u32[]{:S(2)}) collective-permute-start(f32[2,3,16,128]{3,2,1,0:T(8,128)S(1)} %pad_maximum_fusion.1), channel_id=1, source_target_pairs={{0,16},{24,8},{16,32},{40,24},{32,48},{56,40},{48,64},{72,56},{64,... | collective-permute-start | bytes 147464 | tf_op jit(solution)/shard_map/ppermute | solution.py:423
  55.2 4.9 %collective-permute-start.6 = (f32[3,16,128]{2,1,0:T(8,128)S(1)}, f32[3,16,128]{2,1,0:T(8,128)S(1)}, u32[]{:S(2)}, u32[]{:S(2)}) collective-permute-start(f32[3,16,128]{2,1,0:T(8,128)S(1)} %get-tuple-element.30.own_ref), channel_id=1, source_target_pairs={{16,0},{8,24},{32,16},{24,40},{48,32},{40,56},{64,48},{56,72},{80,... | collective-permute-start | bytes 73736 | tf_op jit(solution)/shard_map/ppermute | solution.py:424
  64.2 5.6 %collective-permute-start.7 = (f32[32,32,128]{2,1,0:T(8,128)S(1)}, f32[32,32,128]{2,1,0:T(8,128)S(1)}, u32[]{:S(2)}, u32[]{:S(2)}) collective-permute-start(f32[32,32,128]{2,1,0:T(8,128)S(1)} %all-to-all-done.1.got_ref), channel_id=1, source_target_pairs={{0,8},{8,0},{1,9},{9,1},{2,10},{10,2},{3,11},{11,3},{4,12},{12,4},... | collective-permute-start | bytes 1572872 | tf_op jit(solution)/shard_map/ppermute | solution.py:431

commit v10 on v9

--- a/solution.py
+++ b/solution.py
@@ -184,7 +184,7 @@
     return ones_where(iota((4, 8, 128), 2) // 32 == iota((4, 8, 128), 0))
 
 
-def gather_kernel(got_ref, piece_ref, rows_ref):
+def gather_kernel(got_ref, piece_ref, rows_ref, block_ref, sems):
     core = lax.axis_index("c")
     half = got_ref.shape[0] // 2
     rows_ref[: 2 * half] = got_ref[...]
@@ -202,7 +202,16 @@
         ],
         axis=0,
     )
-    piece_ref[...] = jnp.broadcast_to(piece[None], piece_ref.shape)
+    block_ref[...] = jnp.broadcast_to(piece[None], block_ref.shape)
+    size = block_ref.shape[0]
+    copies = [
+        pltpu.make_async_copy(block_ref, piece_ref.at[pl.ds(size * k, size)], sems.at[k])
+        for k in range(piece_ref.shape[0] // size)
+    ]
+    for copy in copies:
+        copy.start()
+    for copy in copies:
+        copy.wait()
 
 
 def smooth_kernel(
@@ -291,6 +300,14 @@
     return solution * inverse_ref[pl.ds(at, 5)]
 
 
+def chip_order(ny, nx):
+    rows = [0]
+    while len(rows) < ny:
+        step = ny // (2 * len(rows))
+        rows = rows + [r + step for r in rows]
+    return [nx * r + x for r in rows for x in range(nx)]
+
+
 def last_kernel(
     got_ref, mate_ref, matrix_ref, field_ref, middle_ref, fine_ref, iter_ref, out_ref,
     q_ref, a_ref, d_ref, inverse_ref, w_ref, y_ref, middle_rows, fine_rows,
@@ -302,9 +319,12 @@
     planes = 2 * got_ref.shape[0]
 
     got, mate = got_ref[...], mate_ref[...]
-    second = jnp.where(core == 0, mate, got)
-    second = jnp.concatenate([second[i : i + 1] for i in reversed(range(planes // 2))], axis=0)
-    halves = jnp.where(core == 0, got, mate), second
+    order = chip_order(lax.axis_size("y"), nx)
+    place = [order.index(chip) for chip in range(len(order))]
+    halves = []
+    for half in (jnp.where(core == 0, got, mate), jnp.where(core == 0, mate, got)):
+        halves.append(jnp.concatenate([half[i : i + 1] for i in place], axis=0))
+        place = [len(order) - 1 - i for i in place]
 
     def part(half, k):
         return halves[half][:, 8 * k : 8 * k + 8]
@@ -405,11 +425,21 @@
     )
 
     got = lax.all_to_all(sent, ("c", "z"), 0, 0).reshape(16 * nz, 128)
-    (sent,) = call(
-        gather_kernel, [(chips, 32, 128)], got, scratch=[(16 * nz + 16, 128)]
-    )
+    size = 4 if chips % 4 == 0 else 1
+    sent = pl.pallas_call(
+        gather_kernel,
+        out_shape=jax.ShapeDtypeStruct((chips, 32, 128), F32),
+        in_specs=[pl.BlockSpec(memory_space=pltpu.VMEM)],
+        out_specs=pl.BlockSpec(memory_space=pl.ANY),
+        scratch_shapes=[
+            pltpu.VMEM((16 * nz + 16, 128), F32),
+            pltpu.VMEM((size, 32, 128), F32),
+            pltpu.SemaphoreType.DMA((chips // size,)),
+        ],
+        compiler_params=pltpu.CompilerParams(vmem_limit_bytes=24 * 2**20),
+    )(got)
     one, sent = lax.optimization_barrier((one, sent))
-    evens = list(range(0, 2 * chips, 2))
+    evens = [2 * chip for chip in chip_order(ny, nx)]
     odds = [i + 1 for i in reversed(evens)]
     half = lax.all_to_all(
         sent, ("y", "x", "c"), 0, 0, axis_index_groups=[evens, odds]

time: 73.1 us -> 72.7 us (level)
  starting transfers between devices: 37.2 us -> 35.9 us
    ppermute x1, starting transfers between devices: 4.04 us -> 2.74 us  [shards(): half_mate = lax.ppermute(half, 'c', swap)]
    pallas_call x0 -> x1, Pallas kernels: none -> 0.88 us  [shards(): pl.pallas_call(gather_kernel, out_shape=jax.ShapeDtypeStruct((chips, 32,...]
    pallas_call x6 -> x5, Pallas kernels: 5.08 us -> 4.22 us  [call(): pl.pallas_call(kernel, out_shape=[jax.ShapeDtypeStruct(*(out if isinstanc...]
where the time goes in v10:
time: 72.7 us; the launch traced here: 71.7 us
  starting transfers between devices  35.9 us (49%)
  blocking collectives  16.5 us (23%)
  waiting for transfers between devices  13.3 us (18%)
  Pallas kernels  5.1 us (7%)
  other arithmetic  0.81 us (1%)
    all_to_all x1, blocking collectives, shards(): got = lax.all_to_all(sent, ('c', 'z'), 0, 0).reshape(16 * nz, 128)  16.5 us
    all_to_all x1, starting transfers between devices, shards(): lax.all_to_all(sent, ('y', 'x', 'c'), 0, 0, axis_index_groups=[evens, odds])  13.1 us
    ppermute x1, starting transfers between devices, shards(): face = lax.ppermute(face, ('y', 'x', 'c'), facing)  4.83 us
    ppermute x1, starting transfers between devices, shards(): before = lax.ppermute(tail, 'z', up)  4.83 us
    ppermute x1, waiting for transfers between devices, shards(): after = lax.ppermute(head, 'z', down)  4.29 us
    pallas_call x5, Pallas kernels, call(): pl.pallas_call(kernel, out_shape=[jax.ShapeDtypeStruct(*(out if isinstanc...  4.22 us
    all_to_all x1, waiting for transfers between devices, shards(): lax.all_to_all(sent, ('y', 'x', 'c'), 0, 0, axis_index_groups=[evens, odds])  4 us
    ppermute x1, starting transfers between devices, shards(): inner = lax.ppermute(one, ('y', 'x', 'c'), [(j, i) for i, j in ring])  3.99 us
  transfers between devices with their start and end apart: 9, of which 6 were waited for; matrix products, arithmetic and copies ran while one was open for 0% of the time, Pallas kernels for 0%

profile of v10, /device:TPU:1, one launch (start us, length us, event | category | flops | bytes accessed | tf_op | source)
XLA Modules:
  0.0 71.7 jit_solution(15913259648997049779)
XLA Ops:
  0.0 0.8 %pad_maximum_fusion.own_ref = f32[3,4,16,128]{3,2,1,0:T(8,128)S(1)} fusion(f32[1,4,16,128]{3,2,1,0:T(8,128)} %bitcast.9, f32[1,4,16,128]{3,2,1,0:T(8,128)} %bitcast.10, f32[1,4,16,128]{3,2,1,0:T(8,128)} %bitcast.11), kind=kLoop, calls=%fused_computation | loop fusion | flops 49152 | bytes 196608 | tf_op jit(solution)/shard_map/stack | solution.py:405
  0.8 4.8 %collective-permute-start = (f32[120,128]{1,0:T(8,128)S(1)}, f32[120,128]{1,0:T(8,128)S(1)}, u32[]{:S(2)}, u32[]{:S(2)}) collective-permute-start(f32[120,128]{1,0:T(8,128)S(1)} %get-tuple-element.22), channel_id=1, source_target_pairs={{0,1},{1,2},{2,3},{3,4},{4,5},{5,6},{6,7},{8,9},{9,10},{10,11},{11... | collective-permute-start | bytes 184328 | tf_op jit(solution)/shard_map/ppermute | solution.py:409
  5.7 1.3 %collective-permute-start.1 = (f32[120,128]{1,0:T(8,128)S(1)}, f32[120,128]{1,0:T(8,128)S(1)}, u32[]{:S(2)}, u32[]{:S(2)}) collective-permute-start(f32[120,128]{1,0:T(8,128)S(1)} %get-tuple-element.23), channel_id=1, source_target_pairs={{1,0},{2,1},{3,2},{4,3},{5,4},{6,5},{7,6},{9,8},{10,9},{11,10},{12... | collective-permute-start | bytes 184328 | tf_op jit(solution)/shard_map/ppermute | solution.py:410
  7.0 0.0 collective-permute-done.before_ref
  7.0 4.3 %collective-permute-done.1.after_ref = f32[120,128]{1,0:T(8,128)S(1)} collective-permute-done((f32[120,128]{1,0:T(8,128)S(1)}, f32[120,128]{1,0:T(8,128)S(1)}, u32[]{:S(2)}, u32[]{:S(2)}) %collective-permute-start.1) | collective-permute-done | bytes 61472 | tf_op jit(solution)/shard_map/ppermute | solution.py:410
  11.3 4.8 %collective-permute-start.3 = (f32[344,128]{1,0:T(8,128)S(1)}, f32[344,128]{1,0:T(8,128)S(1)}, u32[]{:S(2)}, u32[]{:S(2)}) collective-permute-start(f32[344,128]{1,0:T(8,128)S(1)} %get-tuple-element.26), channel_id=1, source_target_pairs={{8,16},{16,8},{24,32},{32,24},{40,48},{48,40},{56,64},{64,56},{72,... | collective-permute-start | bytes 528392 | tf_op jit(solution)/shard_map/ppermute | solution.py:418
  16.1 1.9 %collective-permute-start.2 = (f32[336,128]{1,0:T(8,128)S(1)}, f32[336,128]{1,0:T(8,128)S(1)}, u32[]{:S(2)}, u32[]{:S(2)}) collective-permute-start(f32[336,128]{1,0:T(8,128)S(1)} %get-tuple-element.25), channel_id=1, source_target_pairs={{0,8},{8,0},{1,9},{9,1},{2,10},{10,2},{3,11},{11,3},{4,12},{12,4},... | collective-permute-start | bytes 516104 | tf_op jit(solution)/shard_map/ppermute | solution.py:419
  18.1 1.4 %collective-permute-done.2.mate_ref = f32[336,128]{1,0:T(8,128)S(1)} collective-permute-done((f32[336,128]{1,0:T(8,128)S(1)}, f32[336,128]{1,0:T(8,128)S(1)}, u32[]{:S(2)}, u32[]{:S(2)}) %collective-permute-start.2) | collective-permute-done | bytes 172064 | tf_op jit(solution)/shard_map/ppermute | solution.py:419
  19.4 0.0 collective-permute-done.3.face_ref
  19.5 1.0 %shard_map.39 = (f32[8,24,128]{2,1,0:T(8,128)S(1)}, f32[4,8,24,128]{3,2,1,0:T(8,128)S(1)}, f32[16,8,128]{2,1,0:T(8,128)S(1)}, f32[3,16,128]{2,1,0:T(8,128)S(1)}) custom-call(f32[3,4,40,128]{3,2,1,0:T(8,128)S(1)} %get-tuple-element.24.own_ref, f32[336,128]{1,0:T(8,128)S(1)} %collective-permute-done.2.mate_ref, f32[344,128]{1,0:T(8,128)S(1)} %collective-permute-done.3.face_ref), custom_call_target="tpu_custom_call" | custom-call | tf_op jit(solution)/shard_map/pallas_call | solution.py:387
  20.4 16.5 %all_to_all.10 = f32[16,8,128]{2,1,0:T(8,128)S(1)} all-to-all(f32[16,8,128]{2,1,0:T(8,128)S(1)} %get-tuple-element.28), channel_id=1, replica_groups=mesh['y'=8,'x'=4,'c'=2,'z'=8] {'c','z'}, dimensions={0} | all-to-all | bytes 131072 | tf_op jit(solution)/shard_map/all_to_all | solution.py:427
  36.9 0.9 %shard_map.40 = f32[32,32,128]{2,1,0:T(8,128)} custom-call(f32[128,128]{1,0:T(8,128)S(1)} %bitcast.8), custom_call_target="tpu_custom_call" | custom-call | tf_op jit(solution)/shard_map/pallas_call | solution.py:429
  37.8 13.1 %all-to-all-start.1 = ((f32[32,32,128]{2,1,0:T(8,128)}), f32[32,32,128]{2,1,0:T(8,128)S(1)}, u32[]{:S(2)}, u32[]{:S(2)}) async-start(f32[32,32,128]{2,1,0:T(8,128)} %shard_map.40), calls=%async_computation.1 | async-start | bytes 1048576 | tf_op jit(solution)/shard_map/all_to_all | solution.py:444
  50.9 1.9 %collective-permute-start.4 = (f32[3,16,128]{2,1,0:T(8,128)S(1)}, f32[3,16,128]{2,1,0:T(8,128)S(1)}, u32[]{:S(2)}, u32[]{:S(2)}) collective-permute-start(f32[3,16,128]{2,1,0:T(8,128)S(1)} %get-tuple-element.30.own_ref), channel_id=1, source_target_pairs={{0,8},{8,0},{1,9},{9,1},{2,10},{10,2},{3,11},{11,3},{4,12},{12,4},... | collective-permute-start | bytes 73736 | tf_op jit(solution)/shard_map/ppermute | solution.py:448
  52.8 1.2 %collective-permute-done.4.mate_ref = f32[3,16,128]{2,1,0:T(8,128)S(1)} collective-permute-done((f32[3,16,128]{2,1,0:T(8,128)S(1)}, f32[3,16,128]{2,1,0:T(8,128)S(1)}, u32[]{:S(2)}, u32[]{:S(2)}) %collective-permute-start.4) | collective-permute-done | bytes 24608 | tf_op jit(solution)/shard_map/ppermute | solution.py:448
  54.0 1.3 %collective-permute-start.5 = (f32[2,3,16,128]{3,2,1,0:T(8,128)S(1)}, f32[2,3,16,128]{3,2,1,0:T(8,128)S(1)}, u32[]{:S(2)}, u32[]{:S(2)}) collective-permute-start(f32[2,3,16,128]{3,2,1,0:T(8,128)S(1)} %pad_maximum_fusion.1), channel_id=1, source_target_pairs={{0,16},{24,8},{16,32},{40,24},{32,48},{56,40},{48,64},{72,56},{64,... | collective-permute-start | bytes 147464 | tf_op jit(solution)/shard_map/ppermute | solution.py:453
  55.3 4.0 %collective-permute-start.6 = (f32[3,16,128]{2,1,0:T(8,128)S(1)}, f32[3,16,128]{2,1,0:T(8,128)S(1)}, u32[]{:S(2)}, u32[]{:S(2)}) collective-permute-start(f32[3,16,128]{2,1,0:T(8,128)S(1)} %get-tuple-element.30.own_ref), channel_id=1, source_target_pairs={{16,0},{8,24},{32,16},{24,40},{48,32},{40,56},{64,48},{56,72},{80,... | collective-permute-start | bytes 73736 | tf_op jit(solution)/shard_map/ppermute | solution.py:454
  59.3 0.9 %collective-permute-done.6.inner_ref = f32[3,16,128]{2,1,0:T(8,128)S(1)} collective-permute-done((f32[3,16,128]{2,1,0:T(8,128)S(1)}, f32[3,16,128]{2,1,0:T(8,128)S(1)}, u32[]{:S(2)}, u32[]{:S(2)}) %collective-permute-start.6) | collective-permute-done | bytes 24608 | tf_op jit(solution)/shard_map/ppermute | solution.py:454
  60.2 0.0 collective-permute-done.5.outer_ref
  60.2 0.3 shard_map.41
  60.5 4.0 %all-to-all-done.1.got_ref = f32[32,32,128]{2,1,0:T(8,128)S(1)} async-done(((f32[32,32,128]{2,1,0:T(8,128)}), f32[32,32,128]{2,1,0:T(8,128)S(1)}, u32[]{:S(2)}, u32[]{:S(2)}) %all-to-all-start.1) | async-done | bytes 524320 | tf_op jit(solution)/shard_map/all_to_all | solution.py:444
  64.5 2.7 %collective-permute-start.7 = (f32[32,32,128]{2,1,0:T(8,128)S(1)}, f32[32,32,128]{2,1,0:T(8,128)S(1)}, u32[]{:S(2)}, u32[]{:S(2)}) collective-permute-start(f32[32,32,128]{2,1,0:T(8,128)S(1)} %all-to-all-done.1.got_ref), channel_id=1, source_target_pairs={{0,8},{8,0},{1,9},{9,1},{2,10},{10,2},{3,11},{11,3},{4,12},{12,4},... | collective-permute-start | bytes 1572872 | tf_op jit(solution)/shard_map/ppermute | solution.py:461
  67.3 1.5 %collective-permute-done.7.mate_ref = f32[32,32,128]{2,1,0:T(8,128)S(1)} collective-permute-done((f32[32,32,128]{2,1,0:T(8,128)S(1)}, f32[32,32,128]{2,1,0:T(8,128)S(1)}, u32[]{:S(2)}, u32[]{:S(2)}) %collective-permute-start.7) | collective-permute-done | bytes 524320 | tf_op jit(solution)/shard_map/ppermute | solution.py:461
  68.8 2.9 %shard_map.42 = f32[4,16,128]{2,1,0:T(8,128)} custom-call(f32[32,32,128]{2,1,0:T(8,128)S(1)} %all-to-all-done.1.got_ref, f32[32,32,128]{2,1,0:T(8,128)S(1)} %collective-permute-done.7.mate_ref, bf16[384,256]{1,0:T(8,128)(2,1)S(1)} %get-tuple-element.34.matrix_ref, f32[4,5,16,128]{3,2,1,0:T(8,128)S(1)} %get-tuple-element.35.field_ref, ...), custom_call_target="tpu_custom_call" | custom-call | tf_op jit(solution)/shard_map/pallas_call | solution.py:387
  (4 shorter events, 0.1 us)
Async XLA Ops:
  0.8 6.1 %collective-permute-start = (f32[120,128]{1,0:T(8,128)S(1)}, f32[120,128]{1,0:T(8,128)S(1)}, u32[]{:S(2)}, u32[]{:S(2)}) collective-permute-start(f32[120,128]{1,0:T(8,128)S(1)} %get-tuple-element.22), channel_id=1, source_target_pairs={{0,1},{1,2},{2,3},{3,4},{4,5},{5,6},{6,7},{8,9},{9,10},{10,11},{11... | collective-permute-start | bytes 184328 | tf_op jit(solution)/shard_map/ppermute | solution.py:409
  5.7 5.6 %collective-permute-start.1 = (f32[120,128]{1,0:T(8,128)S(1)}, f32[120,128]{1,0:T(8,128)S(1)}, u32[]{:S(2)}, u32[]{:S(2)}) collective-permute-start(f32[120,128]{1,0:T(8,128)S(1)} %get-tuple-element.23), channel_id=1, source_target_pairs={{1,0},{2,1},{3,2},{4,3},{5,4},{6,5},{7,6},{9,8},{10,9},{11,10},{12... | collective-permute-start | bytes 184328 | tf_op jit(solution)/shard_map/ppermute | solution.py:410
  11.3 8.1 %collective-permute-start.3 = (f32[344,128]{1,0:T(8,128)S(1)}, f32[344,128]{1,0:T(8,128)S(1)}, u32[]{:S(2)}, u32[]{:S(2)}) collective-permute-start(f32[344,128]{1,0:T(8,128)S(1)} %get-tuple-element.26), channel_id=1, source_target_pairs={{8,16},{16,8},{24,32},{32,24},{40,48},{48,40},{56,64},{64,56},{72,... | collective-permute-start | bytes 528392 | tf_op jit(solution)/shard_map/ppermute | solution.py:418
  16.1 3.3 %collective-permute-start.2 = (f32[336,128]{1,0:T(8,128)S(1)}, f32[336,128]{1,0:T(8,128)S(1)}, u32[]{:S(2)}, u32[]{:S(2)}) collective-permute-start(f32[336,128]{1,0:T(8,128)S(1)} %get-tuple-element.25), channel_id=1, source_target_pairs={{0,8},{8,0},{1,9},{9,1},{2,10},{10,2},{3,11},{11,3},{4,12},{12,4},... | collective-permute-start | bytes 516104 | tf_op jit(solution)/shard_map/ppermute | solution.py:419
  37.8 26.8 %all-to-all-start.1 = ((f32[32,32,128]{2,1,0:T(8,128)}), f32[32,32,128]{2,1,0:T(8,128)S(1)}, u32[]{:S(2)}, u32[]{:S(2)}) async-start(f32[32,32,128]{2,1,0:T(8,128)} %shard_map.40), calls=%async_computation.1 | async-start | bytes 1048576 | tf_op jit(solution)/shard_map/all_to_all | solution.py:444
  50.9 3.1 %collective-permute-start.4 = (f32[3,16,128]{2,1,0:T(8,128)S(1)}, f32[3,16,128]{2,1,0:T(8,128)S(1)}, u32[]{:S(2)}, u32[]{:S(2)}) collective-permute-start(f32[3,16,128]{2,1,0:T(8,128)S(1)} %get-tuple-element.30.own_ref), channel_id=1, source_target_pairs={{0,8},{8,0},{1,9},{9,1},{2,10},{10,2},{3,11},{11,3},{4,12},{12,4},... | collective-permute-start | bytes 73736 | tf_op jit(solution)/shard_map/ppermute | solution.py:448
  54.0 6.2 %collective-permute-start.5 = (f32[2,3,16,128]{3,2,1,0:T(8,128)S(1)}, f32[2,3,16,128]{3,2,1,0:T(8,128)S(1)}, u32[]{:S(2)}, u32[]{:S(2)}) collective-permute-start(f32[2,3,16,128]{3,2,1,0:T(8,128)S(1)} %pad_maximum_fusion.1), channel_id=1, source_target_pairs={{0,16},{24,8},{16,32},{40,24},{32,48},{56,40},{48,64},{72,56},{64,... | collective-permute-start | bytes 147464 | tf_op jit(solution)/shard_map/ppermute | solution.py:453
  55.3 4.9 %collective-permute-start.6 = (f32[3,16,128]{2,1,0:T(8,128)S(1)}, f32[3,16,128]{2,1,0:T(8,128)S(1)}, u32[]{:S(2)}, u32[]{:S(2)}) collective-permute-start(f32[3,16,128]{2,1,0:T(8,128)S(1)} %get-tuple-element.30.own_ref), channel_id=1, source_target_pairs={{16,0},{8,24},{32,16},{24,40},{48,32},{40,56},{64,48},{56,72},{80,... | collective-permute-start | bytes 73736 | tf_op jit(solution)/shard_map/ppermute | solution.py:454
  64.5 4.3 %collective-permute-start.7 = (f32[32,32,128]{2,1,0:T(8,128)S(1)}, f32[32,32,128]{2,1,0:T(8,128)S(1)}, u32[]{:S(2)}, u32[]{:S(2)}) collective-permute-start(f32[32,32,128]{2,1,0:T(8,128)S(1)} %all-to-all-done.1.got_ref), channel_id=1, source_target_pairs={{0,8},{8,0},{1,9},{9,1},{2,10},{10,2},{3,11},{11,3},{4,12},{12,4},... | collective-permute-start | bytes 1572872 | tf_op jit(solution)/shard_map/ppermute | solution.py:461

commit v11 on v10

--- a/solution.py
+++ b/solution.py
@@ -274,10 +274,9 @@
         inverse_ref[padded] = 1.0 / (d_ref[own] - a_ref[own])
 
     def product(ref):
-        for i in starts:
-            own, wide = slice(i, i + chunk), slice(i + 1, i + chunk + 3)
-            z = ref[wide] * inverse_ref[wide]
-            y_ref[own] = d_ref[own] * z[1:-1] - a_ref[own] * coarse_box(z, matrix)
+        wide = slice(1, planes + 3)
+        z = ref[wide] * inverse_ref[wide]
+        y_ref[...] = d_ref[...] * z[1:-1] - a_ref[...] * coarse_box(z, matrix)
 
     product(q_ref)
     solution = jnp.zeros((5, 8, 128), F32)
@@ -452,13 +451,13 @@
         ring += [(2 * i, 2 * i + 2), (2 * i + 3, 2 * i + 1)]
     outer = lax.ppermute(pairs, ("y", "x", "c"), ring)
     inner = lax.ppermute(one, ("y", "x", "c"), [(j, i) for i, j in ring])
+    half, outer, inner = lax.optimization_barrier((half, outer, inner))
+    half_mate = lax.ppermute(half, "c", swap)
     fields, middle_iter, matrix = call(
         smooth_kernel,
         [(4, 5, 16, 128), (5, 16, 128), ((384, 256), jnp.bfloat16)],
         one, mate, outer, inner,
     )
-    half, fields, middle_iter = lax.optimization_barrier((half, fields, middle_iter))
-    half_mate = lax.ppermute(half, "c", swap)
     (result,) = call(
         last_kernel, [source.shape],
         half, half_mate, matrix, fields, middle_iter, fine_fields, fine_iter,

time: 72.7 us -> 72.5 us (level)
  no operation moved by 1% of the time
where the time goes in v11:
time: 72.5 us; the launch traced here: 71.8 us
  starting transfers between devices  35.9 us (50%)
  blocking collectives  16.5 us (23%)
  waiting for transfers between devices  13.3 us (18%)
  Pallas kernels  5.21 us (7%)
  other arithmetic  0.81 us (1%)
    all_to_all x1, blocking collectives, shards(): got = lax.all_to_all(sent, ('c', 'z'), 0, 0).reshape(16 * nz, 128)  16.5 us
    all_to_all x1, starting transfers between devices, shards(): lax.all_to_all(sent, ('y', 'x', 'c'), 0, 0, axis_index_groups=[evens, odds])  13.1 us
    ppermute x1, starting transfers between devices, shards(): face = lax.ppermute(face, ('y', 'x', 'c'), facing)  4.83 us
    ppermute x1, starting transfers between devices, shards(): before = lax.ppermute(tail, 'z', up)  4.83 us
    pallas_call x5, Pallas kernels, call(): pl.pallas_call(kernel, out_shape=[jax.ShapeDtypeStruct(*(out if isinstanc...  4.33 us
    all_to_all x1, waiting for transfers between devices, shards(): lax.all_to_all(sent, ('y', 'x', 'c'), 0, 0, axis_index_groups=[evens, odds])  4.33 us
    ppermute x1, waiting for transfers between devices, shards(): after = lax.ppermute(head, 'z', down)  4.29 us
    ppermute x1, starting transfers between devices, shards(): inner = lax.ppermute(one, ('y', 'x', 'c'), [(j, i) for i, j in ring])  3.99 us
  transfers between devices with their start and end apart: 9, of which 6 were waited for; matrix products, arithmetic and copies ran while one was open for 0% of the time, Pallas kernels for 0%

profile of v11, /device:TPU:1, one launch (start us, length us, event | category | flops | bytes accessed | tf_op | source)
XLA Modules:
  0.0 71.8 jit_solution(2647420162026460152)
XLA Ops:
  0.0 0.8 %pad_maximum_fusion.own_ref = f32[3,4,16,128]{3,2,1,0:T(8,128)S(1)} fusion(f32[1,4,16,128]{3,2,1,0:T(8,128)} %bitcast.9, f32[1,4,16,128]{3,2,1,0:T(8,128)} %bitcast.10, f32[1,4,16,128]{3,2,1,0:T(8,128)} %bitcast.11), kind=kLoop, calls=%fused_computation | loop fusion | flops 49152 | bytes 196608 | tf_op jit(solution)/shard_map/stack | solution.py:404
  0.8 4.8 %collective-permute-start = (f32[120,128]{1,0:T(8,128)S(1)}, f32[120,128]{1,0:T(8,128)S(1)}, u32[]{:S(2)}, u32[]{:S(2)}) collective-permute-start(f32[120,128]{1,0:T(8,128)S(1)} %get-tuple-element.22), channel_id=1, source_target_pairs={{0,1},{1,2},{2,3},{3,4},{4,5},{5,6},{6,7},{8,9},{9,10},{10,11},{11... | collective-permute-start | bytes 184328 | tf_op jit(solution)/shard_map/ppermute | solution.py:408
  5.7 1.3 %collective-permute-start.1 = (f32[120,128]{1,0:T(8,128)S(1)}, f32[120,128]{1,0:T(8,128)S(1)}, u32[]{:S(2)}, u32[]{:S(2)}) collective-permute-start(f32[120,128]{1,0:T(8,128)S(1)} %get-tuple-element.23), channel_id=1, source_target_pairs={{1,0},{2,1},{3,2},{4,3},{5,4},{6,5},{7,6},{9,8},{10,9},{11,10},{12... | collective-permute-start | bytes 184328 | tf_op jit(solution)/shard_map/ppermute | solution.py:409
  7.0 0.0 collective-permute-done.before_ref
  7.0 4.3 %collective-permute-done.1.after_ref = f32[120,128]{1,0:T(8,128)S(1)} collective-permute-done((f32[120,128]{1,0:T(8,128)S(1)}, f32[120,128]{1,0:T(8,128)S(1)}, u32[]{:S(2)}, u32[]{:S(2)}) %collective-permute-start.1) | collective-permute-done | bytes 61472 | tf_op jit(solution)/shard_map/ppermute | solution.py:409
  11.3 4.8 %collective-permute-start.3 = (f32[344,128]{1,0:T(8,128)S(1)}, f32[344,128]{1,0:T(8,128)S(1)}, u32[]{:S(2)}, u32[]{:S(2)}) collective-permute-start(f32[344,128]{1,0:T(8,128)S(1)} %get-tuple-element.26), channel_id=1, source_target_pairs={{8,16},{16,8},{24,32},{32,24},{40,48},{48,40},{56,64},{64,56},{72,... | collective-permute-start | bytes 528392 | tf_op jit(solution)/shard_map/ppermute | solution.py:417
  16.1 1.9 %collective-permute-start.2 = (f32[336,128]{1,0:T(8,128)S(1)}, f32[336,128]{1,0:T(8,128)S(1)}, u32[]{:S(2)}, u32[]{:S(2)}) collective-permute-start(f32[336,128]{1,0:T(8,128)S(1)} %get-tuple-element.25), channel_id=1, source_target_pairs={{0,8},{8,0},{1,9},{9,1},{2,10},{10,2},{3,11},{11,3},{4,12},{12,4},... | collective-permute-start | bytes 516104 | tf_op jit(solution)/shard_map/ppermute | solution.py:418
  18.1 1.4 %collective-permute-done.2.mate_ref = f32[336,128]{1,0:T(8,128)S(1)} collective-permute-done((f32[336,128]{1,0:T(8,128)S(1)}, f32[336,128]{1,0:T(8,128)S(1)}, u32[]{:S(2)}, u32[]{:S(2)}) %collective-permute-start.2) | collective-permute-done | bytes 172064 | tf_op jit(solution)/shard_map/ppermute | solution.py:418
  19.4 0.0 collective-permute-done.3.face_ref
  19.5 1.0 %shard_map.39 = (f32[8,24,128]{2,1,0:T(8,128)S(1)}, f32[4,8,24,128]{3,2,1,0:T(8,128)S(1)}, f32[16,8,128]{2,1,0:T(8,128)S(1)}, f32[3,16,128]{2,1,0:T(8,128)S(1)}) custom-call(f32[3,4,40,128]{3,2,1,0:T(8,128)S(1)} %get-tuple-element.24.own_ref, f32[336,128]{1,0:T(8,128)S(1)} %collective-permute-done.2.mate_ref, f32[344,128]{1,0:T(8,128)S(1)} %collective-permute-done.3.face_ref), custom_call_target="tpu_custom_call" | custom-call | tf_op jit(solution)/shard_map/pallas_call | solution.py:386
  20.4 16.5 %all_to_all.10 = f32[16,8,128]{2,1,0:T(8,128)S(1)} all-to-all(f32[16,8,128]{2,1,0:T(8,128)S(1)} %get-tuple-element.28), channel_id=1, replica_groups=mesh['y'=8,'x'=4,'c'=2,'z'=8] {'c','z'}, dimensions={0} | all-to-all | bytes 131072 | tf_op jit(solution)/shard_map/all_to_all | solution.py:426
  36.9 0.9 %shard_map.40 = f32[32,32,128]{2,1,0:T(8,128)} custom-call(f32[128,128]{1,0:T(8,128)S(1)} %bitcast.8), custom_call_target="tpu_custom_call" | custom-call | tf_op jit(solution)/shard_map/pallas_call | solution.py:428
  37.8 13.1 %all-to-all-start.1 = ((f32[32,32,128]{2,1,0:T(8,128)}), f32[32,32,128]{2,1,0:T(8,128)S(1)}, u32[]{:S(2)}, u32[]{:S(2)}) async-start(f32[32,32,128]{2,1,0:T(8,128)} %shard_map.40), calls=%async_computation.1 | async-start | bytes 1048576 | tf_op jit(solution)/shard_map/all_to_all | solution.py:443
  50.9 1.9 %collective-permute-start.4 = (f32[3,16,128]{2,1,0:T(8,128)S(1)}, f32[3,16,128]{2,1,0:T(8,128)S(1)}, u32[]{:S(2)}, u32[]{:S(2)}) collective-permute-start(f32[3,16,128]{2,1,0:T(8,128)S(1)} %get-tuple-element.30.own_ref), channel_id=1, source_target_pairs={{0,8},{8,0},{1,9},{9,1},{2,10},{10,2},{3,11},{11,3},{4,12},{12,4},... | collective-permute-start | bytes 73736 | tf_op jit(solution)/shard_map/ppermute | solution.py:447
  52.8 1.2 %collective-permute-done.4.mate_ref = f32[3,16,128]{2,1,0:T(8,128)S(1)} collective-permute-done((f32[3,16,128]{2,1,0:T(8,128)S(1)}, f32[3,16,128]{2,1,0:T(8,128)S(1)}, u32[]{:S(2)}, u32[]{:S(2)}) %collective-permute-start.4) | collective-permute-done | bytes 24608 | tf_op jit(solution)/shard_map/ppermute | solution.py:447
  54.0 1.3 %collective-permute-start.5 = (f32[2,3,16,128]{3,2,1,0:T(8,128)S(1)}, f32[2,3,16,128]{3,2,1,0:T(8,128)S(1)}, u32[]{:S(2)}, u32[]{:S(2)}) collective-permute-start(f32[2,3,16,128]{3,2,1,0:T(8,128)S(1)} %pad_maximum_fusion.1), channel_id=1, source_target_pairs={{0,16},{24,8},{16,32},{40,24},{32,48},{56,40},{48,64},{72,56},{64,... | collective-permute-start | bytes 147464 | tf_op jit(solution)/shard_map/ppermute | solution.py:452
  55.3 4.0 %collective-permute-start.6 = (f32[3,16,128]{2,1,0:T(8,128)S(1)}, f32[3,16,128]{2,1,0:T(8,128)S(1)}, u32[]{:S(2)}, u32[]{:S(2)}) collective-permute-start(f32[3,16,128]{2,1,0:T(8,128)S(1)} %get-tuple-element.30.own_ref), channel_id=1, source_target_pairs={{16,0},{8,24},{32,16},{24,40},{48,32},{40,56},{64,48},{56,72},{80,... | collective-permute-start | bytes 73736 | tf_op jit(solution)/shard_map/ppermute | solution.py:453
  59.3 0.9 %collective-permute-done.6.inner_ref = f32[3,16,128]{2,1,0:T(8,128)S(1)} collective-permute-done((f32[3,16,128]{2,1,0:T(8,128)S(1)}, f32[3,16,128]{2,1,0:T(8,128)S(1)}, u32[]{:S(2)}, u32[]{:S(2)}) %collective-permute-start.6) | collective-permute-done | bytes 24608 | tf_op jit(solution)/shard_map/ppermute | solution.py:453
  60.2 0.0 collective-permute-done.5.outer_ref
  60.2 4.3 %all-to-all-done.1.got_ref = f32[32,32,128]{2,1,0:T(8,128)S(1)} async-done(((f32[32,32,128]{2,1,0:T(8,128)}), f32[32,32,128]{2,1,0:T(8,128)S(1)}, u32[]{:S(2)}, u32[]{:S(2)}) %all-to-all-start.1) | async-done | bytes 524320 | tf_op jit(solution)/shard_map/all_to_all | solution.py:443
  64.5 2.7 %collective-permute-start.7 = (f32[32,32,128]{2,1,0:T(8,128)S(1)}, f32[32,32,128]{2,1,0:T(8,128)S(1)}, u32[]{:S(2)}, u32[]{:S(2)}) collective-permute-start(f32[32,32,128]{2,1,0:T(8,128)S(1)} %all-to-all-done.1.got_ref), channel_id=1, source_target_pairs={{0,8},{8,0},{1,9},{9,1},{2,10},{10,2},{3,11},{11,3},{4,12},{12,4},... | collective-permute-start | bytes 1572872 | tf_op jit(solution)/shard_map/ppermute | solution.py:455
  67.3 0.3 shard_map.41
  67.6 1.2 %collective-permute-done.7.mate_ref = f32[32,32,128]{2,1,0:T(8,128)S(1)} collective-permute-done((f32[32,32,128]{2,1,0:T(8,128)S(1)}, f32[32,32,128]{2,1,0:T(8,128)S(1)}, u32[]{:S(2)}, u32[]{:S(2)}) %collective-permute-start.7) | collective-permute-done | bytes 524320 | tf_op jit(solution)/shard_map/ppermute | solution.py:455
  68.8 3.0 %shard_map.42 = f32[4,16,128]{2,1,0:T(8,128)} custom-call(f32[32,32,128]{2,1,0:T(8,128)S(1)} %all-to-all-done.1.got_ref, f32[32,32,128]{2,1,0:T(8,128)S(1)} %collective-permute-done.7.mate_ref, bf16[384,256]{1,0:T(8,128)(2,1)S(1)} %get-tuple-element.34.matrix_ref, f32[4,5,16,128]{3,2,1,0:T(8,128)S(1)} %get-tuple-element.35.field_ref, ...), custom_call_target="tpu_custom_call" | custom-call | tf_op jit(solution)/shard_map/pallas_call | solution.py:386
  (4 shorter events, 0.1 us)
Async XLA Ops:
  0.8 6.1 %collective-permute-start = (f32[120,128]{1,0:T(8,128)S(1)}, f32[120,128]{1,0:T(8,128)S(1)}, u32[]{:S(2)}, u32[]{:S(2)}) collective-permute-start(f32[120,128]{1,0:T(8,128)S(1)} %get-tuple-element.22), channel_id=1, source_target_pairs={{0,1},{1,2},{2,3},{3,4},{4,5},{5,6},{6,7},{8,9},{9,10},{10,11},{11... | collective-permute-start | bytes 184328 | tf_op jit(solution)/shard_map/ppermute | solution.py:408
  5.7 5.6 %collective-permute-start.1 = (f32[120,128]{1,0:T(8,128)S(1)}, f32[120,128]{1,0:T(8,128)S(1)}, u32[]{:S(2)}, u32[]{:S(2)}) collective-permute-start(f32[120,128]{1,0:T(8,128)S(1)} %get-tuple-element.23), channel_id=1, source_target_pairs={{1,0},{2,1},{3,2},{4,3},{5,4},{6,5},{7,6},{9,8},{10,9},{11,10},{12... | collective-permute-start | bytes 184328 | tf_op jit(solution)/shard_map/ppermute | solution.py:409
  11.3 8.1 %collective-permute-start.3 = (f32[344,128]{1,0:T(8,128)S(1)}, f32[344,128]{1,0:T(8,128)S(1)}, u32[]{:S(2)}, u32[]{:S(2)}) collective-permute-start(f32[344,128]{1,0:T(8,128)S(1)} %get-tuple-element.26), channel_id=1, source_target_pairs={{8,16},{16,8},{24,32},{32,24},{40,48},{48,40},{56,64},{64,56},{72,... | collective-permute-start | bytes 528392 | tf_op jit(solution)/shard_map/ppermute | solution.py:417
  16.1 3.3 %collective-permute-start.2 = (f32[336,128]{1,0:T(8,128)S(1)}, f32[336,128]{1,0:T(8,128)S(1)}, u32[]{:S(2)}, u32[]{:S(2)}) collective-permute-start(f32[336,128]{1,0:T(8,128)S(1)} %get-tuple-element.25), channel_id=1, source_target_pairs={{0,8},{8,0},{1,9},{9,1},{2,10},{10,2},{3,11},{11,3},{4,12},{12,4},... | collective-permute-start | bytes 516104 | tf_op jit(solution)/shard_map/ppermute | solution.py:418
  37.8 26.8 %all-to-all-start.1 = ((f32[32,32,128]{2,1,0:T(8,128)}), f32[32,32,128]{2,1,0:T(8,128)S(1)}, u32[]{:S(2)}, u32[]{:S(2)}) async-start(f32[32,32,128]{2,1,0:T(8,128)} %shard_map.40), calls=%async_computation.1 | async-start | bytes 1048576 | tf_op jit(solution)/shard_map/all_to_all | solution.py:443
  50.9 3.1 %collective-permute-start.4 = (f32[3,16,128]{2,1,0:T(8,128)S(1)}, f32[3,16,128]{2,1,0:T(8,128)S(1)}, u32[]{:S(2)}, u32[]{:S(2)}) collective-permute-start(f32[3,16,128]{2,1,0:T(8,128)S(1)} %get-tuple-element.30.own_ref), channel_id=1, source_target_pairs={{0,8},{8,0},{1,9},{9,1},{2,10},{10,2},{3,11},{11,3},{4,12},{12,4},... | collective-permute-start | bytes 73736 | tf_op jit(solution)/shard_map/ppermute | solution.py:447
  54.0 6.2 %collective-permute-start.5 = (f32[2,3,16,128]{3,2,1,0:T(8,128)S(1)}, f32[2,3,16,128]{3,2,1,0:T(8,128)S(1)}, u32[]{:S(2)}, u32[]{:S(2)}) collective-permute-start(f32[2,3,16,128]{3,2,1,0:T(8,128)S(1)} %pad_maximum_fusion.1), channel_id=1, source_target_pairs={{0,16},{24,8},{16,32},{40,24},{32,48},{56,40},{48,64},{72,56},{64,... | collective-permute-start | bytes 147464 | tf_op jit(solution)/shard_map/ppermute | solution.py:452
  55.3 4.9 %collective-permute-start.6 = (f32[3,16,128]{2,1,0:T(8,128)S(1)}, f32[3,16,128]{2,1,0:T(8,128)S(1)}, u32[]{:S(2)}, u32[]{:S(2)}) collective-permute-start(f32[3,16,128]{2,1,0:T(8,128)S(1)} %get-tuple-element.30.own_ref), channel_id=1, source_target_pairs={{16,0},{8,24},{32,16},{24,40},{48,32},{40,56},{64,48},{56,72},{80,... | collective-permute-start | bytes 73736 | tf_op jit(solution)/shard_map/ppermute | solution.py:453
  64.5 4.3 %collective-permute-start.7 = (f32[32,32,128]{2,1,0:T(8,128)S(1)}, f32[32,32,128]{2,1,0:T(8,128)S(1)}, u32[]{:S(2)}, u32[]{:S(2)}) collective-permute-start(f32[32,32,128]{2,1,0:T(8,128)S(1)} %all-to-all-done.1.got_ref), channel_id=1, source_target_pairs={{0,8},{8,0},{1,9},{9,1},{2,10},{10,2},{3,11},{11,3},{4,12},{12,4},... | collective-permute-start | bytes 1572872 | tf_op jit(solution)/shard_map/ppermute | solution.py:455

commit v12 on v11

--- a/solution.py
+++ b/solution.py
@@ -215,7 +215,7 @@
 
 
 def smooth_kernel(
-    own_ref, mate_ref, outer_ref, inner_ref, field_ref, iter_ref, matrix_ref
+    own_ref, mate_ref, outer_ref, inner_ref, field_ref, iter_ref, matrix_ref, spread_ref, fine_ref
 ):
     left = lax.axis_index("c") == 0
     for k in range(3):
@@ -231,6 +231,10 @@
     v = w * f
     iter_ref[...] = v + w * (f - middle_apply(v, a, s))
     matrix_ref[...] = box_matrix()
+    lane, out = iota((128, 128), 0), iota((128, 128), 1)
+    spread_ref[...] = ones_where(lane % 32 == (out % 64) // 2).astype(jnp.bfloat16)
+    lane, out = iota((128, 256), 0), iota((128, 256), 1)
+    fine_ref[...] = ones_where(lane == out // 2).astype(jnp.bfloat16)
 
 
 def box_matrix():
@@ -273,10 +277,13 @@
         own, padded = slice(i, i + chunk), slice(i + 2, i + chunk + 2)
         inverse_ref[padded] = 1.0 / (d_ref[own] - a_ref[own])
 
+    span = 8 if planes % 8 == 0 else 2
+
     def product(ref):
-        wide = slice(1, planes + 3)
-        z = ref[wide] * inverse_ref[wide]
-        y_ref[...] = d_ref[...] * z[1:-1] - a_ref[...] * coarse_box(z, matrix)
+        for i in range(0, planes, span):
+            own, wide = slice(i, i + span), slice(i + 1, i + span + 3)
+            z = ref[wide] * inverse_ref[wide]
+            y_ref[own] = d_ref[own] * z[1:-1] - a_ref[own] * coarse_box(z, matrix)
 
     product(q_ref)
     solution = jnp.zeros((5, 8, 128), F32)
@@ -308,7 +315,7 @@
 
 
 def last_kernel(
-    got_ref, mate_ref, matrix_ref, field_ref, middle_ref, fine_ref, iter_ref, out_ref,
+    got_ref, mate_ref, matrix_ref, spread_ref, double_ref, field_ref, middle_ref, fine_ref, iter_ref, out_ref,
     q_ref, a_ref, d_ref, inverse_ref, w_ref, y_ref, middle_rows, fine_rows,
 ):
     nx = lax.axis_size("x")
@@ -345,8 +352,7 @@
 
     mask = quarter_mask()
     stack = jnp.concatenate([(near[p][None] * mask).reshape(32, 128) for p in range(5)], axis=0)
-    spread = ones_where(iota((128, 128), 0) % 32 == (iota((128, 128), 1) % 64) // 2)
-    mixed = dot(stack, spread)
+    mixed = dot(stack, spread_ref[...])
     size = (middle_rows.shape[0] - 16) // 5
     edge = jnp.zeros((4, 128), F32)
     window = []
@@ -364,8 +370,7 @@
     for _ in range(2):
         v = v + w * (f - middle_apply(v, a, s))
 
-    lane, out = iota((128, 256), 0), iota((128, 256), 1)
-    mixed = dot(v[1:4].reshape(48, 128), ones_where(lane == out // 2))
+    mixed = dot(v[1:4].reshape(48, 128), double_ref[...])
     halves = [mixed[:16, 128:], mixed[16:32, :128], mixed[16:32, 128:], mixed[32:, :128]]
     refined = []
     for p, t in enumerate(halves):
@@ -453,14 +458,15 @@
     inner = lax.ppermute(one, ("y", "x", "c"), [(j, i) for i, j in ring])
     half, outer, inner = lax.optimization_barrier((half, outer, inner))
     half_mate = lax.ppermute(half, "c", swap)
-    fields, middle_iter, matrix = call(
+    fields, middle_iter, *matrices = call(
         smooth_kernel,
-        [(4, 5, 16, 128), (5, 16, 128), ((384, 256), jnp.bfloat16)],
+        [(4, 5, 16, 128), (5, 16, 128)]
+        + [(shape, jnp.bfloat16) for shape in ((384, 256), (128, 128), (128, 256))],
         one, mate, outer, inner,
     )
     (result,) = call(
         last_kernel, [source.shape],
-        half, half_mate, matrix, fields, middle_iter, fine_fields, fine_iter,
+        half, half_mate, *matrices, fields, middle_iter, fine_fields, fine_iter,
         scratch=[(2 * chips + 4, 8, 128)] + [(2 * chips, 8, 128)] * 2
         + [(2 * chips + 4, 8, 128)] * 2 + [(2 * chips, 8, 128)]
         + [(5 * (8 * nz + 8) + 16, 128), (4 * 24 + 16, 128)],

time: 72.5 us -> 72.7 us (level)
  no operation moved by 1% of the time
where the time goes in v12:
time: 72.7 us; the launch traced here: 72 us
  starting transfers between devices  35.9 us (49%)
  blocking collectives  16.5 us (23%)
  waiting for transfers between devices  13.3 us (18%)
  Pallas kernels  5.45 us (7%)
  other arithmetic  0.81 us (1%)
    all_to_all x1, blocking collectives, shards(): got = lax.all_to_all(sent, ('c', 'z'), 0, 0).reshape(16 * nz, 128)  16.5 us
    all_to_all x1, starting transfers between devices, shards(): lax.all_to_all(sent, ('y', 'x', 'c'), 0, 0, axis_index_groups=[evens, odds])  13.1 us
    ppermute x1, starting transfers between devices, shards(): face = lax.ppermute(face, ('y', 'x', 'c'), facing)  4.83 us
    ppermute x1, starting transfers between devices, shards(): before = lax.ppermute(tail, 'z', up)  4.83 us
    pallas_call x5, Pallas kernels, call(): pl.pallas_call(kernel, out_shape=[jax.ShapeDtypeStruct(*(out if isinstanc...  4.57 us
    all_to_all x1, waiting for transfers between devices, shards(): lax.all_to_all(sent, ('y', 'x', 'c'), 0, 0, axis_index_groups=[evens, odds])  4.33 us
    ppermute x1, waiting for transfers between devices, shards(): after = lax.ppermute(head, 'z', down)  4.29 us
    ppermute x1, starting transfers between devices, shards(): inner = lax.ppermute(one, ('y', 'x', 'c'), [(j, i) for i, j in ring])  3.99 us
  transfers between devices with their start and end apart: 9, of which 6 were waited for; matrix products, arithmetic and copies ran while one was open for 0% of the time, Pallas kernels for 0%

profile of v12, /device:TPU:1, one launch (start us, length us, event | category | flops | bytes accessed | tf_op | source)
XLA Modules:
  0.0 72.0 jit_solution(14494257895969016967)
XLA Ops:
  0.0 0.8 %pad_maximum_fusion.own_ref = f32[3,4,16,128]{3,2,1,0:T(8,128)S(1)} fusion(f32[1,4,16,128]{3,2,1,0:T(8,128)} %bitcast.9, f32[1,4,16,128]{3,2,1,0:T(8,128)} %bitcast.10, f32[1,4,16,128]{3,2,1,0:T(8,128)} %bitcast.11), kind=kLoop, calls=%fused_computation | loop fusion | flops 49152 | bytes 196608 | tf_op jit(solution)/shard_map/stack | solution.py:409
  0.8 4.8 %collective-permute-start = (f32[120,128]{1,0:T(8,128)S(1)}, f32[120,128]{1,0:T(8,128)S(1)}, u32[]{:S(2)}, u32[]{:S(2)}) collective-permute-start(f32[120,128]{1,0:T(8,128)S(1)} %get-tuple-element.24), channel_id=1, source_target_pairs={{0,1},{1,2},{2,3},{3,4},{4,5},{5,6},{6,7},{8,9},{9,10},{10,11},{11... | collective-permute-start | bytes 184328 | tf_op jit(solution)/shard_map/ppermute | solution.py:413
  5.7 1.3 %collective-permute-start.1 = (f32[120,128]{1,0:T(8,128)S(1)}, f32[120,128]{1,0:T(8,128)S(1)}, u32[]{:S(2)}, u32[]{:S(2)}) collective-permute-start(f32[120,128]{1,0:T(8,128)S(1)} %get-tuple-element.25), channel_id=1, source_target_pairs={{1,0},{2,1},{3,2},{4,3},{5,4},{6,5},{7,6},{9,8},{10,9},{11,10},{12... | collective-permute-start | bytes 184328 | tf_op jit(solution)/shard_map/ppermute | solution.py:414
  7.0 0.0 collective-permute-done.before_ref
  7.0 4.3 %collective-permute-done.1.after_ref = f32[120,128]{1,0:T(8,128)S(1)} collective-permute-done((f32[120,128]{1,0:T(8,128)S(1)}, f32[120,128]{1,0:T(8,128)S(1)}, u32[]{:S(2)}, u32[]{:S(2)}) %collective-permute-start.1) | collective-permute-done | bytes 61472 | tf_op jit(solution)/shard_map/ppermute | solution.py:414
  11.3 4.8 %collective-permute-start.3 = (f32[344,128]{1,0:T(8,128)S(1)}, f32[344,128]{1,0:T(8,128)S(1)}, u32[]{:S(2)}, u32[]{:S(2)}) collective-permute-start(f32[344,128]{1,0:T(8,128)S(1)} %get-tuple-element.28), channel_id=1, source_target_pairs={{8,16},{16,8},{24,32},{32,24},{40,48},{48,40},{56,64},{64,56},{72,... | collective-permute-start | bytes 528392 | tf_op jit(solution)/shard_map/ppermute | solution.py:422
  16.1 1.9 %collective-permute-start.2 = (f32[336,128]{1,0:T(8,128)S(1)}, f32[336,128]{1,0:T(8,128)S(1)}, u32[]{:S(2)}, u32[]{:S(2)}) collective-permute-start(f32[336,128]{1,0:T(8,128)S(1)} %get-tuple-element.27), channel_id=1, source_target_pairs={{0,8},{8,0},{1,9},{9,1},{2,10},{10,2},{3,11},{11,3},{4,12},{12,4},... | collective-permute-start | bytes 516104 | tf_op jit(solution)/shard_map/ppermute | solution.py:423
  18.1 1.4 %collective-permute-done.2.mate_ref = f32[336,128]{1,0:T(8,128)S(1)} collective-permute-done((f32[336,128]{1,0:T(8,128)S(1)}, f32[336,128]{1,0:T(8,128)S(1)}, u32[]{:S(2)}, u32[]{:S(2)}) %collective-permute-start.2) | collective-permute-done | bytes 172064 | tf_op jit(solution)/shard_map/ppermute | solution.py:423
  19.4 0.0 collective-permute-done.3.face_ref
  19.5 1.0 %shard_map.39 = (f32[8,24,128]{2,1,0:T(8,128)S(1)}, f32[4,8,24,128]{3,2,1,0:T(8,128)S(1)}, f32[16,8,128]{2,1,0:T(8,128)S(1)}, f32[3,16,128]{2,1,0:T(8,128)S(1)}) custom-call(f32[3,4,40,128]{3,2,1,0:T(8,128)S(1)} %get-tuple-element.26.own_ref, f32[336,128]{1,0:T(8,128)S(1)} %collective-permute-done.2.mate_ref, f32[344,128]{1,0:T(8,128)S(1)} %collective-permute-done.3.face_ref), custom_call_target="tpu_custom_call" | custom-call | tf_op jit(solution)/shard_map/pallas_call | solution.py:391
  20.4 16.5 %all_to_all.10 = f32[16,8,128]{2,1,0:T(8,128)S(1)} all-to-all(f32[16,8,128]{2,1,0:T(8,128)S(1)} %get-tuple-element.30), channel_id=1, replica_groups=mesh['y'=8,'x'=4,'c'=2,'z'=8] {'c','z'}, dimensions={0} | all-to-all | bytes 131072 | tf_op jit(solution)/shard_map/all_to_all | solution.py:431
  36.9 0.9 %shard_map.40 = f32[32,32,128]{2,1,0:T(8,128)} custom-call(f32[128,128]{1,0:T(8,128)S(1)} %bitcast.8), custom_call_target="tpu_custom_call" | custom-call | tf_op jit(solution)/shard_map/pallas_call | solution.py:433
  37.8 13.1 %all-to-all-start.1 = ((f32[32,32,128]{2,1,0:T(8,128)}), f32[32,32,128]{2,1,0:T(8,128)S(1)}, u32[]{:S(2)}, u32[]{:S(2)}) async-start(f32[32,32,128]{2,1,0:T(8,128)} %shard_map.40), calls=%async_computation.1 | async-start | bytes 1048576 | tf_op jit(solution)/shard_map/all_to_all | solution.py:448
  50.9 1.9 %collective-permute-start.4 = (f32[3,16,128]{2,1,0:T(8,128)S(1)}, f32[3,16,128]{2,1,0:T(8,128)S(1)}, u32[]{:S(2)}, u32[]{:S(2)}) collective-permute-start(f32[3,16,128]{2,1,0:T(8,128)S(1)} %get-tuple-element.32.own_ref), channel_id=1, source_target_pairs={{0,8},{8,0},{1,9},{9,1},{2,10},{10,2},{3,11},{11,3},{4,12},{12,4},... | collective-permute-start | bytes 73736 | tf_op jit(solution)/shard_map/ppermute | solution.py:452
  52.8 1.2 %collective-permute-done.4.mate_ref = f32[3,16,128]{2,1,0:T(8,128)S(1)} collective-permute-done((f32[3,16,128]{2,1,0:T(8,128)S(1)}, f32[3,16,128]{2,1,0:T(8,128)S(1)}, u32[]{:S(2)}, u32[]{:S(2)}) %collective-permute-start.4) | collective-permute-done | bytes 24608 | tf_op jit(solution)/shard_map/ppermute | solution.py:452
  54.0 1.3 %collective-permute-start.5 = (f32[2,3,16,128]{3,2,1,0:T(8,128)S(1)}, f32[2,3,16,128]{3,2,1,0:T(8,128)S(1)}, u32[]{:S(2)}, u32[]{:S(2)}) collective-permute-start(f32[2,3,16,128]{3,2,1,0:T(8,128)S(1)} %pad_maximum_fusion.1), channel_id=1, source_target_pairs={{0,16},{24,8},{16,32},{40,24},{32,48},{56,40},{48,64},{72,56},{64,... | collective-permute-start | bytes 147464 | tf_op jit(solution)/shard_map/ppermute | solution.py:457
  55.3 4.0 %collective-permute-start.6 = (f32[3,16,128]{2,1,0:T(8,128)S(1)}, f32[3,16,128]{2,1,0:T(8,128)S(1)}, u32[]{:S(2)}, u32[]{:S(2)}) collective-permute-start(f32[3,16,128]{2,1,0:T(8,128)S(1)} %get-tuple-element.32.own_ref), channel_id=1, source_target_pairs={{16,0},{8,24},{32,16},{24,40},{48,32},{40,56},{64,48},{56,72},{80,... | collective-permute-start | bytes 73736 | tf_op jit(solution)/shard_map/ppermute | solution.py:458
  59.3 0.9 %collective-permute-done.6.inner_ref = f32[3,16,128]{2,1,0:T(8,128)S(1)} collective-permute-done((f32[3,16,128]{2,1,0:T(8,128)S(1)}, f32[3,16,128]{2,1,0:T(8,128)S(1)}, u32[]{:S(2)}, u32[]{:S(2)}) %collective-permute-start.6) | collective-permute-done | bytes 24608 | tf_op jit(solution)/shard_map/ppermute | solution.py:458
  60.2 0.0 collective-permute-done.5.outer_ref
  60.2 4.3 %all-to-all-done.1.got_ref = f32[32,32,128]{2,1,0:T(8,128)S(1)} async-done(((f32[32,32,128]{2,1,0:T(8,128)}), f32[32,32,128]{2,1,0:T(8,128)S(1)}, u32[]{:S(2)}, u32[]{:S(2)}) %all-to-all-start.1) | async-done | bytes 524320 | tf_op jit(solution)/shard_map/all_to_all | solution.py:448
  64.5 2.7 %collective-permute-start.7 = (f32[32,32,128]{2,1,0:T(8,128)S(1)}, f32[32,32,128]{2,1,0:T(8,128)S(1)}, u32[]{:S(2)}, u32[]{:S(2)}) collective-permute-start(f32[32,32,128]{2,1,0:T(8,128)S(1)} %all-to-all-done.1.got_ref), channel_id=1, source_target_pairs={{0,8},{8,0},{1,9},{9,1},{2,10},{10,2},{3,11},{11,3},{4,12},{12,4},... | collective-permute-start | bytes 1572872 | tf_op jit(solution)/shard_map/ppermute | solution.py:460
  67.3 0.3 shard_map.41
  67.6 1.2 %collective-permute-done.7.mate_ref = f32[32,32,128]{2,1,0:T(8,128)S(1)} collective-permute-done((f32[32,32,128]{2,1,0:T(8,128)S(1)}, f32[32,32,128]{2,1,0:T(8,128)S(1)}, u32[]{:S(2)}, u32[]{:S(2)}) %collective-permute-start.7) | collective-permute-done | bytes 524320 | tf_op jit(solution)/shard_map/ppermute | solution.py:460
  68.8 3.2 %shard_map.42 = f32[4,16,128]{2,1,0:T(8,128)} custom-call(f32[32,32,128]{2,1,0:T(8,128)S(1)} %all-to-all-done.1.got_ref, f32[32,32,128]{2,1,0:T(8,128)S(1)} %collective-permute-done.7.mate_ref, bf16[384,256]{1,0:T(8,128)(2,1)S(1)} %get-tuple-element.36.matrix_ref, bf16[128,128]{1,0:T(8,128)(2,1)S(1)} %get-tuple-element.37.spread_ref, ...), custom_call_target="tpu_custom_call" | custom-call | tf_op jit(solution)/shard_map/pallas_call | solution.py:391
  (4 shorter events, 0.1 us)
Async XLA Ops:
  0.8 6.1 %collective-permute-start = (f32[120,128]{1,0:T(8,128)S(1)}, f32[120,128]{1,0:T(8,128)S(1)}, u32[]{:S(2)}, u32[]{:S(2)}) collective-permute-start(f32[120,128]{1,0:T(8,128)S(1)} %get-tuple-element.24), channel_id=1, source_target_pairs={{0,1},{1,2},{2,3},{3,4},{4,5},{5,6},{6,7},{8,9},{9,10},{10,11},{11... | collective-permute-start | bytes 184328 | tf_op jit(solution)/shard_map/ppermute | solution.py:413
  5.7 5.6 %collective-permute-start.1 = (f32[120,128]{1,0:T(8,128)S(1)}, f32[120,128]{1,0:T(8,128)S(1)}, u32[]{:S(2)}, u32[]{:S(2)}) collective-permute-start(f32[120,128]{1,0:T(8,128)S(1)} %get-tuple-element.25), channel_id=1, source_target_pairs={{1,0},{2,1},{3,2},{4,3},{5,4},{6,5},{7,6},{9,8},{10,9},{11,10},{12... | collective-permute-start | bytes 184328 | tf_op jit(solution)/shard_map/ppermute | solution.py:414
  11.3 8.1 %collective-permute-start.3 = (f32[344,128]{1,0:T(8,128)S(1)}, f32[344,128]{1,0:T(8,128)S(1)}, u32[]{:S(2)}, u32[]{:S(2)}) collective-permute-start(f32[344,128]{1,0:T(8,128)S(1)} %get-tuple-element.28), channel_id=1, source_target_pairs={{8,16},{16,8},{24,32},{32,24},{40,48},{48,40},{56,64},{64,56},{72,... | collective-permute-start | bytes 528392 | tf_op jit(solution)/shard_map/ppermute | solution.py:422
  16.1 3.3 %collective-permute-start.2 = (f32[336,128]{1,0:T(8,128)S(1)}, f32[336,128]{1,0:T(8,128)S(1)}, u32[]{:S(2)}, u32[]{:S(2)}) collective-permute-start(f32[336,128]{1,0:T(8,128)S(1)} %get-tuple-element.27), channel_id=1, source_target_pairs={{0,8},{8,0},{1,9},{9,1},{2,10},{10,2},{3,11},{11,3},{4,12},{12,4},... | collective-permute-start | bytes 516104 | tf_op jit(solution)/shard_map/ppermute | solution.py:423
  37.8 26.8 %all-to-all-start.1 = ((f32[32,32,128]{2,1,0:T(8,128)}), f32[32,32,128]{2,1,0:T(8,128)S(1)}, u32[]{:S(2)}, u32[]{:S(2)}) async-start(f32[32,32,128]{2,1,0:T(8,128)} %shard_map.40), calls=%async_computation.1 | async-start | bytes 1048576 | tf_op jit(solution)/shard_map/all_to_all | solution.py:448
  50.9 3.1 %collective-permute-start.4 = (f32[3,16,128]{2,1,0:T(8,128)S(1)}, f32[3,16,128]{2,1,0:T(8,128)S(1)}, u32[]{:S(2)}, u32[]{:S(2)}) collective-permute-start(f32[3,16,128]{2,1,0:T(8,128)S(1)} %get-tuple-element.32.own_ref), channel_id=1, source_target_pairs={{0,8},{8,0},{1,9},{9,1},{2,10},{10,2},{3,11},{11,3},{4,12},{12,4},... | collective-permute-start | bytes 73736 | tf_op jit(solution)/shard_map/ppermute | solution.py:452
  54.0 6.2 %collective-permute-start.5 = (f32[2,3,16,128]{3,2,1,0:T(8,128)S(1)}, f32[2,3,16,128]{3,2,1,0:T(8,128)S(1)}, u32[]{:S(2)}, u32[]{:S(2)}) collective-permute-start(f32[2,3,16,128]{3,2,1,0:T(8,128)S(1)} %pad_maximum_fusion.1), channel_id=1, source_target_pairs={{0,16},{24,8},{16,32},{40,24},{32,48},{56,40},{48,64},{72,56},{64,... | collective-permute-start | bytes 147464 | tf_op jit(solution)/shard_map/ppermute | solution.py:457
  55.3 4.9 %collective-permute-start.6 = (f32[3,16,128]{2,1,0:T(8,128)S(1)}, f32[3,16,128]{2,1,0:T(8,128)S(1)}, u32[]{:S(2)}, u32[]{:S(2)}) collective-permute-start(f32[3,16,128]{2,1,0:T(8,128)S(1)} %get-tuple-element.32.own_ref), channel_id=1, source_target_pairs={{16,0},{8,24},{32,16},{24,40},{48,32},{40,56},{64,48},{56,72},{80,... | collective-permute-start | bytes 73736 | tf_op jit(solution)/shard_map/ppermute | solution.py:458
  64.5 4.3 %collective-permute-start.7 = (f32[32,32,128]{2,1,0:T(8,128)S(1)}, f32[32,32,128]{2,1,0:T(8,128)S(1)}, u32[]{:S(2)}, u32[]{:S(2)}) collective-permute-start(f32[32,32,128]{2,1,0:T(8,128)S(1)} %all-to-all-done.1.got_ref), channel_id=1, source_target_pairs={{0,8},{8,0},{1,9},{9,1},{2,10},{10,2},{3,11},{11,3},{4,12},{12,4},... | collective-permute-start | bytes 1572872 | tf_op jit(solution)/shard_map/ppermute | solution.py:460

commit v13 on v12

--- a/solution.py
+++ b/solution.py
@@ -277,7 +277,7 @@
         own, padded = slice(i, i + chunk), slice(i + 2, i + chunk + 2)
         inverse_ref[padded] = 1.0 / (d_ref[own] - a_ref[own])
 
-    span = 8 if planes % 8 == 0 else 2
+    span = 16 if planes % 16 == 0 else 2
 
     def product(ref):
         for i in range(0, planes, span):

time: 72.7 us -> 72.5 us (level)
  no operation moved by 1% of the time
where the time goes in v13:
time: 72.5 us; the launch traced here: 71.7 us
  starting transfers between devices  35.9 us (50%)
  blocking collectives  16.5 us (23%)
  waiting for transfers between devices  13.3 us (18%)
  Pallas kernels  5.18 us (7%)
  other arithmetic  0.81 us (1%)
    all_to_all x1, blocking collectives, shards(): got = lax.all_to_all(sent, ('c', 'z'), 0, 0).reshape(16 * nz, 128)  16.5 us
    all_to_all x1, starting transfers between devices, shards(): lax.all_to_all(sent, ('y', 'x', 'c'), 0, 0, axis_index_groups=[evens, odds])  13.1 us
    ppermute x1, starting transfers between devices, shards(): face = lax.ppermute(face, ('y', 'x', 'c'), facing)  4.83 us
    ppermute x1, starting transfers between devices, shards(): before = lax.ppermute(tail, 'z', up)  4.83 us
    all_to_all x1, waiting for transfers between devices, shards(): lax.all_to_all(sent, ('y', 'x', 'c'), 0, 0, axis_index_groups=[evens, odds])  4.33 us
    pallas_call x5, Pallas kernels, call(): pl.pallas_call(kernel, out_shape=[jax.ShapeDtypeStruct(*(out if isinstanc...  4.3 us
    ppermute x1, waiting for transfers between devices, shards(): after = lax.ppermute(head, 'z', down)  4.29 us
    ppermute x1, starting transfers between devices, shards(): inner = lax.ppermute(one, ('y', 'x', 'c'), [(j, i) for i, j in ring])  3.99 us
  transfers between devices with their start and end apart: 9, of which 6 were waited for; matrix products, arithmetic and copies ran while one was open for 0% of the time, Pallas kernels for 0%

profile of v13, /device:TPU:1, one launch (start us, length us, event | category | flops | bytes accessed | tf_op | source)
XLA Modules:
  0.0 71.7 jit_solution(1929918545840357658)
XLA Ops:
  0.0 0.8 %pad_maximum_fusion.own_ref = f32[3,4,16,128]{3,2,1,0:T(8,128)S(1)} fusion(f32[1,4,16,128]{3,2,1,0:T(8,128)} %bitcast.9, f32[1,4,16,128]{3,2,1,0:T(8,128)} %bitcast.10, f32[1,4,16,128]{3,2,1,0:T(8,128)} %bitcast.11), kind=kLoop, calls=%fused_computation | loop fusion | flops 49152 | bytes 196608 | tf_op jit(solution)/shard_map/stack | solution.py:409
  0.8 4.8 %collective-permute-start = (f32[120,128]{1,0:T(8,128)S(1)}, f32[120,128]{1,0:T(8,128)S(1)}, u32[]{:S(2)}, u32[]{:S(2)}) collective-permute-start(f32[120,128]{1,0:T(8,128)S(1)} %get-tuple-element.24), channel_id=1, source_target_pairs={{0,1},{1,2},{2,3},{3,4},{4,5},{5,6},{6,7},{8,9},{9,10},{10,11},{11... | collective-permute-start | bytes 184328 | tf_op jit(solution)/shard_map/ppermute | solution.py:413
  5.7 1.3 %collective-permute-start.1 = (f32[120,128]{1,0:T(8,128)S(1)}, f32[120,128]{1,0:T(8,128)S(1)}, u32[]{:S(2)}, u32[]{:S(2)}) collective-permute-start(f32[120,128]{1,0:T(8,128)S(1)} %get-tuple-element.25), channel_id=1, source_target_pairs={{1,0},{2,1},{3,2},{4,3},{5,4},{6,5},{7,6},{9,8},{10,9},{11,10},{12... | collective-permute-start | bytes 184328 | tf_op jit(solution)/shard_map/ppermute | solution.py:414
  7.0 0.0 collective-permute-done.before_ref
  7.0 4.3 %collective-permute-done.1.after_ref = f32[120,128]{1,0:T(8,128)S(1)} collective-permute-done((f32[120,128]{1,0:T(8,128)S(1)}, f32[120,128]{1,0:T(8,128)S(1)}, u32[]{:S(2)}, u32[]{:S(2)}) %collective-permute-start.1) | collective-permute-done | bytes 61472 | tf_op jit(solution)/shard_map/ppermute | solution.py:414
  11.3 4.8 %collective-permute-start.3 = (f32[344,128]{1,0:T(8,128)S(1)}, f32[344,128]{1,0:T(8,128)S(1)}, u32[]{:S(2)}, u32[]{:S(2)}) collective-permute-start(f32[344,128]{1,0:T(8,128)S(1)} %get-tuple-element.28), channel_id=1, source_target_pairs={{8,16},{16,8},{24,32},{32,24},{40,48},{48,40},{56,64},{64,56},{72,... | collective-permute-start | bytes 528392 | tf_op jit(solution)/shard_map/ppermute | solution.py:422
  16.1 1.9 %collective-permute-start.2 = (f32[336,128]{1,0:T(8,128)S(1)}, f32[336,128]{1,0:T(8,128)S(1)}, u32[]{:S(2)}, u32[]{:S(2)}) collective-permute-start(f32[336,128]{1,0:T(8,128)S(1)} %get-tuple-element.27), channel_id=1, source_target_pairs={{0,8},{8,0},{1,9},{9,1},{2,10},{10,2},{3,11},{11,3},{4,12},{12,4},... | collective-permute-start | bytes 516104 | tf_op jit(solution)/shard_map/ppermute | solution.py:423
  18.1 1.4 %collective-permute-done.2.mate_ref = f32[336,128]{1,0:T(8,128)S(1)} collective-permute-done((f32[336,128]{1,0:T(8,128)S(1)}, f32[336,128]{1,0:T(8,128)S(1)}, u32[]{:S(2)}, u32[]{:S(2)}) %collective-permute-start.2) | collective-permute-done | bytes 172064 | tf_op jit(solution)/shard_map/ppermute | solution.py:423
  19.4 0.0 collective-permute-done.3.face_ref
  19.5 1.0 %shard_map.39 = (f32[8,24,128]{2,1,0:T(8,128)S(1)}, f32[4,8,24,128]{3,2,1,0:T(8,128)S(1)}, f32[16,8,128]{2,1,0:T(8,128)S(1)}, f32[3,16,128]{2,1,0:T(8,128)S(1)}) custom-call(f32[3,4,40,128]{3,2,1,0:T(8,128)S(1)} %get-tuple-element.26.own_ref, f32[336,128]{1,0:T(8,128)S(1)} %collective-permute-done.2.mate_ref, f32[344,128]{1,0:T(8,128)S(1)} %collective-permute-done.3.face_ref), custom_call_target="tpu_custom_call" | custom-call | tf_op jit(solution)/shard_map/pallas_call | solution.py:391
  20.4 16.5 %all_to_all.10 = f32[16,8,128]{2,1,0:T(8,128)S(1)} all-to-all(f32[16,8,128]{2,1,0:T(8,128)S(1)} %get-tuple-element.30), channel_id=1, replica_groups=mesh['y'=8,'x'=4,'c'=2,'z'=8] {'c','z'}, dimensions={0} | all-to-all | bytes 131072 | tf_op jit(solution)/shard_map/all_to_all | solution.py:431
  36.9 0.9 %shard_map.40 = f32[32,32,128]{2,1,0:T(8,128)} custom-call(f32[128,128]{1,0:T(8,128)S(1)} %bitcast.8), custom_call_target="tpu_custom_call" | custom-call | tf_op jit(solution)/shard_map/pallas_call | solution.py:433
  37.8 13.1 %all-to-all-start.1 = ((f32[32,32,128]{2,1,0:T(8,128)}), f32[32,32,128]{2,1,0:T(8,128)S(1)}, u32[]{:S(2)}, u32[]{:S(2)}) async-start(f32[32,32,128]{2,1,0:T(8,128)} %shard_map.40), calls=%async_computation.1 | async-start | bytes 1048576 | tf_op jit(solution)/shard_map/all_to_all | solution.py:448
  50.9 1.9 %collective-permute-start.4 = (f32[3,16,128]{2,1,0:T(8,128)S(1)}, f32[3,16,128]{2,1,0:T(8,128)S(1)}, u32[]{:S(2)}, u32[]{:S(2)}) collective-permute-start(f32[3,16,128]{2,1,0:T(8,128)S(1)} %get-tuple-element.32.own_ref), channel_id=1, source_target_pairs={{0,8},{8,0},{1,9},{9,1},{2,10},{10,2},{3,11},{11,3},{4,12},{12,4},... | collective-permute-start | bytes 73736 | tf_op jit(solution)/shard_map/ppermute | solution.py:452
  52.8 1.2 %collective-permute-done.4.mate_ref = f32[3,16,128]{2,1,0:T(8,128)S(1)} collective-permute-done((f32[3,16,128]{2,1,0:T(8,128)S(1)}, f32[3,16,128]{2,1,0:T(8,128)S(1)}, u32[]{:S(2)}, u32[]{:S(2)}) %collective-permute-start.4) | collective-permute-done | bytes 24608 | tf_op jit(solution)/shard_map/ppermute | solution.py:452
  54.0 1.3 %collective-permute-start.5 = (f32[2,3,16,128]{3,2,1,0:T(8,128)S(1)}, f32[2,3,16,128]{3,2,1,0:T(8,128)S(1)}, u32[]{:S(2)}, u32[]{:S(2)}) collective-permute-start(f32[2,3,16,128]{3,2,1,0:T(8,128)S(1)} %pad_maximum_fusion.1), channel_id=1, source_target_pairs={{0,16},{24,8},{16,32},{40,24},{32,48},{56,40},{48,64},{72,56},{64,... | collective-permute-start | bytes 147464 | tf_op jit(solution)/shard_map/ppermute | solution.py:457
  55.3 4.0 %collective-permute-start.6 = (f32[3,16,128]{2,1,0:T(8,128)S(1)}, f32[3,16,128]{2,1,0:T(8,128)S(1)}, u32[]{:S(2)}, u32[]{:S(2)}) collective-permute-start(f32[3,16,128]{2,1,0:T(8,128)S(1)} %get-tuple-element.32.own_ref), channel_id=1, source_target_pairs={{16,0},{8,24},{32,16},{24,40},{48,32},{40,56},{64,48},{56,72},{80,... | collective-permute-start | bytes 73736 | tf_op jit(solution)/shard_map/ppermute | solution.py:458
  59.3 0.9 %collective-permute-done.6.inner_ref = f32[3,16,128]{2,1,0:T(8,128)S(1)} collective-permute-done((f32[3,16,128]{2,1,0:T(8,128)S(1)}, f32[3,16,128]{2,1,0:T(8,128)S(1)}, u32[]{:S(2)}, u32[]{:S(2)}) %collective-permute-start.6) | collective-permute-done | bytes 24608 | tf_op jit(solution)/shard_map/ppermute | solution.py:458
  60.2 0.0 collective-permute-done.5.outer_ref
  60.2 4.3 %all-to-all-done.1.got_ref = f32[32,32,128]{2,1,0:T(8,128)S(1)} async-done(((f32[32,32,128]{2,1,0:T(8,128)}), f32[32,32,128]{2,1,0:T(8,128)S(1)}, u32[]{:S(2)}, u32[]{:S(2)}) %all-to-all-start.1) | async-done | bytes 524320 | tf_op jit(solution)/shard_map/all_to_all | solution.py:448
  64.5 2.7 %collective-permute-start.7 = (f32[32,32,128]{2,1,0:T(8,128)S(1)}, f32[32,32,128]{2,1,0:T(8,128)S(1)}, u32[]{:S(2)}, u32[]{:S(2)}) collective-permute-start(f32[32,32,128]{2,1,0:T(8,128)S(1)} %all-to-all-done.1.got_ref), channel_id=1, source_target_pairs={{0,8},{8,0},{1,9},{9,1},{2,10},{10,2},{3,11},{11,3},{4,12},{12,4},... | collective-permute-start | bytes 1572872 | tf_op jit(solution)/shard_map/ppermute | solution.py:460
  67.3 0.3 shard_map.41
  67.6 1.2 %collective-permute-done.7.mate_ref = f32[32,32,128]{2,1,0:T(8,128)S(1)} collective-permute-done((f32[32,32,128]{2,1,0:T(8,128)S(1)}, f32[32,32,128]{2,1,0:T(8,128)S(1)}, u32[]{:S(2)}, u32[]{:S(2)}) %collective-permute-start.7) | collective-permute-done | bytes 524320 | tf_op jit(solution)/shard_map/ppermute | solution.py:460
  68.8 2.9 %shard_map.42 = f32[4,16,128]{2,1,0:T(8,128)} custom-call(f32[32,32,128]{2,1,0:T(8,128)S(1)} %all-to-all-done.1.got_ref, f32[32,32,128]{2,1,0:T(8,128)S(1)} %collective-permute-done.7.mate_ref, bf16[384,256]{1,0:T(8,128)(2,1)S(1)} %get-tuple-element.36.matrix_ref, bf16[128,128]{1,0:T(8,128)(2,1)S(1)} %get-tuple-element.37.spread_ref, ...), custom_call_target="tpu_custom_call" | custom-call | tf_op jit(solution)/shard_map/pallas_call | solution.py:391
  (4 shorter events, 0.1 us)
Async XLA Ops:
  0.8 6.1 %collective-permute-start = (f32[120,128]{1,0:T(8,128)S(1)}, f32[120,128]{1,0:T(8,128)S(1)}, u32[]{:S(2)}, u32[]{:S(2)}) collective-permute-start(f32[120,128]{1,0:T(8,128)S(1)} %get-tuple-element.24), channel_id=1, source_target_pairs={{0,1},{1,2},{2,3},{3,4},{4,5},{5,6},{6,7},{8,9},{9,10},{10,11},{11... | collective-permute-start | bytes 184328 | tf_op jit(solution)/shard_map/ppermute | solution.py:413
  5.7 5.6 %collective-permute-start.1 = (f32[120,128]{1,0:T(8,128)S(1)}, f32[120,128]{1,0:T(8,128)S(1)}, u32[]{:S(2)}, u32[]{:S(2)}) collective-permute-start(f32[120,128]{1,0:T(8,128)S(1)} %get-tuple-element.25), channel_id=1, source_target_pairs={{1,0},{2,1},{3,2},{4,3},{5,4},{6,5},{7,6},{9,8},{10,9},{11,10},{12... | collective-permute-start | bytes 184328 | tf_op jit(solution)/shard_map/ppermute | solution.py:414
  11.3 8.1 %collective-permute-start.3 = (f32[344,128]{1,0:T(8,128)S(1)}, f32[344,128]{1,0:T(8,128)S(1)}, u32[]{:S(2)}, u32[]{:S(2)}) collective-permute-start(f32[344,128]{1,0:T(8,128)S(1)} %get-tuple-element.28), channel_id=1, source_target_pairs={{8,16},{16,8},{24,32},{32,24},{40,48},{48,40},{56,64},{64,56},{72,... | collective-permute-start | bytes 528392 | tf_op jit(solution)/shard_map/ppermute | solution.py:422
  16.1 3.3 %collective-permute-start.2 = (f32[336,128]{1,0:T(8,128)S(1)}, f32[336,128]{1,0:T(8,128)S(1)}, u32[]{:S(2)}, u32[]{:S(2)}) collective-permute-start(f32[336,128]{1,0:T(8,128)S(1)} %get-tuple-element.27), channel_id=1, source_target_pairs={{0,8},{8,0},{1,9},{9,1},{2,10},{10,2},{3,11},{11,3},{4,12},{12,4},... | collective-permute-start | bytes 516104 | tf_op jit(solution)/shard_map/ppermute | solution.py:423
  37.8 26.8 %all-to-all-start.1 = ((f32[32,32,128]{2,1,0:T(8,128)}), f32[32,32,128]{2,1,0:T(8,128)S(1)}, u32[]{:S(2)}, u32[]{:S(2)}) async-start(f32[32,32,128]{2,1,0:T(8,128)} %shard_map.40), calls=%async_computation.1 | async-start | bytes 1048576 | tf_op jit(solution)/shard_map/all_to_all | solution.py:448
  50.9 3.1 %collective-permute-start.4 = (f32[3,16,128]{2,1,0:T(8,128)S(1)}, f32[3,16,128]{2,1,0:T(8,128)S(1)}, u32[]{:S(2)}, u32[]{:S(2)}) collective-permute-start(f32[3,16,128]{2,1,0:T(8,128)S(1)} %get-tuple-element.32.own_ref), channel_id=1, source_target_pairs={{0,8},{8,0},{1,9},{9,1},{2,10},{10,2},{3,11},{11,3},{4,12},{12,4},... | collective-permute-start | bytes 73736 | tf_op jit(solution)/shard_map/ppermute | solution.py:452
  54.0 6.2 %collective-permute-start.5 = (f32[2,3,16,128]{3,2,1,0:T(8,128)S(1)}, f32[2,3,16,128]{3,2,1,0:T(8,128)S(1)}, u32[]{:S(2)}, u32[]{:S(2)}) collective-permute-start(f32[2,3,16,128]{3,2,1,0:T(8,128)S(1)} %pad_maximum_fusion.1), channel_id=1, source_target_pairs={{0,16},{24,8},{16,32},{40,24},{32,48},{56,40},{48,64},{72,56},{64,... | collective-permute-start | bytes 147464 | tf_op jit(solution)/shard_map/ppermute | solution.py:457
  55.3 4.9 %collective-permute-start.6 = (f32[3,16,128]{2,1,0:T(8,128)S(1)}, f32[3,16,128]{2,1,0:T(8,128)S(1)}, u32[]{:S(2)}, u32[]{:S(2)}) collective-permute-start(f32[3,16,128]{2,1,0:T(8,128)S(1)} %get-tuple-element.32.own_ref), channel_id=1, source_target_pairs={{16,0},{8,24},{32,16},{24,40},{48,32},{40,56},{64,48},{56,72},{80,... | collective-permute-start | bytes 73736 | tf_op jit(solution)/shard_map/ppermute | solution.py:458
  64.5 4.3 %collective-permute-start.7 = (f32[32,32,128]{2,1,0:T(8,128)S(1)}, f32[32,32,128]{2,1,0:T(8,128)S(1)}, u32[]{:S(2)}, u32[]{:S(2)}) collective-permute-start(f32[32,32,128]{2,1,0:T(8,128)S(1)} %all-to-all-done.1.got_ref), channel_id=1, source_target_pairs={{0,8},{8,0},{1,9},{9,1},{2,10},{10,2},{3,11},{11,3},{4,12},{12,4},... | collective-permute-start | bytes 1572872 | tf_op jit(solution)/shard_map/ppermute | solution.py:460
